TPU v7x, 32 devices: a whole 2x2x4 slice. The times are simulated.
32 devices in a mesh: group: 4 (over z), tp: 4 (over y, core), fork: 2 (over x).
Axes of the slice: x: 2, y: 2, z: 4, core: 2. Of those that a mesh axis runs over, the one named last changes fastest.
Arguments:
- prompt_hidden: bfloat16 [4, 512, 8192], P(None, 'group'), may hold values from -6 to 6
- kv_weight: bfloat16 [8192, 2048], P(None, ('tp', 'fork')), may hold values from -0.0625 to 0.0625
- kv_bias: float32 [2048], P(('tp', 'fork')), may hold values from -3 to 3
- new_query: bfloat16 [4, 8, 4, 8192], P('group', ('tp', 'fork')), may hold values from -105 to 105
- new_kv: bfloat16 [4, 8, 4, 2048], P('group', ('tp', 'fork')), may hold values from -3 to 3
- decode_prompt: int32 [4], replicated, may hold values from 0 to 3, as said below
- sample_counts: int32 [4], replicated, may hold values from 1 to 8, 24 in all
- page_table: int32 [4, 64], P('group'), may hold values from 0 to 63, each once within a row
Outputs:
- attention_out: bfloat16 [4, 8, 4, 8192], P('group', ('tp', 'fork'))
- kv_cache: bfloat16 [4, 64, 8, 2048], P('group', None, None, ('tp', 'fork'))
Inputs may be any that keep to these rules, and one draw needn't show every extreme that they name: `decode_prompt`: each prompt is decoded by exactly 1 group. `page_table`: each row is a permutation of the 64 slots.
All inputs are finite; a program needn't handle non-finite values.
Results may differ from a plain program's by a relative error of at most 0.0067.
Values may be sent and summed in bfloat16 or wider, within the bound.
No kernel may reach another device: no remote copies, remote signals or barrier semaphores. Data moves between devices by JAX's collectives and lax.ppermute only.
A program may use at most 128 MiB of HBM per device.

v0:
```python
import jax
import jax.numpy as jnp
from jax import lax
from jax.sharding import PartitionSpec as P

KV_HEADS = 8
HEAD_DIM = 128
Q_PER_KV = 8
PAGE = 8


rope_base = 1000000.0


def rotate(vectors, positions):
    half_dim = HEAD_DIM // 2
    frequency = rope_base ** (-(2.0 * jnp.arange(half_dim, dtype=jnp.float32)) / HEAD_DIM)
    angles = positions.astype(jnp.float32)[:, None, None] * frequency[None, None, :]
    cosine = jnp.cos(angles)
    sine_of = jnp.sin(angles)
    leading = vectors[..., :half_dim]
    trailing = vectors[..., half_dim:]
    return jnp.concatenate(
        [leading * cosine - trailing * sine_of, trailing * cosine + leading * sine_of], axis=-1
    )


def attend(queries, recent_keys, recent_values, history):
    scaling = HEAD_DIM ** (-0.5)
    past_keys = history[:, :, :HEAD_DIM]
    past_values = history[:, :, HEAD_DIM:]
    past_scores = (
        jnp.einsum("snhge,lhe->snhgl", queries, past_keys, preferred_element_type=jnp.float32)
        * scaling
    )
    recent_scores = (
        jnp.einsum("snhge,smhe->snhgm", queries, recent_keys, preferred_element_type=jnp.float32)
        * scaling
    )
    offsets = jnp.arange(recent_keys.shape[1], dtype=jnp.int32)
    visible = offsets[:, None] >= offsets[None, :]
    recent_scores = jnp.where(visible[None, :, None, None, :], recent_scores, -jnp.inf)
    highest = jnp.maximum(jnp.max(past_scores, axis=-1), jnp.max(recent_scores, axis=-1))[..., None]
    past_weight = jnp.exp(past_scores - highest)
    recent_weight = jnp.exp(recent_scores - highest)
    denominator = jnp.sum(past_weight, axis=-1, keepdims=True) + jnp.sum(
        recent_weight, axis=-1, keepdims=True
    )
    past_weight = (past_weight / denominator).astype(jnp.bfloat16)
    recent_weight = (recent_weight / denominator).astype(jnp.bfloat16)
    blended = jnp.einsum(
        "snhgl,lhe->snhge", past_weight, past_values, preferred_element_type=jnp.float32
    )
    blended = blended + jnp.einsum(
        "snhgm,smhe->snhge", recent_weight, recent_values, preferred_element_type=jnp.float32
    )
    return blended.astype(jnp.bfloat16)


def local(
    prompt_hidden, kv_weight, kv_bias, new_query, new_kv, decode_prompt, sample_counts, page_table
):
    prompt_count, block_len, model_width = prompt_hidden.shape
    group_index = lax.axis_index("group")
    projected = (
        jnp.dot(
            prompt_hidden.reshape(prompt_count * block_len, model_width),
            kv_weight,
            preferred_element_type=jnp.float32,
        )
        + kv_bias
    )
    projected = projected.reshape(prompt_count, block_len, 1, 2, HEAD_DIM)
    positions = group_index * block_len + jnp.arange(block_len, dtype=jnp.int32)
    rotated = rotate(projected[:, :, :, 0], positions)
    local_pages = jnp.stack([rotated, projected[:, :, :, 1]], axis=3).astype(jnp.bfloat16)
    local_pages = local_pages.reshape(prompt_count, block_len, 2 * HEAD_DIM)
    own_prompt = decode_prompt[group_index]
    history = lax.dynamic_index_in_dim(
        lax.all_gather(local_pages, "group", axis=1, tiled=True), own_prompt, 0, keepdims=False
    )
    history_len = history.shape[0]
    page_blocks = history.reshape(history_len // PAGE, PAGE, 2 * HEAD_DIM)
    slot_ids = jnp.arange(history_len // PAGE, dtype=jnp.int32)
    table_row = page_table[0]
    source_page = jnp.sum(
        jnp.where(table_row[None, :] == slot_ids[:, None], slot_ids[None, :], 0), axis=1
    )
    kv_cache = jnp.take(page_blocks, source_page, axis=0)[None]
    group_ids = jnp.arange(decode_prompt.shape[0], dtype=jnp.int32)
    earlier = jnp.sum(jnp.where((group_ids < group_index) & (decode_prompt == own_prompt), 1, 0))
    live_limit = sample_counts[own_prompt]
    per_device = new_query.shape[1]
    new_steps = new_query.shape[2]
    row_width = new_query.shape[3]
    members = lax.axis_size(("tp", "fork"))
    group_samples = per_device * members
    head_history = history.reshape(history_len, 1, 2 * HEAD_DIM)
    queries = new_query.reshape(per_device, new_steps, KV_HEADS, Q_PER_KV, HEAD_DIM)
    recent = new_kv.reshape(per_device, new_steps, KV_HEADS, 2, HEAD_DIM)
    blended = attend(
        queries,
        recent[:, :, :, 0],
        recent[:, :, :, 1],
        lax.all_gather(head_history, ("tp", "fork"), axis=1, tiled=True),
    )
    sample_ids = (
        earlier * group_samples
        + lax.axis_index(("tp", "fork")) * per_device
        + jnp.arange(per_device, dtype=jnp.int32)
    )
    alive = sample_ids < live_limit
    blended = jnp.where(alive[:, None, None, None, None], blended, jnp.zeros_like(blended))
    attention_out = blended.reshape(1, per_device, new_steps, row_width)
    return (attention_out, kv_cache)


def solution(mesh):
    return jax.shard_map(
        local,
        mesh=mesh,
        in_specs=(
            P(None, "group", None),
            P(None, ("tp", "fork")),
            P(("tp", "fork")),
            P("group", ("tp", "fork"), None, None),
            P("group", ("tp", "fork"), None, None),
            P(),
            P(),
            P("group", None),
        ),
        out_specs=(P("group", ("tp", "fork"), None, None), P("group", None, None, ("tp", "fork"))),
        check_vma=False,
    )
```

profile of v0, /device:TPU:0, one launch (start us, length us, event | category | flops | bytes accessed | tf_op | source)
XLA Modules:
  0.0 89.2 jit_solution(8478892938635910404)
XLA Ops:
  7.2 0.0 all-gather.4.cloned.1.call-start
  7.2 7.0 %convolution_add_fusion = f32[512,256]{1,0:T(8,128)S(1)} fusion(bf16[512,8192]{1,0:T(8,128)(2,1)} %bitcast.97, bf16[8192,256]{1,0:T(8,128)(2,1)} %param.9, f32[256]{0:T(256)} %param.10), kind=kOutput, calls=%fused_computation.3 | convolution fusion | flops 2147614720 | bytes 13108224 | tf_op jit(solution)/shard_map/dot_general | solution.py:66
  14.2 0.0 copy-start.1
  14.2 0.0 copy-start.3
  14.3 0.0 copy-start
  14.3 0.0 copy-start.4
  14.3 0.0 copy-start.2
  14.3 0.3 reshape.223
  14.6 0.2 slice.35
  14.8 0.3 slice.38
  15.1 0.3 multiply_cosine_fusion
  15.4 0.1 subtract_convert_fusion
  15.6 0.1 maximum_bitcast_fusion
  15.7 0.9 copy.35
  16.6 0.0 all-gather.4.cloned.1.call-update
  16.6 0.0 all-gather.6.cloned.1.call-start
  16.6 0.0 copy-done.1
  16.7 0.6 dynamic_slice.10
  19.2 30.5 %all-gather.4.cloned.1.call-done = bf16[4,512,256]{1,2,0:T(8,128)(2,1)} async-done(((bf16[4,128,256]{1,2,0:T(8,128)(2,1)}), bf16[4,512,256]{1,2,0:T(8,128)(2,1)}) %all-gather.4.cloned.1.call-update) | async-done | bytes 1048592 | tf_op jit(solution)/shard_map/all_gather | solution.py:80
  49.6 1.7 %constant_dynamic-slice_fusion = bf16[1,512,256]{1,2,0:T(8,128)(2,1)} fusion(bf16[4,512,256]{1,2,0:T(8,128)(2,1)} %all-gather.4.cloned.1.call-done, s32[]{:T(128)S(6)} %select_n.53), kind=kLoop, calls=%fused_computation.50 | loop fusion | bytes 524292 | tf_op jit(solution)/shard_map/jit(dynamic_index_in_dim)/dynamic_slice | solution.py:79
  51.3 0.0 all-gather.6.cloned.1.call-update
  51.4 0.0 copy-done.3
  51.4 0.6 dynamic_slice.11
  52.0 0.0 copy-done
  52.0 1.3 %fusion.15 = s32[]{:T(128)} fusion(s32[4]{0:T(128)S(1)} %copy-done.1, s32[]{:T(128)} %bitcast, s32[]{:T(128)S(6)} %axis_index.33), kind=kLoop, calls=%fused_computation.49 | loop fusion | flops 19 | bytes 28 | tf_op jit(solution)/shard_map/reduce_sum | solution.py:91
  54.6 0.0 copy-done.4
  54.6 0.1 select_reduce_fusion
  54.8 0.0 copy-done.2
  54.8 0.4 fusion.18
  55.2 1.1 %copy.43 = bf16[1,512,256]{2,1,0:T(8,128)(2,1)S(1)} copy(bf16[1,512,256]{1,2,0:T(8,128)(2,1)} %constant_dynamic-slice_fusion) | data formatting | bytes 524288 | tf_op jit(solution)/shard_map/jit(dynamic_index_in_dim)/dynamic_slice | solution.py:79
  56.3 0.6 gather_fusion
  56.9 0.8 bitcast_select_fusion
  57.7 20.0 %all-gather.6.cloned.1.call-done = bf16[1,512,2048]{1,2,0:T(8,128)(2,1)} async-done(((bf16[1,512,256]{1,2,0:T(8,128)(2,1)}), bf16[1,512,2048]{1,2,0:T(8,128)(2,1)}) %all-gather.6.cloned.1.call-update) | async-done | bytes 2097168 | tf_op jit(solution)/shard_map/all_gather | solution.py:105
  77.8 1.6 %fusion.17 = (f32[4,8,8]{2,0,1:T(4,128)S(1)}, f32[1,4,8,8,512]{4,3,1,2,0:T(8,128)S(1)}) fusion(bf16[512,8,256]{0,2,1:T(8,128)(2,1)} %bitcast.98, bf16[1,4,64,128]{3,1,2,0:T(4,128)(2,1)S(1)} %bitcast.101), kind=kOutput, calls=%fused_computation.52 | convolution fusion | flops 33816320 | bytes 1639424 | tf_op jit(solution)/shard_map/snhge,lhe->snhgl/dot_general | solution.py:33
  79.4 0.1 fusion.11
  79.5 0.2 fusion.6
  79.7 0.2 convolution_bitcast_fusion.1
  79.9 1.7 %fusion.3 = bf16[1,4,8,8,128]{4,3,1,2,0:T(8,128)(2,1)S(1)} fusion(f32[1,4,8,8,128]{4,3,1,2,0:T(8,128)S(1)} %convolution_bitcast_fusion.1, bf16[512,8,256]{0,2,1:T(8,128)(2,1)} %bitcast.99, f32[1,4,8,8,512]{4,3,1,2,0:T(8,128)S(1)} %get-tuple-element.9, f32[4,8,8]{2,0,1:T(4,128)S(1)} %add.80, f32[4,8,8]{2,0,1:T(4,128)S(1)} %max.9, pred[]{:T(512)} %bitcast.2), kind=kOutput, calls=%fused_computation.8 | convolution fusion | flops 34045952 | bytes 1772032 | tf_op jit(solution)/shard_map/snhgl,lhe->snhge/dot_general | solution.py:51
  81.7 0.7 reshape.231
  (14 shorter events, 0.2 us)
Async XLA Ops:
  7.2 42.5 %all-gather.4.cloned.1.call-start = ((), (), s32[]{:S(2)}) async-start(), calls=%async_computation | async-start | bytes 1310720 | tf_op jit(solution)/shard_map/all_gather | solution.py:80
  14.2 2.4 %copy-start.1 = (s32[4]{0:T(128)S(1)}, s32[4]{0:T(128)}, u32[]{:S(2)}) copy-start(s32[4]{0:T(128)} %param.13) | copy-start | bytes 52
  14.2 37.1 %copy-start.3 = (s32[4]{0:T(128)S(1)}, s32[4]{0:T(128)}, u32[]{:S(2)}) copy-start(s32[4]{0:T(128)} %param.14) | copy-start | bytes 52
  14.3 37.7 %copy-start = (bf16[1,1,4,2048]{3,2,1,0:T(4,128)(2,1)S(1)}, bf16[1,1,4,2048]{3,2,1,0:T(4,128)(2,1)}, u32[]{:S(2)}) copy-start(bf16[1,1,4,2048]{3,2,1,0:T(4,128)(2,1)} %param.12) | copy-start | bytes 49156
  14.3 40.3 %copy-start.4 = (s32[1,64]{1,0:T(1,128)S(1)}, s32[1,64]{1,0:T(1,128)}, u32[]{:S(2)}) copy-start(s32[1,64]{1,0:T(1,128)} %param.15) | copy-start | bytes 772
  14.3 40.5 %copy-start.2 = (bf16[1,1,4,8192]{3,2,1,0:T(4,128)(2,1)S(1)}, bf16[1,1,4,8192]{3,2,1,0:T(4,128)(2,1)}, u32[]{:S(2)}) copy-start(bf16[1,1,4,8192]{3,2,1,0:T(4,128)(2,1)} %param.11) | copy-start | bytes 196612
  16.6 61.2 %all-gather.6.cloned.1.call-start = ((), (), s32[]{:S(2)}) async-start(), calls=%async_computation.1 | async-start | bytes 2359296 | tf_op jit(solution)/shard_map/all_gather | solution.py:105
Sparse Core Ops, SparseCore 0:
  16.7 32.8 all-gather.3
  51.5 26.2 all-gather.5
where the time goes:
time: 89.5 us; the launch traced here: 89.2 us
  waiting for transfers between devices  50.5 us (56%)
  between operations  17.5 us (20%)
  matrix products  11 us (12%)
  local copies, waits for them, and re-layouts  6.92 us (8%)
  other arithmetic  3.21 us (4%)
    all_gather x1, waiting for transfers between devices, local(): lax.all_gather(local_pages, 'group', axis=1, tiled=True)  30.5 us
    all_gather x1, waiting for transfers between devices, local(): lax.all_gather(head_history, ('tp', 'fork'), axis=1, tiled=True)  20 us
    dot_general x1, matrix products, local(): jnp.dot(prompt_hidden.reshape(prompt_count * block_len, model_width), kv_...  6.99 us
    dynamic_slice x2, local copies, waits for them, and re-layouts, local(): lax.dynamic_index_in_dim(lax.all_gather(local_pages, 'group', axis=1, til...  2.77 us
  transfers between devices with their start and end apart: 2, of which 2 were waited for; matrix products, arithmetic and copies ran while one was open for 6% of the time, Pallas kernels for 0%

commit v1 on v0

v1 whole, which is shorter than its diff:
```python
import functools

import jax
import jax.numpy as jnp
from jax import lax
from jax.experimental import pallas as pl
from jax.experimental.pallas import tpu as pltpu
from jax.sharding import PartitionSpec as P

KV_HEADS = 8
HEAD_DIM = 128
Q_PER_KV = 8
PAGE = 8
ROPE_BASE = 1000000.0
MEMBERS = ("tp", "fork")
VMEM_LIMIT = 48 * 1024 * 1024


def partners(groups):
    if groups & (groups - 1) == 0:
        return [
            (lambda me, s=s: me ^ s, lambda me, s=s: me ^ s) for s in range(groups - 1, 0, -1)
        ]
    return [
        (lambda me, s=s: (me + s) % groups, lambda me, s=s: (me + groups - s) % groups)
        for s in range(1, groups)
    ]


def project_kernel(groups, ordered, prompt_ref, x_ref, w_ref, b_ref, *rest):
    outs, (acc_ref, cos_ref, sin_ref) = rest[:-3], rest[-3:]
    step = pl.program_id(0)
    prompts, rows, depth = x_ref.shape
    width = w_ref.shape[1]
    me = lax.axis_index("group")
    part = jnp.dot(
        x_ref[...].reshape(prompts * rows, depth),
        w_ref[...],
        preferred_element_type=jnp.float32,
    ).reshape(prompts, rows, width)

    @pl.when(step == 0)
    def _():
        acc_ref[...] = part + b_ref[...][None]
        lane = lax.broadcasted_iota(jnp.int32, (rows, HEAD_DIM), 1)
        half = HEAD_DIM // 2
        index = jnp.where(lane < half, lane, lane - half).astype(jnp.float32)
        frequency = jnp.exp(index * (-2.0 * 13.815510557964274 / HEAD_DIM))
        position = me * rows + lax.broadcasted_iota(jnp.int32, (rows, HEAD_DIM), 0)
        angle = position.astype(jnp.float32) * frequency
        cos_ref[...] = jnp.cos(angle)
        sine = jnp.sin(angle)
        sin_ref[...] = jnp.where(lane < half, -sine, sine)

    @pl.when(step > 0)
    def _():
        acc_ref[...] += part

    @pl.when(step == pl.num_programs(0) - 1)
    def _():
        for at, out in enumerate(outs):
            if ordered:
                goes_to = partners(groups)[at][0](me) if at < groups - 1 else me
                total = acc_ref[prompt_ref[goes_to]]
            else:
                total = acc_ref[at]
            key = total[:, :HEAD_DIM]
            swapped = jnp.concatenate(
                [key[:, HEAD_DIM // 2 :], key[:, : HEAD_DIM // 2]], axis=1
            )
            out[:, :HEAD_DIM] = (key * cos_ref[...] + swapped * sin_ref[...]).astype(out.dtype)
            out[:, HEAD_DIM:] = total[:, HEAD_DIM:].astype(out.dtype)


def project(groups, ordered, decode_prompt, prompt_hidden, kv_weight, kv_bias):
    prompts, rows, depth = prompt_hidden.shape
    width = kv_weight.shape[1]
    tile = 1024
    return pl.pallas_call(
        functools.partial(project_kernel, groups, ordered),
        grid=(depth // tile,),
        in_specs=[
            pl.BlockSpec(memory_space=pltpu.SMEM),
            pl.BlockSpec((prompts, rows, tile), lambda k: (0, 0, k)),
            pl.BlockSpec((tile, width), lambda k: (k, 0)),
            pl.BlockSpec((1, width), lambda k: (0, 0)),
        ],
        out_specs=[pl.BlockSpec((rows, width), lambda k: (0, 0))] * prompts,
        out_shape=[jax.ShapeDtypeStruct((rows, width), jnp.bfloat16)] * prompts,
        scratch_shapes=[
            pltpu.VMEM((prompts, rows, width), jnp.float32),
            pltpu.VMEM((rows, HEAD_DIM), jnp.float32),
            pltpu.VMEM((rows, HEAD_DIM), jnp.float32),
        ],
        compiler_params=pltpu.CompilerParams(vmem_limit_bytes=VMEM_LIMIT),
        name="project",
    )(decode_prompt, prompt_hidden, kv_weight, kv_bias.reshape(1, width))


def attend_kernel(groups, steps, prompt_ref, count_ref, table_ref, recent_ref, *rest):
    blocks, out_ref, cache_ref, sem = rest[:groups], rest[groups], rest[groups + 1], rest[groups + 2]
    me = lax.axis_index("group")
    samples = recent_ref.shape[0]
    pages = blocks[0].shape[0]
    sources = [source(me) for _, source in partners(groups)] + [me]
    for block, source in zip(blocks, sources):

        def place(j, carry, block=block, source=source):
            slot = table_ref[0, source * pages + j]
            pltpu.make_async_copy(block.at[j], cache_ref.at[slot], sem).start()
            return carry

        lax.fori_loop(0, pages, place, 0, unroll=True)

    own_prompt = prompt_ref[me]
    earlier = jnp.int32(0)
    for g in range(groups):
        same = jnp.logical_and(g < me, prompt_ref[g] == own_prompt)
        earlier = earlier + jnp.where(same, 1, 0)
    live = count_ref[own_prompt] - earlier * samples

    q_rows = Q_PER_KV * steps
    rows = samples * q_rows
    scaling = HEAD_DIM ** (-0.5)
    query = recent_ref[:, :q_rows, :].reshape(rows, HEAD_DIM)
    recent = recent_ref[:, q_rows:, :].astype(jnp.float32).reshape(samples * 2 * steps, HEAD_DIM)
    recent_key = recent.astype(jnp.bfloat16)
    recent_value = jnp.concatenate([recent[steps:], recent[:steps]], axis=0).astype(jnp.bfloat16)
    contract = (((1,), (1,)), ((), ()))

    def scored(keys):
        return (
            lax.dot_general(query, keys, contract, preferred_element_type=jnp.float32) * scaling
        )

    recent_score = scored(recent_key)
    row = lax.broadcasted_iota(jnp.int32, recent_score.shape, 0)
    column = lax.broadcasted_iota(jnp.int32, recent_score.shape, 1)
    visible = jnp.logical_and(
        row // q_rows == column // (2 * steps), column % (2 * steps) <= row % steps
    )
    recent_score = jnp.where(visible, recent_score, -jnp.inf)
    flat = [block[...].reshape(pages * PAGE, 2 * HEAD_DIM) for block in blocks]
    scores = [scored(block[:, :HEAD_DIM]) for block in flat]
    highest = jnp.max(recent_score, axis=1, keepdims=True)
    for score in scores:
        highest = jnp.maximum(highest, jnp.max(score, axis=1, keepdims=True))
    recent_weight = jnp.exp(recent_score - highest)
    weights = [jnp.exp(score - highest) for score in scores]
    total = jnp.sum(recent_weight, axis=1, keepdims=True)
    for weight in weights:
        total = total + jnp.sum(weight, axis=1, keepdims=True)
    blended = jnp.dot(
        (recent_weight / total).astype(jnp.bfloat16),
        recent_value,
        preferred_element_type=jnp.float32,
    )
    for weight, block in zip(weights, flat):
        blended = blended + jnp.dot(
            (weight / total).astype(jnp.bfloat16),
            block[:, HEAD_DIM:],
            preferred_element_type=jnp.float32,
        )
    sample = lax.broadcasted_iota(jnp.int32, blended.shape, 0) // q_rows
    blended = jnp.where(sample < live, blended, 0.0)
    out_ref[...] = blended.astype(jnp.bfloat16).reshape(samples, q_rows, HEAD_DIM)
    pltpu.make_async_copy(cache_ref, cache_ref, sem).wait()


def attend(groups, steps, decode_prompt, sample_counts, page_table, recent, blocks):
    samples = recent.shape[0]
    page_count = page_table.shape[1]
    smem = pl.BlockSpec(memory_space=pltpu.SMEM)
    vmem = pl.BlockSpec(memory_space=pltpu.VMEM)
    return pl.pallas_call(
        functools.partial(attend_kernel, groups, steps),
        in_specs=[smem, smem, smem, vmem] + [vmem] * groups,
        out_specs=[vmem, pl.BlockSpec(memory_space=pl.ANY)],
        out_shape=[
            jax.ShapeDtypeStruct((samples, Q_PER_KV * steps, HEAD_DIM), jnp.bfloat16),
            jax.ShapeDtypeStruct((page_count, PAGE, 2 * HEAD_DIM), jnp.bfloat16),
        ],
        scratch_shapes=[pltpu.SemaphoreType.DMA],
        compiler_params=pltpu.CompilerParams(vmem_limit_bytes=VMEM_LIMIT),
        name="attend",
    )(decode_prompt, sample_counts, page_table, recent, *blocks)


def local(
    prompt_hidden, kv_weight, kv_bias, new_query, new_kv, decode_prompt, sample_counts, page_table
):
    prompts, rows, _ = prompt_hidden.shape
    groups = lax.axis_size("group")
    steps = new_query.shape[2]
    me = lax.axis_index("group")
    ordered = groups == prompts

    projected = project(groups, ordered, decode_prompt, prompt_hidden, kv_weight, kv_bias)
    if ordered:
        outgoing, own = projected[:-1], projected[-1]
    else:
        pages = jnp.stack(projected)

        def pages_of(group):
            return lax.dynamic_index_in_dim(pages, decode_prompt[group], 0, keepdims=False)

        outgoing = [pages_of(goes_to(me)) for goes_to, _ in partners(groups)]
        own = pages_of(me)
    blocks = [
        lax.ppermute(block, "group", [(i, goes_to(i)) for i in range(groups)])
        for block, (goes_to, _) in zip(outgoing, partners(groups))
    ]
    blocks = [
        block.reshape(rows // PAGE, PAGE, 2 * HEAD_DIM) for block in blocks + [own]
    ]

    by_head = new_query.reshape(steps, KV_HEADS, Q_PER_KV, HEAD_DIM).transpose(1, 2, 0, 3)
    kv_by_head = new_kv.reshape(steps, KV_HEADS, 2, HEAD_DIM).transpose(1, 2, 0, 3)
    packed = jnp.concatenate(
        [
            by_head.reshape(KV_HEADS, Q_PER_KV * steps, HEAD_DIM),
            kv_by_head.reshape(KV_HEADS, 2 * steps, HEAD_DIM),
        ],
        axis=1,
    )
    recent = lax.all_to_all(packed, MEMBERS, 0, 0)

    blended, cache = attend(
        groups, steps, decode_prompt, sample_counts, page_table, recent, blocks
    )
    returned = lax.all_to_all(blended, MEMBERS, 0, 0)
    attention_out = returned.reshape(KV_HEADS * Q_PER_KV, steps, HEAD_DIM).transpose(1, 0, 2)
    return attention_out.reshape(new_query.shape), cache[None]


def solution(mesh):
    return jax.shard_map(
        local,
        mesh=mesh,
        in_specs=(
            P(None, "group", None),
            P(None, MEMBERS),
            P(MEMBERS),
            P("group", MEMBERS, None, None),
            P("group", MEMBERS, None, None),
            P(),
            P(),
            P("group", None),
        ),
        out_specs=(P("group", MEMBERS, None, None), P("group", None, None, MEMBERS)),
        check_vma=False,
    )
```

time: 89.5 us -> 40.6 us (0.45)
  waiting for transfers between devices: 50.5 us -> 5.33 us
  between operations: 17.5 us -> 0.7 us
  matrix products: 11 us -> 0 us
  Pallas kernels: 0 us -> 10.2 us
  starting transfers between devices: 0.08 us -> 9.62 us
  blocking collectives: 0 us -> 8.61 us
  local copies, waits for them, and re-layouts: 6.92 us -> 4.16 us
  other arithmetic: 3.21 us -> 1.52 us
    all_gather x2 -> x0, waiting for transfers between devices: 50.5 us -> none  [the longest x1 30.5 us: local(): lax.all_gather(local_pages, 'group', axis=1, tiled=True)]
    dot_general x5 -> x0, matrix products: 11 us -> none  [the longest x1 6.99 us: local(): jnp.dot(prompt_hidden.reshape(prompt_count * block_len, model_width), kv_...]
    pallas_call x0 -> x2, Pallas kernels: none -> 10.2 us  [the longest x1 8.14 us: project(): pl.pallas_call(functools.partial(project_kernel, groups, ordered), grid=(...]
    all_to_all x0 -> x1, blocking collectives: none -> 8.61 us  [local(): returned = lax.all_to_all(blended, MEMBERS, 0, 0)]
    ppermute x0 -> x3, waiting for transfers between devices: none -> 5.33 us  [local(): lax.ppermute(block, 'group', [(i, goes_to(i)) for i in range(groups)])]
    all_to_all x0 -> x1, starting transfers between devices: none -> 5.17 us  [local(): recent = lax.all_to_all(packed, MEMBERS, 0, 0)]
    ppermute x0 -> x3, starting transfers between devices: none -> 4.45 us  [local(): lax.ppermute(block, 'group', [(i, goes_to(i)) for i in range(groups)])]
    unnamed x12 -> x13, local copies, waits for them, and re-layouts: 0.07 us -> 4.16 us
  transfers between devices with their start and end apart: 2 -> 4, of which waited for: 2 -> 2; matrix products, arithmetic and copies ran while one was open for 6% -> 0% of each run, Pallas kernels for 0% -> 20%
where the time goes in v1:
time: 40.6 us; the launch traced here: 40.2 us
  Pallas kernels  10.2 us (25%)
  starting transfers between devices  9.62 us (24%)
  blocking collectives  8.61 us (21%)
  waiting for transfers between devices  5.33 us (13%)
  local copies, waits for them, and re-layouts  4.16 us (10%)
  other arithmetic  1.52 us (4%)
  between operations  0.7 us (2%)
    all_to_all x1, blocking collectives, local(): returned = lax.all_to_all(blended, MEMBERS, 0, 0)  8.61 us
    pallas_call x1, Pallas kernels, project(): pl.pallas_call(functools.partial(project_kernel, groups, ordered), grid=(...  8.14 us
    ppermute x3, waiting for transfers between devices, local(): lax.ppermute(block, 'group', [(i, goes_to(i)) for i in range(groups)])  5.33 us
    all_to_all x1, starting transfers between devices, local(): recent = lax.all_to_all(packed, MEMBERS, 0, 0)  5.17 us
    ppermute x3, starting transfers between devices, local(): lax.ppermute(block, 'group', [(i, goes_to(i)) for i in range(groups)])  4.45 us
    unnamed x13, local copies, waits for them, and re-layouts  4.16 us
    pallas_call x1, Pallas kernels, attend(): pl.pallas_call(functools.partial(attend_kernel, groups, steps), in_specs=...  2.08 us
    concatenate x1, other arithmetic, local(): jnp.concatenate([by_head.reshape(KV_HEADS, Q_PER_KV * steps, HEAD_DIM), k...  1.52 us
  transfers between devices with their start and end apart: 4, of which 2 were waited for; matrix products, arithmetic and copies ran while one was open for 0% of the time, Pallas kernels for 20%

profile of v1, /device:TPU:0, one launch (start us, length us, event | category | flops | bytes accessed | tf_op | source)
XLA Modules:
  0.0 40.2 jit_solution(17999179623708209425)
XLA Ops:
  0.6 0.0 copy-start.2
  0.6 0.0 copy-start.5
  0.7 0.0 copy-start.4
  0.7 1.5 %pad_maximum_fusion = bf16[8,40,128]{2,1,0:T(8,128)(2,1)} fusion(bf16[8,8,128]{2,1,0:T(8,128)(2,1)} %bitcast.28, bf16[8,32,128]{2,1,0:T(8,128)(2,1)} %bitcast.27), kind=kLoop, calls=%fused_computation | loop fusion | flops 163840 | bytes 163840 | tf_op jit(solution)/shard_map/concatenate | solution.py:219
  2.2 5.2 %all-to-all-start = ((bf16[8,40,128]{2,1,0:T(8,128)(2,1)}), bf16[8,40,128]{2,1,0:T(8,128)(2,1)S(1)}, u32[]{:S(2)}, u32[]{:S(2)}) async-start(bf16[8,40,128]{2,1,0:T(8,128)(2,1)} %pad_maximum_fusion), calls=%async_computation | async-start | bytes 163840 | tf_op jit(solution)/shard_map/all_to_all | solution.py:226
  7.3 0.0 copy-start
  7.4 2.2 %copy-done = bf16[8192,256]{1,0:T(8,128)(2,1)S(1)} copy-done((bf16[8192,256]{1,0:T(8,128)(2,1)S(1)}, bf16[8192,256]{1,0:T(8,128)(2,1)}, u32[]{:S(2)}) %copy-start) | copy-done | bytes 4194328
  9.5 0.0 copy-start.1
  9.5 0.7 %copy-done.1 = s32[4]{0:T(128)S(1)} copy-done((s32[4]{0:T(128)S(1)}, s32[4]{0:T(128)}, u32[]{:S(2)}) %copy-start.1) | copy-done | bytes 40
  10.2 0.0 copy-start.3
  10.2 0.7 %copy-done.3 = f32[256]{0:T(256)S(1)} copy-done((f32[256]{0:T(256)S(1)}, f32[256]{0:T(256)}, u32[]{:S(2)}) %copy-start.3) | copy-done | bytes 1048
  10.9 8.1 %project.1 = (bf16[128,256]{1,0:T(8,128)(2,1)S(1)}, bf16[128,256]{1,0:T(8,128)(2,1)S(1)}, bf16[128,256]{1,0:T(8,128)(2,1)S(1)}, bf16[128,256]{1,0:T(8,128)(2,1)S(1)}) custom-call(s32[4]{0:T(128)S(1)} %copy-done.1, bf16[4,128,8192]{2,1,0:T(8,128)(2,1)} %x_ref.1, bf16[8192,256]{1,0:T(8,128)(2,1)S(1)} %copy-done, f32[1,256]{1,0:T(1,128)S(1)} %bitcast.25), custom_call_target="tpu_custom_call" | custom-call | tf_op jit(solution)/shard_map/project/pallas_call | solution.py:79
  19.0 3.7 %collective-permute-start = (bf16[128,256]{1,0:T(8,128)(2,1)S(1)}, bf16[128,256]{1,0:T(8,128)(2,1)S(1)}, u32[]{:S(2)}, u32[]{:S(2)}) collective-permute-start(bf16[128,256]{1,0:T(8,128)(2,1)S(1)} %get-tuple-element.8), channel_id=1, source_target_pairs={{0,24},{8,16},{16,8},{24,0},{1,25},{9,17},{17,9},{25,1},{2,26},{10... | collective-permute-start | bytes 196616 | tf_op jit(solution)/shard_map/ppermute | solution.py:210
  22.7 0.0 collective-permute-start.1
  22.7 0.8 %collective-permute-start.2 = (bf16[128,256]{1,0:T(8,128)(2,1)S(1)}, bf16[128,256]{1,0:T(8,128)(2,1)S(1)}, u32[]{:S(2)}, u32[]{:S(2)}) collective-permute-start(bf16[128,256]{1,0:T(8,128)(2,1)S(1)} %get-tuple-element.10), channel_id=1, source_target_pairs={{0,8},{8,0},{16,24},{24,16},{1,9},{9,1},{17,25},{25,17},{2,10},{10... | collective-permute-start | bytes 196616 | tf_op jit(solution)/shard_map/ppermute | solution.py:210
  23.5 2.2 %collective-permute-done = bf16[128,256]{1,0:T(8,128)(2,1)S(1)} collective-permute-done((bf16[128,256]{1,0:T(8,128)(2,1)S(1)}, bf16[128,256]{1,0:T(8,128)(2,1)S(1)}, u32[]{:S(2)}, u32[]{:S(2)}) %collective-permute-start) | collective-permute-done | bytes 65568 | tf_op jit(solution)/shard_map/ppermute | solution.py:210
  25.6 3.2 %collective-permute-done.1 = bf16[128,256]{1,0:T(8,128)(2,1)S(1)} collective-permute-done((bf16[128,256]{1,0:T(8,128)(2,1)S(1)}, bf16[128,256]{1,0:T(8,128)(2,1)S(1)}, u32[]{:S(2)}, u32[]{:S(2)}) %collective-permute-start.1) | collective-permute-done | bytes 65568 | tf_op jit(solution)/shard_map/ppermute | solution.py:210
  28.8 0.0 collective-permute-done.2
  28.8 0.0 all-to-all-done.recent_ref
  28.8 0.0 copy-done.2
  28.8 0.0 copy-done.5
  28.8 0.0 copy-done.4
  28.8 2.1 %attend.1 = (bf16[8,32,128]{2,1,0:T(8,128)(2,1)S(1)}, bf16[64,8,256]{2,1,0:T(8,128)(2,1)}) custom-call(s32[4]{0:T(128)S(1)} %copy-done.2, s32[4]{0:T(128)S(1)} %copy-done.4, s32[1,64]{1,0:T(1,128)S(1)} %copy-done.5, bf16[8,40,128]{2,1,0:T(8,128)(2,1)S(1)} %all-to-all-done.recent_ref, bf16[16,8,256]{2,1,0:T(8,128)(2,1)S(1)} %bitcast.22, ...), custom_call_target="tpu_custom_call" | custom-call | tf_op jit(solution)/shard_map/attend/pallas_call | solution.py:175
  30.9 8.6 %all_to_all.10 = bf16[8,32,128]{2,1,0:T(8,128)(2,1)S(1)} all-to-all(bf16[8,32,128]{2,1,0:T(8,128)(2,1)S(1)} %get-tuple-element.12), channel_id=1, replica_groups=mesh['group'=4,'tp'=4,'fork'=2] {'tp','fork'}, dimensions={0} | all-to-all | bytes 131072 | tf_op jit(solution)/shard_map/all_to_all | solution.py:231
  39.5 0.6 %copy.14 = bf16[1,1,4,8192]{3,2,1,0:T(4,128)(2,1)} copy(bf16[1,1,4,8192]{3,2,1,0:T(4,128)(2,1)S(1)} %bitcast.26) | data formatting | bytes 131072
Async XLA Ops:
  0.6 28.2 %copy-start.2 = (s32[4]{0:T(128)S(1)}, s32[4]{0:T(128)}, u32[]{:S(2)}) copy-start(s32[4]{0:T(128)} %prompt_ref.3) | copy-start | bytes 52
  0.6 28.2 %copy-start.5 = (s32[1,64]{1,0:T(1,128)S(1)}, s32[1,64]{1,0:T(1,128)}, u32[]{:S(2)}) copy-start(s32[1,64]{1,0:T(1,128)} %table_ref.1) | copy-start | bytes 772
  0.7 28.2 %copy-start.4 = (s32[4]{0:T(128)S(1)}, s32[4]{0:T(128)}, u32[]{:S(2)}) copy-start(s32[4]{0:T(128)} %count_ref.1) | copy-start | bytes 52
  2.2 26.6 %all-to-all-start = ((bf16[8,40,128]{2,1,0:T(8,128)(2,1)}), bf16[8,40,128]{2,1,0:T(8,128)(2,1)S(1)}, u32[]{:S(2)}, u32[]{:S(2)}) async-start(bf16[8,40,128]{2,1,0:T(8,128)(2,1)} %pad_maximum_fusion), calls=%async_computation | async-start | bytes 163840 | tf_op jit(solution)/shard_map/all_to_all | solution.py:226
  7.3 2.2 %copy-start = (bf16[8192,256]{1,0:T(8,128)(2,1)S(1)}, bf16[8192,256]{1,0:T(8,128)(2,1)}, u32[]{:S(2)}) copy-start(bf16[8192,256]{1,0:T(8,128)(2,1)} %w_ref.1) | copy-start | bytes 12582916
  9.5 0.7 %copy-start.1 = (s32[4]{0:T(128)S(1)}, s32[4]{0:T(128)}, u32[]{:S(2)}) copy-start(s32[4]{0:T(128)} %prompt_ref.3) | copy-start | bytes 52
  10.2 0.7 %copy-start.3 = (f32[256]{0:T(256)S(1)}, f32[256]{0:T(256)}, u32[]{:S(2)}) copy-start(f32[256]{0:T(256)} %param.10) | copy-start | bytes 3076
  19.0 6.6 %collective-permute-start = (bf16[128,256]{1,0:T(8,128)(2,1)S(1)}, bf16[128,256]{1,0:T(8,128)(2,1)S(1)}, u32[]{:S(2)}, u32[]{:S(2)}) collective-permute-start(bf16[128,256]{1,0:T(8,128)(2,1)S(1)} %get-tuple-element.8), channel_id=1, source_target_pairs={{0,24},{8,16},{16,8},{24,0},{1,25},{9,17},{17,9},{25,1},{2,26},{10... | collective-permute-start | bytes 196616 | tf_op jit(solution)/shard_map/ppermute | solution.py:210
  22.7 6.1 %collective-permute-start.1 = (bf16[128,256]{1,0:T(8,128)(2,1)S(1)}, bf16[128,256]{1,0:T(8,128)(2,1)S(1)}, u32[]{:S(2)}, u32[]{:S(2)}) collective-permute-start(bf16[128,256]{1,0:T(8,128)(2,1)S(1)} %get-tuple-element.9), channel_id=1, source_target_pairs={{0,16},{8,24},{16,0},{24,8},{1,17},{9,25},{17,1},{25,9},{2,18},{10... | collective-permute-start | bytes 196616 | tf_op jit(solution)/shard_map/ppermute | solution.py:210
  22.7 6.1 %collective-permute-start.2 = (bf16[128,256]{1,0:T(8,128)(2,1)S(1)}, bf16[128,256]{1,0:T(8,128)(2,1)S(1)}, u32[]{:S(2)}, u32[]{:S(2)}) collective-permute-start(bf16[128,256]{1,0:T(8,128)(2,1)S(1)} %get-tuple-element.10), channel_id=1, source_target_pairs={{0,8},{8,0},{16,24},{24,16},{1,9},{9,1},{17,25},{25,17},{2,10},{10... | collective-permute-start | bytes 196616 | tf_op jit(solution)/shard_map/ppermute | solution.py:210

commit v2 on v1

v2 whole, which is shorter than its diff:
```python
import functools
import math

import jax
import jax.numpy as jnp
from jax import lax
from jax.experimental import pallas as pl
from jax.experimental.pallas import tpu as pltpu
from jax.sharding import PartitionSpec as P

KV_HEADS = 8
HEAD_DIM = 128
Q_PER_KV = 8
PAGE = 8
ROPE_BASE = 1000000.0
MEMBERS = ("tp", "fork")
CHUNK = 1024
PROJECT_VMEM = 62 * 1024 * 1024
VMEM_LIMIT = 48 * 1024 * 1024
PACK_VMEM = 4 * 1024 * 1024
HIDE_FLOPS = 20 * 10**9


def partners(groups):
    if groups & (groups - 1) == 0:
        return [
            (lambda me, s=s: me ^ s, lambda me, s=s: me ^ s) for s in range(groups - 1, 0, -1)
        ]
    return [
        (lambda me, s=s: (me + s) % groups, lambda me, s=s: (me + groups - s) % groups)
        for s in range(1, groups)
    ]


def project_kernel(
    groups,
    ordered,
    prompt_hbm,
    x_hbm,
    w_hbm,
    b_hbm,
    query_hbm,
    recent_hbm,
    *rest,
):
    outs, packed_hbm, rest = rest[: x_hbm.shape[0]], rest[x_hbm.shape[0]], rest[x_hbm.shape[0] + 1 :]
    prompt_ref, b_ref, query_ref, recent_ref, packed_ref, x_ref, w_ref, total_ref, out_ref = rest[:9]
    small_sem, x_sem, w_sem, out_sem, packed_sem = rest[9:]
    chunks, prompts, rows, depth = x_ref.shape
    small = [
        pltpu.make_async_copy(source, target, small_sem.at[at])
        for at, (source, target) in enumerate(
            [
                (prompt_hbm, prompt_ref),
                (b_hbm, b_ref),
                (recent_hbm, recent_ref),
                (query_hbm, query_ref),
            ]
        )
    ]

    def large(at):
        begin = pl.multiple_of(at * depth, depth)
        return (
            pltpu.make_async_copy(w_hbm.at[pl.ds(begin, depth)], w_ref.at[at], w_sem.at[at]),
            pltpu.make_async_copy(x_hbm.at[:, :, pl.ds(begin, depth)], x_ref.at[at], x_sem.at[at]),
        )

    for copy in small:
        copy.start()
    for at in range(chunks):
        for copy in large(at):
            copy.start()

    me = lax.axis_index("group")
    half = HEAD_DIM // 2
    lane = lax.broadcasted_iota(jnp.int32, (rows, HEAD_DIM), 1)
    index = jnp.where(lane < half, lane, lane - half).astype(jnp.float32)
    frequency = jnp.exp(index * (-2.0 * math.log(ROPE_BASE) / HEAD_DIM))
    position = me * rows + lax.broadcasted_iota(jnp.int32, (rows, HEAD_DIM), 0)
    angle = position.astype(jnp.float32) * frequency
    cosine = jnp.cos(angle)
    sine = jnp.sin(angle)
    sine = jnp.where(lane < half, -sine, sine)
    total_ref[...] = jnp.zeros_like(total_ref)

    def accumulate(at, carry):
        for copy in large(at):
            copy.wait()
        part = jnp.dot(
            x_ref[at].reshape(prompts * rows, depth),
            w_ref[at],
            preferred_element_type=jnp.float32,
        )
        total_ref[...] += part.reshape(total_ref.shape)
        return carry

    early = chunks - chunks // 4
    lax.fori_loop(0, early, accumulate, 0)
    for copy in small:
        copy.wait()
    q_rows = query_ref.shape[1]
    packed_ref[:, :q_rows, :] = query_ref[...]
    packed_ref[:, q_rows:, :] = recent_ref[...]
    pack = pltpu.make_async_copy(packed_ref, packed_hbm, packed_sem)
    pack.start()
    lax.fori_loop(early, chunks, accumulate, 0)
    for at, out in enumerate(outs):
        prompt = at
        if ordered:
            prompt = prompt_ref[partners(groups)[at][0](me) if at < groups - 1 else me]
        total = total_ref[prompt] + b_ref[...]
        key = total[:, :HEAD_DIM]
        swapped = jnp.concatenate([key[:, half:], key[:, :half]], axis=1)
        out_ref[at, :, :HEAD_DIM] = (key * cosine + swapped * sine).astype(out.dtype)
        out_ref[at, :, HEAD_DIM:] = total[:, HEAD_DIM:].astype(out.dtype)
        pltpu.make_async_copy(out_ref.at[at], out, out_sem.at[at]).start()
    pack.wait()
    for at, out in enumerate(outs):
        pltpu.make_async_copy(out_ref.at[at], out, out_sem.at[at]).wait()


def project(groups, ordered, decode_prompt, prompt_hidden, kv_weight, kv_bias, query, recent):
    prompts, rows, depth = prompt_hidden.shape
    width = kv_weight.shape[1]
    chunks = depth // CHUNK
    packed_shape = (query.shape[0], query.shape[1] + recent.shape[1], HEAD_DIM)
    anywhere = pl.BlockSpec(memory_space=pl.ANY)
    return pl.pallas_call(
        functools.partial(project_kernel, groups, ordered),
        in_specs=[anywhere] * 6,
        out_specs=[anywhere] * (prompts + 1),
        out_shape=[jax.ShapeDtypeStruct((rows, width), jnp.bfloat16)] * prompts
        + [jax.ShapeDtypeStruct(packed_shape, query.dtype)],
        scratch_shapes=[
            pltpu.SMEM(decode_prompt.shape, jnp.int32),
            pltpu.VMEM((1, width), jnp.float32),
            pltpu.VMEM(query.shape, query.dtype),
            pltpu.VMEM(recent.shape, recent.dtype),
            pltpu.VMEM(packed_shape, query.dtype),
            pltpu.VMEM((chunks, prompts, rows, CHUNK), jnp.bfloat16),
            pltpu.VMEM((chunks, CHUNK, width), jnp.bfloat16),
            pltpu.VMEM((prompts, rows, width), jnp.float32),
            pltpu.VMEM((prompts, rows, width), jnp.bfloat16),
            pltpu.SemaphoreType.DMA((4,)),
            pltpu.SemaphoreType.DMA((chunks,)),
            pltpu.SemaphoreType.DMA((chunks,)),
            pltpu.SemaphoreType.DMA((prompts,)),
            pltpu.SemaphoreType.DMA,
        ],
        compiler_params=pltpu.CompilerParams(vmem_limit_bytes=PROJECT_VMEM),
        name="project",
    )(decode_prompt, prompt_hidden, kv_weight, kv_bias.reshape(1, width), query, recent)


def store_kernel(groups, table_ref, *rest):
    blocks, (cache_ref, sem) = rest[:groups], rest[groups:]
    me = lax.axis_index("group")
    pages = blocks[0].shape[0]
    sources = [source(me) for _, source in partners(groups)] + [me]
    for block, source in zip(blocks, sources):

        def place(j, carry, block=block, source=source):
            slot = table_ref[0, source * pages + j]
            pltpu.make_async_copy(block.at[j], cache_ref.at[slot], sem).start()
            return carry

        lax.fori_loop(0, pages, place, 0, unroll=True)
    pltpu.make_async_copy(cache_ref, cache_ref, sem).wait()


def store(groups, page_table, blocks):
    return pl.pallas_call(
        functools.partial(store_kernel, groups),
        in_specs=[pl.BlockSpec(memory_space=pltpu.SMEM)]
        + [pl.BlockSpec(memory_space=pltpu.VMEM)] * groups,
        out_specs=pl.BlockSpec(memory_space=pl.ANY),
        out_shape=jax.ShapeDtypeStruct((page_table.shape[1],) + blocks[0].shape[1:], jnp.bfloat16),
        scratch_shapes=[pltpu.SemaphoreType.DMA],
        cost_estimate=pl.CostEstimate(flops=HIDE_FLOPS, transcendentals=0, bytes_accessed=0),
        compiler_params=pltpu.CompilerParams(vmem_limit_bytes=PACK_VMEM),
        name="store",
    )(page_table, *blocks)


def attend_kernel(groups, steps, prompt_ref, count_ref, cache_ref, recent_ref, *rest):
    del cache_ref
    blocks, out_ref = rest[:groups], rest[groups]
    me = lax.axis_index("group")
    samples = recent_ref.shape[0]
    pages = blocks[0].shape[0]
    own_prompt = prompt_ref[me]
    earlier = jnp.int32(0)
    for g in range(groups):
        same = jnp.logical_and(g < me, prompt_ref[g] == own_prompt)
        earlier = earlier + jnp.where(same, 1, 0)
    live = count_ref[own_prompt] - earlier * samples

    q_rows = Q_PER_KV * steps
    rows = samples * q_rows
    scaling = HEAD_DIM ** (-0.5)
    query = recent_ref[:, :q_rows, :].reshape(rows, HEAD_DIM)
    recent = recent_ref[:, q_rows:, :].astype(jnp.float32).reshape(samples * 2 * steps, HEAD_DIM)
    recent_key = recent.astype(jnp.bfloat16)
    recent_value = jnp.concatenate([recent[steps:], recent[:steps]], axis=0).astype(jnp.bfloat16)
    contract = (((1,), (1,)), ((), ()))

    def scored(keys):
        return (
            lax.dot_general(query, keys, contract, preferred_element_type=jnp.float32) * scaling
        )

    recent_score = scored(recent_key)
    row = lax.broadcasted_iota(jnp.int32, recent_score.shape, 0)
    column = lax.broadcasted_iota(jnp.int32, recent_score.shape, 1)
    visible = jnp.logical_and(
        row // q_rows == column // (2 * steps), column % (2 * steps) <= row % steps
    )
    recent_score = jnp.where(visible, recent_score, -jnp.inf)
    flat = [block[...].reshape(pages * PAGE, 2 * HEAD_DIM) for block in blocks]
    scores = [scored(block[:, :HEAD_DIM]) for block in flat]
    highest = jnp.max(recent_score, axis=1, keepdims=True)
    for score in scores:
        highest = jnp.maximum(highest, jnp.max(score, axis=1, keepdims=True))
    recent_weight = jnp.exp(recent_score - highest)
    weights = [jnp.exp(score - highest) for score in scores]
    total = jnp.sum(recent_weight, axis=1, keepdims=True)
    for weight in weights:
        total = total + jnp.sum(weight, axis=1, keepdims=True)
    blended = jnp.dot(
        (recent_weight / total).astype(jnp.bfloat16),
        recent_value,
        preferred_element_type=jnp.float32,
    )
    for weight, block in zip(weights, flat):
        blended = blended + jnp.dot(
            (weight / total).astype(jnp.bfloat16),
            block[:, HEAD_DIM:],
            preferred_element_type=jnp.float32,
        )
    sample = lax.broadcasted_iota(jnp.int32, blended.shape, 0) // q_rows
    blended = jnp.where(sample < live, blended, 0.0)
    out_ref[...] = blended.astype(jnp.bfloat16).reshape(samples, q_rows, HEAD_DIM)


def attend(groups, steps, decode_prompt, sample_counts, cache, recent, blocks):
    samples = recent.shape[0]
    smem = pl.BlockSpec(memory_space=pltpu.SMEM)
    vmem = pl.BlockSpec(memory_space=pltpu.VMEM)
    return pl.pallas_call(
        functools.partial(attend_kernel, groups, steps),
        in_specs=[smem, smem, pl.BlockSpec(memory_space=pl.ANY), vmem] + [vmem] * groups,
        out_specs=vmem,
        out_shape=jax.ShapeDtypeStruct((samples, Q_PER_KV * steps, HEAD_DIM), jnp.bfloat16),
        compiler_params=pltpu.CompilerParams(vmem_limit_bytes=VMEM_LIMIT),
        name="attend",
    )(decode_prompt, sample_counts, cache, recent, *blocks)


def local(
    prompt_hidden, kv_weight, kv_bias, new_query, new_kv, decode_prompt, sample_counts, page_table
):
    prompts, rows, _ = prompt_hidden.shape
    groups = lax.axis_size("group")
    steps = new_query.shape[2]
    me = lax.axis_index("group")
    ordered = groups == prompts

    by_head = new_query.reshape(steps, KV_HEADS, Q_PER_KV, HEAD_DIM).transpose(1, 2, 0, 3)
    kv_by_head = new_kv.reshape(steps, KV_HEADS, 2, HEAD_DIM).transpose(1, 2, 0, 3)
    *projected, packed = project(
        groups,
        ordered,
        decode_prompt,
        prompt_hidden,
        kv_weight,
        kv_bias,
        by_head.reshape(KV_HEADS, Q_PER_KV * steps, HEAD_DIM),
        kv_by_head.reshape(KV_HEADS, 2 * steps, HEAD_DIM),
    )
    if ordered:
        outgoing, own = projected[:-1], projected[-1]
    else:
        pages = jnp.stack(projected)

        def pages_of(group):
            return lax.dynamic_index_in_dim(pages, decode_prompt[group], 0, keepdims=False)

        outgoing = [pages_of(goes_to(me)) for goes_to, _ in partners(groups)]
        own = pages_of(me)
    blocks = [
        lax.ppermute(block, "group", [(i, goes_to(i)) for i in range(groups)])
        for block, (goes_to, _) in zip(outgoing, partners(groups))
    ]
    blocks = [
        block.reshape(rows // PAGE, PAGE, 2 * HEAD_DIM) for block in blocks + [own]
    ]

    recent = lax.all_to_all(packed, MEMBERS, 0, 0)

    cache = store(groups, page_table, blocks)
    blended = attend(groups, steps, decode_prompt, sample_counts, cache, recent, blocks)
    returned = lax.all_to_all(blended, MEMBERS, 0, 0)
    attention_out = returned.reshape(KV_HEADS * Q_PER_KV, steps, HEAD_DIM).transpose(1, 0, 2)
    return attention_out.reshape(new_query.shape), cache[None]


def solution(mesh):
    return jax.shard_map(
        local,
        mesh=mesh,
        in_specs=(
            P(None, "group", None),
            P(None, MEMBERS),
            P(MEMBERS),
            P("group", MEMBERS, None, None),
            P("group", MEMBERS, None, None),
            P(),
            P(),
            P("group", None),
        ),
        out_specs=(P("group", MEMBERS, None, None), P("group", None, None, MEMBERS)),
        check_vma=False,
    )
```

time: 40.6 us -> 31.8 us (0.78)
  waiting for transfers between devices: 5.33 us -> 2.64 us
  local copies, waits for them, and re-layouts: 4.16 us -> 2.43 us
  other arithmetic: 1.52 us -> 0 us
  blocking collectives: 8.61 us -> 7.22 us
  Pallas kernels: 10.2 us -> 8.9 us
    ppermute x3, waiting for transfers between devices: 5.33 us -> 1.3 us  [local(): lax.ppermute(block, 'group', [(i, goes_to(i)) for i in range(groups)])]
    unnamed x13, local copies, waits for them, and re-layouts: 4.16 us -> 2.43 us
    concatenate x1 -> x0, other arithmetic: 1.52 us -> none  [local(): jnp.concatenate([by_head.reshape(KV_HEADS, Q_PER_KV * steps, HEAD_DIM), k...]
    all_to_all x1, blocking collectives: 8.61 us -> 7.22 us  [local(): returned = lax.all_to_all(blended, MEMBERS, 0, 0)]
    all_to_all x1, waiting for transfers between devices: 0.01 us -> 1.33 us  [local(): recent = lax.all_to_all(packed, MEMBERS, 0, 0)]
    all_to_all x1, starting transfers between devices: 5.17 us -> 3.87 us  [local(): recent = lax.all_to_all(packed, MEMBERS, 0, 0)]
    ppermute x3, starting transfers between devices: 4.45 us -> 5.76 us  [local(): lax.ppermute(block, 'group', [(i, goes_to(i)) for i in range(groups)])]
    pallas_call x1, Pallas kernels: 2.08 us -> 1.41 us  [attend(): pl.pallas_call(functools.partial(attend_kernel, groups, steps), in_specs=...]
  transfers between devices with their start and end apart: 4 -> 4, of which waited for: 2 -> 2; matrix products, arithmetic and copies ran while one was open for 0% -> 0% of each run, Pallas kernels for 20% -> 4%
where the time goes in v2:
time: 31.8 us; the launch traced here: 31.5 us
  starting transfers between devices  9.62 us (30%)
  Pallas kernels  8.9 us (28%)
  blocking collectives  7.22 us (23%)
  waiting for transfers between devices  2.64 us (8%)
  local copies, waits for them, and re-layouts  2.43 us (8%)
  between operations  0.69 us (2%)
    all_to_all x1, blocking collectives, local(): returned = lax.all_to_all(blended, MEMBERS, 0, 0)  7.22 us
    pallas_call x1, Pallas kernels, project(): pl.pallas_call(functools.partial(project_kernel, groups, ordered), in_spe...  6.1 us
    ppermute x3, starting transfers between devices, local(): lax.ppermute(block, 'group', [(i, goes_to(i)) for i in range(groups)])  5.76 us
    all_to_all x1, starting transfers between devices, local(): recent = lax.all_to_all(packed, MEMBERS, 0, 0)  3.87 us
    unnamed x13, local copies, waits for them, and re-layouts  2.43 us
    pallas_call x1, Pallas kernels, attend(): pl.pallas_call(functools.partial(attend_kernel, groups, steps), in_specs=...  1.41 us
    pallas_call x1, Pallas kernels, store(): pl.pallas_call(functools.partial(store_kernel, groups), in_specs=[pl.Bloc...  1.39 us
    all_to_all x1, waiting for transfers between devices, local(): recent = lax.all_to_all(packed, MEMBERS, 0, 0)  1.33 us
  transfers between devices with their start and end apart: 4, of which 2 were waited for; matrix products, arithmetic and copies ran while one was open for 0% of the time, Pallas kernels for 4%

profile of v2, /device:TPU:0, one launch (start us, length us, event | category | flops | bytes accessed | tf_op | source)
XLA Modules:
  0.0 31.5 jit_solution(3758427921270174170)
XLA Ops:
  0.6 0.0 copy-start.5
  0.6 6.1 %project.1 = (bf16[128,256]{1,0:T(8,128)(2,1)}, bf16[128,256]{1,0:T(8,128)(2,1)}, bf16[128,256]{1,0:T(8,128)(2,1)}, bf16[128,256]{1,0:T(8,128)(2,1)}, bf16[8,40,128]{2,1,0:T(8,128)(2,1)}) custom-call(s32[4]{0:T(128)} %prompt_ref.1, bf16[4,128,8192]{2,1,0:T(8,128)(2,1)} %x_hbm.1, bf16[8192,256]{1,0:T(8,128)(2,1)} %w_hbm.1, f32[1,256]{1,0:T(1,128)} %bitcast.33, ...), custom_call_target="tpu_custom_call" | custom-call | tf_op jit(solution)/shard_map/project/pallas_call | solution.py:129
  6.7 5.1 %collective-permute-start = (bf16[128,256]{1,0:T(8,128)(2,1)}, bf16[128,256]{1,0:T(8,128)(2,1)S(1)}, u32[]{:S(2)}, u32[]{:S(2)}) collective-permute-start(bf16[128,256]{1,0:T(8,128)(2,1)} %get-tuple-element.7), channel_id=1, source_target_pairs={{0,24},{8,16},{16,8},{24,0},{1,25},{9,17},{17,9},{25,1},{2,26},{10... | collective-permute-start | bytes 196616 | tf_op jit(solution)/shard_map/ppermute | solution.py:292
  11.9 0.0 collective-permute-start.1
  11.9 0.6 %collective-permute-start.2 = (bf16[128,256]{1,0:T(8,128)(2,1)}, bf16[128,256]{1,0:T(8,128)(2,1)S(1)}, u32[]{:S(2)}, u32[]{:S(2)}) collective-permute-start(bf16[128,256]{1,0:T(8,128)(2,1)} %get-tuple-element.9), channel_id=1, source_target_pairs={{0,8},{8,0},{16,24},{24,16},{1,9},{9,1},{17,25},{25,17},{2,10},{10... | collective-permute-start | bytes 196616 | tf_op jit(solution)/shard_map/ppermute | solution.py:292
  12.5 3.9 %all-to-all-start = ((bf16[8,40,128]{2,1,0:T(8,128)(2,1)}), bf16[8,40,128]{2,1,0:T(8,128)(2,1)S(1)}, u32[]{:S(2)}, u32[]{:S(2)}) async-start(bf16[8,40,128]{2,1,0:T(8,128)(2,1)} %get-tuple-element.11), calls=%async_computation | async-start | bytes 163840 | tf_op jit(solution)/shard_map/all_to_all | solution.py:299
  16.4 0.0 collective-permute-done
  16.4 1.3 %collective-permute-done.1 = bf16[128,256]{1,0:T(8,128)(2,1)S(1)} collective-permute-done((bf16[128,256]{1,0:T(8,128)(2,1)}, bf16[128,256]{1,0:T(8,128)(2,1)S(1)}, u32[]{:S(2)}, u32[]{:S(2)}) %collective-permute-start.1) | collective-permute-done | bytes 65568 | tf_op jit(solution)/shard_map/ppermute | solution.py:292
  17.7 0.0 collective-permute-done.2
  17.7 0.0 copy-done.5
  17.7 0.0 copy-start.1
  17.7 0.8 %copy-done.1 = bf16[128,256]{1,0:T(8,128)(2,1)S(1)} copy-done((bf16[128,256]{1,0:T(8,128)(2,1)S(1)}, bf16[128,256]{1,0:T(8,128)(2,1)}, u32[]{:S(2)}) %copy-start.1) | copy-done | bytes 65560
  18.5 0.0 copy-start.2
  18.5 0.0 copy-start.3
  18.5 0.0 copy-start.4
  18.5 1.4 %store.1.cache_ref = bf16[64,8,256]{2,1,0:T(8,128)(2,1)} custom-call(s32[1,64]{1,0:T(1,128)S(1)} %copy-done.5, bf16[16,8,256]{2,1,0:T(8,128)(2,1)S(1)} %bitcast.24, bf16[16,8,256]{2,1,0:T(8,128)(2,1)S(1)} %bitcast.26, bf16[16,8,256]{2,1,0:T(8,128)(2,1)S(1)} %bitcast.28, bf16[16,8,256]{2,1,0:T(8,128)(2,1)S(1)} %bitcast.22), custom_call_target="tpu_custom_call" | custom-call | flops 20000000000 | tf_op jit(solution)/shard_map/store/pallas_call | solution.py:173
  19.9 1.3 %all-to-all-done.recent_ref = bf16[8,40,128]{2,1,0:T(8,128)(2,1)S(1)} async-done(((bf16[8,40,128]{2,1,0:T(8,128)(2,1)}), bf16[8,40,128]{2,1,0:T(8,128)(2,1)S(1)}, u32[]{:S(2)}, u32[]{:S(2)}) %all-to-all-start) | async-done | bytes 81952 | tf_op jit(solution)/shard_map/all_to_all | solution.py:299
  21.3 0.0 copy-done.2
  21.3 0.0 copy-done.3
  21.3 0.0 copy-done.4
  21.3 0.0 copy-start
  21.3 0.9 %copy-done = bf16[64,8,256]{2,1,0:T(8,128)(2,1)S(1)} copy-done((bf16[64,8,256]{2,1,0:T(8,128)(2,1)S(1)}, bf16[64,8,256]{2,1,0:T(8,128)(2,1)}, u32[]{:S(2)}) %copy-start) | copy-done | bytes 262168
  22.2 1.4 %attend.1 = bf16[8,32,128]{2,1,0:T(8,128)(2,1)S(1)} custom-call(s32[4]{0:T(128)S(1)} %copy-done.3, s32[4]{0:T(128)S(1)} %copy-done.4, bf16[64,8,256]{2,1,0:T(8,128)(2,1)S(1)} %copy-done, bf16[8,40,128]{2,1,0:T(8,128)(2,1)S(1)} %all-to-all-done.recent_ref, bf16[16,8,256]{2,1,0:T(8,128)(2,1)S(1)} %bitcast.25, bf16[16,8,256]{2,1,0:T(8,128)(2,1)S(1)} %bitcast.27, ...), custom_call_target="tpu_custom_call" | custom-call | tf_op jit(solution)/shard_map/attend/pallas_call | solution.py:250
  23.6 7.2 %all_to_all.10 = bf16[8,32,128]{2,1,0:T(8,128)(2,1)S(1)} all-to-all(bf16[8,32,128]{2,1,0:T(8,128)(2,1)S(1)} %attend.1), channel_id=1, replica_groups=mesh['group'=4,'tp'=4,'fork'=2] {'tp','fork'}, dimensions={0} | all-to-all | bytes 131072 | tf_op jit(solution)/shard_map/all_to_all | solution.py:303
  30.9 0.6 %copy.14 = bf16[1,1,4,8192]{3,2,1,0:T(4,128)(2,1)} copy(bf16[1,1,4,8192]{3,2,1,0:T(4,128)(2,1)S(1)} %bitcast.30) | data formatting | bytes 131072
Async XLA Ops:
  0.6 17.0 %copy-start.5 = (s32[1,64]{1,0:T(1,128)S(1)}, s32[1,64]{1,0:T(1,128)}, u32[]{:S(2)}) copy-start(s32[1,64]{1,0:T(1,128)} %table_ref.1) | copy-start | bytes 772
  6.7 9.6 %collective-permute-start = (bf16[128,256]{1,0:T(8,128)(2,1)}, bf16[128,256]{1,0:T(8,128)(2,1)S(1)}, u32[]{:S(2)}, u32[]{:S(2)}) collective-permute-start(bf16[128,256]{1,0:T(8,128)(2,1)} %get-tuple-element.7), channel_id=1, source_target_pairs={{0,24},{8,16},{16,8},{24,0},{1,25},{9,17},{17,9},{25,1},{2,26},{10... | collective-permute-start | bytes 196616 | tf_op jit(solution)/shard_map/ppermute | solution.py:292
  11.9 5.8 %collective-permute-start.1 = (bf16[128,256]{1,0:T(8,128)(2,1)}, bf16[128,256]{1,0:T(8,128)(2,1)S(1)}, u32[]{:S(2)}, u32[]{:S(2)}) collective-permute-start(bf16[128,256]{1,0:T(8,128)(2,1)} %get-tuple-element.8), channel_id=1, source_target_pairs={{0,16},{8,24},{16,0},{24,8},{1,17},{9,25},{17,1},{25,9},{2,18},{10... | collective-permute-start | bytes 196616 | tf_op jit(solution)/shard_map/ppermute | solution.py:292
  11.9 5.8 %collective-permute-start.2 = (bf16[128,256]{1,0:T(8,128)(2,1)}, bf16[128,256]{1,0:T(8,128)(2,1)S(1)}, u32[]{:S(2)}, u32[]{:S(2)}) collective-permute-start(bf16[128,256]{1,0:T(8,128)(2,1)} %get-tuple-element.9), channel_id=1, source_target_pairs={{0,8},{8,0},{16,24},{24,16},{1,9},{9,1},{17,25},{25,17},{2,10},{10... | collective-permute-start | bytes 196616 | tf_op jit(solution)/shard_map/ppermute | solution.py:292
  12.5 8.8 %all-to-all-start = ((bf16[8,40,128]{2,1,0:T(8,128)(2,1)}), bf16[8,40,128]{2,1,0:T(8,128)(2,1)S(1)}, u32[]{:S(2)}, u32[]{:S(2)}) async-start(bf16[8,40,128]{2,1,0:T(8,128)(2,1)} %get-tuple-element.11), calls=%async_computation | async-start | bytes 163840 | tf_op jit(solution)/shard_map/all_to_all | solution.py:299
  17.7 0.8 %copy-start.1 = (bf16[128,256]{1,0:T(8,128)(2,1)S(1)}, bf16[128,256]{1,0:T(8,128)(2,1)}, u32[]{:S(2)}) copy-start(bf16[128,256]{1,0:T(8,128)(2,1)} %get-tuple-element.10) | copy-start | bytes 196612
  18.5 2.7 %copy-start.2 = (bf16[128,256]{1,0:T(8,128)(2,1)S(1)}, bf16[128,256]{1,0:T(8,128)(2,1)}, u32[]{:S(2)}) copy-start(bf16[128,256]{1,0:T(8,128)(2,1)} %get-tuple-element.10) | copy-start | bytes 196612
  18.5 2.7 %copy-start.3 = (s32[4]{0:T(128)S(1)}, s32[4]{0:T(128)}, u32[]{:S(2)}) copy-start(s32[4]{0:T(128)} %prompt_ref.1) | copy-start | bytes 52
  18.5 2.7 %copy-start.4 = (s32[4]{0:T(128)S(1)}, s32[4]{0:T(128)}, u32[]{:S(2)}) copy-start(s32[4]{0:T(128)} %count_ref.1) | copy-start | bytes 52
  21.3 1.0 %copy-start = (bf16[64,8,256]{2,1,0:T(8,128)(2,1)S(1)}, bf16[64,8,256]{2,1,0:T(8,128)(2,1)}, u32[]{:S(2)}) copy-start(bf16[64,8,256]{2,1,0:T(8,128)(2,1)} %store.1.cache_ref) | copy-start | bytes 786436

commit v3 on v2

--- a/solution.py
+++ b/solution.py
@@ -15,8 +15,7 @@
 ROPE_BASE = 1000000.0
 MEMBERS = ("tp", "fork")
 CHUNK = 1024
-PROJECT_VMEM = 62 * 1024 * 1024
-VMEM_LIMIT = 48 * 1024 * 1024
+VMEM_LIMIT = 40 * 1024 * 1024
 PACK_VMEM = 4 * 1024 * 1024
 HIDE_FLOPS = 20 * 10**9
 
@@ -30,6 +29,10 @@
         (lambda me, s=s: (me + s) % groups, lambda me, s=s: (me + groups - s) % groups)
         for s in range(1, groups)
     ]
+
+
+def in_hbm(array):
+    return pltpu.with_memory_space_constraint(array, pltpu.HBM)
 
 
 def project_kernel(
@@ -43,9 +46,9 @@
     recent_hbm,
     *rest,
 ):
-    outs, packed_hbm, rest = rest[: x_hbm.shape[0]], rest[x_hbm.shape[0]], rest[x_hbm.shape[0] + 1 :]
-    prompt_ref, b_ref, query_ref, recent_ref, packed_ref, x_ref, w_ref, total_ref, out_ref = rest[:9]
-    small_sem, x_sem, w_sem, out_sem, packed_sem = rest[9:]
+    outs, packed_ref, rest = rest[: x_hbm.shape[0]], rest[x_hbm.shape[0]], rest[x_hbm.shape[0] + 1 :]
+    prompt_ref, b_ref, query_ref, recent_ref, x_ref, w_ref, total_ref = rest[:7]
+    small_sem, x_sem, w_sem = rest[7:]
     chunks, prompts, rows, depth = x_ref.shape
     small = [
         pltpu.make_async_copy(source, target, small_sem.at[at])
@@ -102,8 +105,6 @@
     q_rows = query_ref.shape[1]
     packed_ref[:, :q_rows, :] = query_ref[...]
     packed_ref[:, q_rows:, :] = recent_ref[...]
-    pack = pltpu.make_async_copy(packed_ref, packed_hbm, packed_sem)
-    pack.start()
     lax.fori_loop(early, chunks, accumulate, 0)
     for at, out in enumerate(outs):
         prompt = at
@@ -112,12 +113,8 @@
         total = total_ref[prompt] + b_ref[...]
         key = total[:, :HEAD_DIM]
         swapped = jnp.concatenate([key[:, half:], key[:, :half]], axis=1)
-        out_ref[at, :, :HEAD_DIM] = (key * cosine + swapped * sine).astype(out.dtype)
-        out_ref[at, :, HEAD_DIM:] = total[:, HEAD_DIM:].astype(out.dtype)
-        pltpu.make_async_copy(out_ref.at[at], out, out_sem.at[at]).start()
-    pack.wait()
-    for at, out in enumerate(outs):
-        pltpu.make_async_copy(out_ref.at[at], out, out_sem.at[at]).wait()
+        out[:, :HEAD_DIM] = (key * cosine + swapped * sine).astype(out.dtype)
+        out[:, HEAD_DIM:] = total[:, HEAD_DIM:].astype(out.dtype)
 
 
 def project(groups, ordered, decode_prompt, prompt_hidden, kv_weight, kv_bias, query, recent):
@@ -125,32 +122,28 @@
     width = kv_weight.shape[1]
     chunks = depth // CHUNK
     packed_shape = (query.shape[0], query.shape[1] + recent.shape[1], HEAD_DIM)
-    anywhere = pl.BlockSpec(memory_space=pl.ANY)
+    operands = (decode_prompt, prompt_hidden, kv_weight, kv_bias.reshape(1, width), query, recent)
     return pl.pallas_call(
         functools.partial(project_kernel, groups, ordered),
-        in_specs=[anywhere] * 6,
-        out_specs=[anywhere] * (prompts + 1),
-        out_shape=[jax.ShapeDtypeStruct((rows, width), jnp.bfloat16)] * prompts
-        + [jax.ShapeDtypeStruct(packed_shape, query.dtype)],
+        in_specs=[pl.BlockSpec(memory_space=pl.ANY)] * len(operands),
+        out_specs=[pl.BlockSpec(memory_space=pltpu.VMEM)] * (prompts + 1),
+        out_shape=[pltpu.VMEM((rows, width), jnp.bfloat16)] * prompts
+        + [pltpu.VMEM(packed_shape, query.dtype)],
         scratch_shapes=[
             pltpu.SMEM(decode_prompt.shape, jnp.int32),
             pltpu.VMEM((1, width), jnp.float32),
             pltpu.VMEM(query.shape, query.dtype),
             pltpu.VMEM(recent.shape, recent.dtype),
-            pltpu.VMEM(packed_shape, query.dtype),
             pltpu.VMEM((chunks, prompts, rows, CHUNK), jnp.bfloat16),
             pltpu.VMEM((chunks, CHUNK, width), jnp.bfloat16),
             pltpu.VMEM((prompts, rows, width), jnp.float32),
-            pltpu.VMEM((prompts, rows, width), jnp.bfloat16),
             pltpu.SemaphoreType.DMA((4,)),
             pltpu.SemaphoreType.DMA((chunks,)),
             pltpu.SemaphoreType.DMA((chunks,)),
-            pltpu.SemaphoreType.DMA((prompts,)),
-            pltpu.SemaphoreType.DMA,
         ],
-        compiler_params=pltpu.CompilerParams(vmem_limit_bytes=PROJECT_VMEM),
+        compiler_params=pltpu.CompilerParams(vmem_limit_bytes=VMEM_LIMIT),
         name="project",
-    )(decode_prompt, prompt_hidden, kv_weight, kv_bias.reshape(1, width), query, recent)
+    )(*map(in_hbm, operands))
 
 
 def store_kernel(groups, table_ref, *rest):
@@ -254,7 +247,7 @@
         out_shape=jax.ShapeDtypeStruct((samples, Q_PER_KV * steps, HEAD_DIM), jnp.bfloat16),
         compiler_params=pltpu.CompilerParams(vmem_limit_bytes=VMEM_LIMIT),
         name="attend",
-    )(decode_prompt, sample_counts, cache, recent, *blocks)
+    )(decode_prompt, sample_counts, in_hbm(cache), recent, *blocks)
 
 
 def local(

time: 31.8 us -> 30.7 us (0.965)
  local copies, waits for them, and re-layouts: 2.43 us -> 0.64 us
  waiting for transfers between devices: 2.64 us -> 3.46 us
    unnamed x13 -> x7, local copies, waits for them, and re-layouts: 2.43 us -> 0.64 us
    all_to_all x1, waiting for transfers between devices: 1.33 us -> 2.37 us  [local(): recent = lax.all_to_all(packed, MEMBERS, 0, 0)]
  transfers between devices with their start and end apart: 4 -> 4, of which waited for: 2 -> 2; matrix products, arithmetic and copies ran while one was open for 0% -> 0% of each run, Pallas kernels for 4% -> 5%
where the time goes in v3:
time: 30.7 us; the launch traced here: 30.4 us
  starting transfers between devices  9.62 us (31%)
  Pallas kernels  8.76 us (29%)
  blocking collectives  7.22 us (24%)
  waiting for transfers between devices  3.46 us (11%)
  between operations  0.68 us (2%)
  local copies, waits for them, and re-layouts  0.64 us (2%)
    all_to_all x1, blocking collectives, local(): returned = lax.all_to_all(blended, MEMBERS, 0, 0)  7.22 us
    pallas_call x1, Pallas kernels, project(): pl.pallas_call(functools.partial(project_kernel, groups, ordered), in_spe...  5.96 us
    ppermute x3, starting transfers between devices, local(): lax.ppermute(block, 'group', [(i, goes_to(i)) for i in range(groups)])  5.76 us
    all_to_all x1, starting transfers between devices, local(): recent = lax.all_to_all(packed, MEMBERS, 0, 0)  3.87 us
    all_to_all x1, waiting for transfers between devices, local(): recent = lax.all_to_all(packed, MEMBERS, 0, 0)  2.37 us
    pallas_call x1, Pallas kernels, attend(): pl.pallas_call(functools.partial(attend_kernel, groups, steps), in_specs=...  1.41 us
    pallas_call x1, Pallas kernels, store(): pl.pallas_call(functools.partial(store_kernel, groups), in_specs=[pl.Bloc...  1.39 us
    ppermute x3, waiting for transfers between devices, local(): lax.ppermute(block, 'group', [(i, goes_to(i)) for i in range(groups)])  1.09 us
  transfers between devices with their start and end apart: 4, of which 2 were waited for; matrix products, arithmetic and copies ran while one was open for 0% of the time, Pallas kernels for 5%

profile of v3, /device:TPU:0, one launch (start us, length us, event | category | flops | bytes accessed | tf_op | source)
XLA Modules:
  0.0 30.4 jit_solution(6917706821854121585)
XLA Ops:
  0.6 0.0 copy-start.2
  0.6 6.0 %project.1 = (bf16[128,256]{1,0:T(8,128)(2,1)S(1)}, bf16[128,256]{1,0:T(8,128)(2,1)S(1)}, bf16[128,256]{1,0:T(8,128)(2,1)S(1)}, bf16[128,256]{1,0:T(8,128)(2,1)S(1)}, bf16[8,40,128]{2,1,0:T(8,128)(2,1)}) custom-call(s32[4]{0:T(128)} %prompt_ref.1, bf16[4,128,8192]{2,1,0:T(8,128)(2,1)} %x_hbm.1, bf16[8192,256]{1,0:T(8,128)(2,1)} %w_hbm.1, f32[1,256]{1,0:T(1,128)} %bitcast.33, ...), custom_call_target="tpu_custom_call" | custom-call | tf_op jit(solution)/shard_map/project/pallas_call | solution.py:126
  6.6 5.1 %collective-permute-start = (bf16[128,256]{1,0:T(8,128)(2,1)S(1)}, bf16[128,256]{1,0:T(8,128)(2,1)S(1)}, u32[]{:S(2)}, u32[]{:S(2)}) collective-permute-start(bf16[128,256]{1,0:T(8,128)(2,1)S(1)} %get-tuple-element.7), channel_id=1, source_target_pairs={{0,24},{8,16},{16,8},{24,0},{1,25},{9,17},{17,9},{25,1},{2,26},{10... | collective-permute-start | bytes 196616 | tf_op jit(solution)/shard_map/ppermute | solution.py:285
  11.7 0.0 collective-permute-start.1
  11.7 0.6 %collective-permute-start.2 = (bf16[128,256]{1,0:T(8,128)(2,1)S(1)}, bf16[128,256]{1,0:T(8,128)(2,1)S(1)}, u32[]{:S(2)}, u32[]{:S(2)}) collective-permute-start(bf16[128,256]{1,0:T(8,128)(2,1)S(1)} %get-tuple-element.9), channel_id=1, source_target_pairs={{0,8},{8,0},{16,24},{24,16},{1,9},{9,1},{17,25},{25,17},{2,10},{10... | collective-permute-start | bytes 196616 | tf_op jit(solution)/shard_map/ppermute | solution.py:285
  12.4 3.9 %all-to-all-start = ((bf16[8,40,128]{2,1,0:T(8,128)(2,1)}), bf16[8,40,128]{2,1,0:T(8,128)(2,1)S(1)}, u32[]{:S(2)}, u32[]{:S(2)}) async-start(bf16[8,40,128]{2,1,0:T(8,128)(2,1)} %get-tuple-element.11), calls=%async_computation | async-start | bytes 163840 | tf_op jit(solution)/shard_map/all_to_all | solution.py:292
  16.2 0.0 collective-permute-done
  16.2 1.1 %collective-permute-done.1 = bf16[128,256]{1,0:T(8,128)(2,1)S(1)} collective-permute-done((bf16[128,256]{1,0:T(8,128)(2,1)S(1)}, bf16[128,256]{1,0:T(8,128)(2,1)S(1)}, u32[]{:S(2)}, u32[]{:S(2)}) %collective-permute-start.1) | collective-permute-done | bytes 65568 | tf_op jit(solution)/shard_map/ppermute | solution.py:285
  17.3 0.0 collective-permute-done.2
  17.3 0.0 copy-done.2
  17.3 0.0 copy-start
  17.3 0.0 copy-start.1
  17.4 1.4 %store.1.cache_ref = bf16[64,8,256]{2,1,0:T(8,128)(2,1)} custom-call(s32[1,64]{1,0:T(1,128)S(1)} %copy-done.2, bf16[16,8,256]{2,1,0:T(8,128)(2,1)S(1)} %bitcast.23, bf16[16,8,256]{2,1,0:T(8,128)(2,1)S(1)} %bitcast.25, bf16[16,8,256]{2,1,0:T(8,128)(2,1)S(1)} %bitcast.27, bf16[16,8,256]{2,1,0:T(8,128)(2,1)S(1)} %bitcast.21), custom_call_target="tpu_custom_call" | custom-call | flops 20000000000 | tf_op jit(solution)/shard_map/store/pallas_call | solution.py:166
  18.7 2.4 %all-to-all-done.recent_ref = bf16[8,40,128]{2,1,0:T(8,128)(2,1)S(1)} async-done(((bf16[8,40,128]{2,1,0:T(8,128)(2,1)}), bf16[8,40,128]{2,1,0:T(8,128)(2,1)S(1)}, u32[]{:S(2)}, u32[]{:S(2)}) %all-to-all-start) | async-done | bytes 81952 | tf_op jit(solution)/shard_map/all_to_all | solution.py:292
  21.1 0.0 copy-done
  21.1 0.0 copy-done.1
  21.1 1.4 %attend.1 = bf16[8,32,128]{2,1,0:T(8,128)(2,1)S(1)} custom-call(s32[4]{0:T(128)S(1)} %copy-done, s32[4]{0:T(128)S(1)} %copy-done.1, bf16[64,8,256]{2,1,0:T(8,128)(2,1)} %store.1.cache_ref, bf16[8,40,128]{2,1,0:T(8,128)(2,1)S(1)} %all-to-all-done.recent_ref, bf16[16,8,256]{2,1,0:T(8,128)(2,1)S(1)} %bitcast.24, bf16[16,8,256]{2,1,0:T(8,128)(2,1)S(1)} %bitcast.26, ...), custom_call_target="tpu_custom_call" | custom-call | tf_op jit(solution)/shard_map/attend/pallas_call | solution.py:243
  22.5 7.2 %all_to_all.10 = bf16[8,32,128]{2,1,0:T(8,128)(2,1)S(1)} all-to-all(bf16[8,32,128]{2,1,0:T(8,128)(2,1)S(1)} %attend.1), channel_id=1, replica_groups=mesh['group'=4,'tp'=4,'fork'=2] {'tp','fork'}, dimensions={0} | all-to-all | bytes 131072 | tf_op jit(solution)/shard_map/all_to_all | solution.py:296
  29.8 0.6 %copy.14 = bf16[1,1,4,8192]{3,2,1,0:T(4,128)(2,1)} copy(bf16[1,1,4,8192]{3,2,1,0:T(4,128)(2,1)S(1)} %bitcast.30) | data formatting | bytes 131072
Async XLA Ops:
  0.6 16.7 %copy-start.2 = (s32[1,64]{1,0:T(1,128)S(1)}, s32[1,64]{1,0:T(1,128)}, u32[]{:S(2)}) copy-start(s32[1,64]{1,0:T(1,128)} %table_ref.1) | copy-start | bytes 772
  6.6 9.6 %collective-permute-start = (bf16[128,256]{1,0:T(8,128)(2,1)S(1)}, bf16[128,256]{1,0:T(8,128)(2,1)S(1)}, u32[]{:S(2)}, u32[]{:S(2)}) collective-permute-start(bf16[128,256]{1,0:T(8,128)(2,1)S(1)} %get-tuple-element.7), channel_id=1, source_target_pairs={{0,24},{8,16},{16,8},{24,0},{1,25},{9,17},{17,9},{25,1},{2,26},{10... | collective-permute-start | bytes 196616 | tf_op jit(solution)/shard_map/ppermute | solution.py:285
  11.7 5.6 %collective-permute-start.1 = (bf16[128,256]{1,0:T(8,128)(2,1)S(1)}, bf16[128,256]{1,0:T(8,128)(2,1)S(1)}, u32[]{:S(2)}, u32[]{:S(2)}) collective-permute-start(bf16[128,256]{1,0:T(8,128)(2,1)S(1)} %get-tuple-element.8), channel_id=1, source_target_pairs={{0,16},{8,24},{16,0},{24,8},{1,17},{9,25},{17,1},{25,9},{2,18},{10... | collective-permute-start | bytes 196616 | tf_op jit(solution)/shard_map/ppermute | solution.py:285
  11.7 5.6 %collective-permute-start.2 = (bf16[128,256]{1,0:T(8,128)(2,1)S(1)}, bf16[128,256]{1,0:T(8,128)(2,1)S(1)}, u32[]{:S(2)}, u32[]{:S(2)}) collective-permute-start(bf16[128,256]{1,0:T(8,128)(2,1)S(1)} %get-tuple-element.9), channel_id=1, source_target_pairs={{0,8},{8,0},{16,24},{24,16},{1,9},{9,1},{17,25},{25,17},{2,10},{10... | collective-permute-start | bytes 196616 | tf_op jit(solution)/shard_map/ppermute | solution.py:285
  12.4 8.8 %all-to-all-start = ((bf16[8,40,128]{2,1,0:T(8,128)(2,1)}), bf16[8,40,128]{2,1,0:T(8,128)(2,1)S(1)}, u32[]{:S(2)}, u32[]{:S(2)}) async-start(bf16[8,40,128]{2,1,0:T(8,128)(2,1)} %get-tuple-element.11), calls=%async_computation | async-start | bytes 163840 | tf_op jit(solution)/shard_map/all_to_all | solution.py:292
  17.3 3.8 %copy-start = (s32[4]{0:T(128)S(1)}, s32[4]{0:T(128)}, u32[]{:S(2)}) copy-start(s32[4]{0:T(128)} %prompt_ref.1) | copy-start | bytes 52
  17.3 3.8 %copy-start.1 = (s32[4]{0:T(128)S(1)}, s32[4]{0:T(128)}, u32[]{:S(2)}) copy-start(s32[4]{0:T(128)} %count_ref.1) | copy-start | bytes 52

commit v4 on v3

--- a/solution.py
+++ b/solution.py
@@ -31,6 +31,10 @@
     ]
 
 
+SIBLING = 2
+PEERS = (5, 4, 1)
+
+
 def in_hbm(array):
     return pltpu.with_memory_space_constraint(array, pltpu.HBM)
 
@@ -39,6 +43,7 @@
     groups,
     ordered,
     prompt_hbm,
+    count_hbm,
     x_hbm,
     w_hbm,
     b_hbm,
@@ -46,15 +51,18 @@
     recent_hbm,
     *rest,
 ):
-    outs, packed_ref, rest = rest[: x_hbm.shape[0]], rest[x_hbm.shape[0]], rest[x_hbm.shape[0] + 1 :]
-    prompt_ref, b_ref, query_ref, recent_ref, x_ref, w_ref, total_ref = rest[:7]
-    small_sem, x_sem, w_sem = rest[7:]
+    prompts = x_hbm.shape[0]
+    packets = len(PEERS) + 1
+    outs, packed, rest = rest[:prompts], rest[prompts : prompts + packets], rest[prompts + packets :]
+    alive_ref, prompt_ref, count_ref, b_ref, query_ref, recent_ref, x_ref, w_ref, total_ref = rest[:9]
+    small_sem, x_sem, w_sem = rest[9:]
     chunks, prompts, rows, depth = x_ref.shape
     small = [
         pltpu.make_async_copy(source, target, small_sem.at[at])
         for at, (source, target) in enumerate(
             [
                 (prompt_hbm, prompt_ref),
+                (count_hbm, count_ref),
                 (b_hbm, b_ref),
                 (recent_hbm, recent_ref),
                 (query_hbm, query_ref),
@@ -103,8 +111,21 @@
     for copy in small:
         copy.wait()
     q_rows = query_ref.shape[1]
-    packed_ref[:, :q_rows, :] = query_ref[...]
-    packed_ref[:, q_rows:, :] = recent_ref[...]
+    member = lax.axis_index(MEMBERS)
+    for distance, packet in zip(PEERS + (0,), packed):
+        for at in range(2):
+            head = member ^ distance ^ (SIBLING * at)
+            packet[at, :q_rows, :] = query_ref[head]
+            packet[at, q_rows:, :] = recent_ref[head]
+    own_prompt = prompt_ref[me]
+    earlier = jnp.int32(0)
+    for g in range(groups):
+        same = jnp.logical_and(g < me, prompt_ref[g] == own_prompt)
+        earlier = earlier + jnp.where(same, 1, 0)
+    limit = count_ref[own_prompt] - earlier * lax.axis_size(MEMBERS)
+    for at, distance in enumerate(PEERS + (0,)):
+        live = jnp.where((member ^ distance) < limit, 1.0, 0.0)
+        alive_ref[at * q_rows : (at + 1) * q_rows, :] = jnp.full((q_rows, HEAD_DIM), live)
     lax.fori_loop(early, chunks, accumulate, 0)
     for at, out in enumerate(outs):
         prompt = at
@@ -117,27 +138,30 @@
         out[:, HEAD_DIM:] = total[:, HEAD_DIM:].astype(out.dtype)
 
 
-def project(groups, ordered, decode_prompt, prompt_hidden, kv_weight, kv_bias, query, recent):
+def project(groups, ordered, decode_prompt, sample_counts, prompt_hidden, kv_weight, kv_bias, query, recent):
     prompts, rows, depth = prompt_hidden.shape
     width = kv_weight.shape[1]
     chunks = depth // CHUNK
-    packed_shape = (query.shape[0], query.shape[1] + recent.shape[1], HEAD_DIM)
-    operands = (decode_prompt, prompt_hidden, kv_weight, kv_bias.reshape(1, width), query, recent)
+    packet = pltpu.VMEM((2, query.shape[1] + recent.shape[1], HEAD_DIM), query.dtype)
+    packets = [packet] * (len(PEERS) + 1)
+    alive = pltpu.VMEM((len(packets) * query.shape[1], HEAD_DIM), jnp.float32)
+    bias = kv_bias.reshape(1, width)
+    operands = (decode_prompt, sample_counts, prompt_hidden, kv_weight, bias, query, recent)
     return pl.pallas_call(
         functools.partial(project_kernel, groups, ordered),
         in_specs=[pl.BlockSpec(memory_space=pl.ANY)] * len(operands),
-        out_specs=[pl.BlockSpec(memory_space=pltpu.VMEM)] * (prompts + 1),
-        out_shape=[pltpu.VMEM((rows, width), jnp.bfloat16)] * prompts
-        + [pltpu.VMEM(packed_shape, query.dtype)],
+        out_specs=[pl.BlockSpec(memory_space=pltpu.VMEM)] * (prompts + len(packets) + 1),
+        out_shape=[pltpu.VMEM((rows, width), jnp.bfloat16)] * prompts + packets + [alive],
         scratch_shapes=[
             pltpu.SMEM(decode_prompt.shape, jnp.int32),
+            pltpu.SMEM(sample_counts.shape, jnp.int32),
             pltpu.VMEM((1, width), jnp.float32),
             pltpu.VMEM(query.shape, query.dtype),
             pltpu.VMEM(recent.shape, recent.dtype),
             pltpu.VMEM((chunks, prompts, rows, CHUNK), jnp.bfloat16),
             pltpu.VMEM((chunks, CHUNK, width), jnp.bfloat16),
             pltpu.VMEM((prompts, rows, width), jnp.float32),
-            pltpu.SemaphoreType.DMA((4,)),
+            pltpu.SemaphoreType.DMA((5,)),
             pltpu.SemaphoreType.DMA((chunks,)),
             pltpu.SemaphoreType.DMA((chunks,)),
         ],
@@ -176,26 +200,42 @@
     )(page_table, *blocks)
 
 
-def attend_kernel(groups, steps, prompt_ref, count_ref, cache_ref, recent_ref, *rest):
-    del cache_ref
-    blocks, out_ref = rest[:groups], rest[groups]
-    me = lax.axis_index("group")
-    samples = recent_ref.shape[0]
-    pages = blocks[0].shape[0]
-    own_prompt = prompt_ref[me]
-    earlier = jnp.int32(0)
-    for g in range(groups):
-        same = jnp.logical_and(g < me, prompt_ref[g] == own_prompt)
-        earlier = earlier + jnp.where(same, 1, 0)
-    live = count_ref[own_prompt] - earlier * samples
-
+def arrange_kernel(steps, *refs):
+    packets, (query_ref, key_ref, value_ref) = refs[:-3], refs[-3:]
     q_rows = Q_PER_KV * steps
-    rows = samples * q_rows
+    for at in range(2):
+        recent = jnp.concatenate(
+            [packet[at, q_rows:, :].astype(jnp.float32) for packet in packets], axis=0
+        )
+        shifted = jnp.concatenate([recent[steps:], recent[:steps]], axis=0)
+        key_ref[at] = recent.astype(key_ref.dtype)
+        value_ref[at] = shifted.astype(value_ref.dtype)
+        for sample, packet in enumerate(packets):
+            query_ref[at, sample * q_rows : (sample + 1) * q_rows, :] = packet[at, :q_rows, :]
+
+
+def arrange(steps, packets):
+    samples, dtype = len(packets), packets[0].dtype
+    vmem = pl.BlockSpec(memory_space=pltpu.VMEM)
+    recent = pltpu.VMEM((2, samples * 2 * steps, HEAD_DIM), dtype)
+    return pl.pallas_call(
+        functools.partial(arrange_kernel, steps),
+        in_specs=[vmem] * samples,
+        out_specs=[vmem] * 3,
+        out_shape=[
+            pltpu.VMEM((2, samples * Q_PER_KV * steps, HEAD_DIM), dtype),
+            recent,
+            recent,
+        ],
+        cost_estimate=pl.CostEstimate(flops=HIDE_FLOPS, transcendentals=0, bytes_accessed=0),
+        compiler_params=pltpu.CompilerParams(vmem_limit_bytes=PACK_VMEM),
+        name="arrange",
+    )(*packets)
+
+
+def attend_head(steps, alive, query, recent_key, recent_value, blocks):
+    q_rows = Q_PER_KV * steps
     scaling = HEAD_DIM ** (-0.5)
-    query = recent_ref[:, :q_rows, :].reshape(rows, HEAD_DIM)
-    recent = recent_ref[:, q_rows:, :].astype(jnp.float32).reshape(samples * 2 * steps, HEAD_DIM)
-    recent_key = recent.astype(jnp.bfloat16)
-    recent_value = jnp.concatenate([recent[steps:], recent[:steps]], axis=0).astype(jnp.bfloat16)
     contract = (((1,), (1,)), ((), ()))
 
     def scored(keys):
@@ -210,44 +250,79 @@
         row // q_rows == column // (2 * steps), column % (2 * steps) <= row % steps
     )
     recent_score = jnp.where(visible, recent_score, -jnp.inf)
-    flat = [block[...].reshape(pages * PAGE, 2 * HEAD_DIM) for block in blocks]
-    scores = [scored(block[:, :HEAD_DIM]) for block in flat]
-    highest = jnp.max(recent_score, axis=1, keepdims=True)
-    for score in scores:
-        highest = jnp.maximum(highest, jnp.max(score, axis=1, keepdims=True))
+    scores = [scored(block[:, :HEAD_DIM]) for block in blocks]
+    highest = functools.reduce(jnp.maximum, scores).max(axis=1, keepdims=True)
+    highest = jnp.maximum(highest, jnp.max(recent_score, axis=1, keepdims=True))
     recent_weight = jnp.exp(recent_score - highest)
     weights = [jnp.exp(score - highest) for score in scores]
-    total = jnp.sum(recent_weight, axis=1, keepdims=True)
-    for weight in weights:
-        total = total + jnp.sum(weight, axis=1, keepdims=True)
+    total = functools.reduce(jnp.add, weights).sum(axis=1, keepdims=True)
+    total = total + jnp.sum(recent_weight, axis=1, keepdims=True)
     blended = jnp.dot(
-        (recent_weight / total).astype(jnp.bfloat16),
-        recent_value,
-        preferred_element_type=jnp.float32,
-    )
-    for weight, block in zip(weights, flat):
+        recent_weight.astype(jnp.bfloat16), recent_value, preferred_element_type=jnp.float32
+    )
+    for weight, block in zip(weights, blocks):
         blended = blended + jnp.dot(
-            (weight / total).astype(jnp.bfloat16),
-            block[:, HEAD_DIM:],
-            preferred_element_type=jnp.float32,
-        )
-    sample = lax.broadcasted_iota(jnp.int32, blended.shape, 0) // q_rows
-    blended = jnp.where(sample < live, blended, 0.0)
-    out_ref[...] = blended.astype(jnp.bfloat16).reshape(samples, q_rows, HEAD_DIM)
-
-
-def attend(groups, steps, decode_prompt, sample_counts, cache, recent, blocks):
-    samples = recent.shape[0]
-    smem = pl.BlockSpec(memory_space=pltpu.SMEM)
+            weight.astype(jnp.bfloat16), block[:, HEAD_DIM:], preferred_element_type=jnp.float32
+        )
+    blended = blended / total
+    return jnp.where(alive > 0.0, blended, 0.0)
+
+
+def attend_kernel(groups, steps, alive_ref, *rest):
+    arranged, rest = rest[:3], rest[3:]
+    head_blocks, outs = (rest[:groups], rest[groups : 2 * groups]), rest[2 * groups :]
+    q_rows = Q_PER_KV * steps
+    for at, refs in enumerate(head_blocks):
+        blended = attend_head(
+            steps,
+            alive_ref[...],
+            *[ref[at] for ref in arranged],
+            [block[...] for block in refs],
+        ).astype(jnp.bfloat16)
+        for to, out in enumerate(outs):
+            out[at] = blended[to * q_rows : (to + 1) * q_rows]
+
+
+def attend(groups, steps, alive, arranged, own_blocks, sibling_blocks):
+    packets = len(PEERS) + 1
     vmem = pl.BlockSpec(memory_space=pltpu.VMEM)
     return pl.pallas_call(
         functools.partial(attend_kernel, groups, steps),
-        in_specs=[smem, smem, pl.BlockSpec(memory_space=pl.ANY), vmem] + [vmem] * groups,
-        out_specs=vmem,
-        out_shape=jax.ShapeDtypeStruct((samples, Q_PER_KV * steps, HEAD_DIM), jnp.bfloat16),
+        in_specs=[vmem] * (1 + len(arranged) + 2 * groups),
+        out_specs=[vmem] * packets,
+        out_shape=[pltpu.VMEM((2, Q_PER_KV * steps, HEAD_DIM), jnp.bfloat16)] * packets,
         compiler_params=pltpu.CompilerParams(vmem_limit_bytes=VMEM_LIMIT),
         name="attend",
-    )(decode_prompt, sample_counts, in_hbm(cache), recent, *blocks)
+    )(alive, *arranged, *own_blocks, *sibling_blocks)
+
+
+def gather_kernel(*refs):
+    parts, out_ref, sem = refs[:-2], refs[-2], refs[-1]
+    member = lax.axis_index(MEMBERS)
+    copies = []
+    for distance, part in zip(PEERS + (0,), parts):
+        for at in range(2):
+            head = member ^ distance ^ (SIBLING * at)
+            copies.append(
+                pltpu.make_async_copy(part.at[at], out_ref.at[head], sem.at[len(copies)])
+            )
+    for copy in copies:
+        copy.start()
+    for copy in copies:
+        copy.wait()
+
+
+def gather(parts):
+    heads, rows, width = 2 * len(parts), parts[0].shape[1], parts[0].shape[2]
+    return pl.pallas_call(
+        gather_kernel,
+        in_specs=[pl.BlockSpec(memory_space=pltpu.VMEM)] * len(parts),
+        out_specs=pl.BlockSpec(memory_space=pl.ANY),
+        out_shape=pltpu.HBM((heads, rows, width), parts[0].dtype),
+        scratch_shapes=[pltpu.SemaphoreType.DMA((heads,))],
+        compiler_params=pltpu.CompilerParams(vmem_limit_bytes=PACK_VMEM),
+        name="gather",
+    )(*parts)
 
 
 def local(
@@ -261,16 +336,18 @@
 
     by_head = new_query.reshape(steps, KV_HEADS, Q_PER_KV, HEAD_DIM).transpose(1, 2, 0, 3)
     kv_by_head = new_kv.reshape(steps, KV_HEADS, 2, HEAD_DIM).transpose(1, 2, 0, 3)
-    *projected, packed = project(
+    results = project(
         groups,
         ordered,
         decode_prompt,
+        sample_counts,
         prompt_hidden,
         kv_weight,
         kv_bias,
         by_head.reshape(KV_HEADS, Q_PER_KV * steps, HEAD_DIM),
         kv_by_head.reshape(KV_HEADS, 2 * steps, HEAD_DIM),
     )
+    projected, packets, alive = results[:prompts], results[prompts:-1], results[-1]
     if ordered:
         outgoing, own = projected[:-1], projected[-1]
     else:
@@ -285,15 +362,23 @@
         lax.ppermute(block, "group", [(i, goes_to(i)) for i in range(groups)])
         for block, (goes_to, _) in zip(outgoing, partners(groups))
     ]
-    blocks = [
-        block.reshape(rows // PAGE, PAGE, 2 * HEAD_DIM) for block in blocks + [own]
-    ]
-
-    recent = lax.all_to_all(packed, MEMBERS, 0, 0)
-
-    cache = store(groups, page_table, blocks)
-    blended = attend(groups, steps, decode_prompt, sample_counts, cache, recent, blocks)
-    returned = lax.all_to_all(blended, MEMBERS, 0, 0)
+    members = lax.axis_size(MEMBERS)
+
+    def to_peer(array, distance):
+        return lax.ppermute(array, MEMBERS, [(i, i ^ distance) for i in range(members)])
+
+    packets = [to_peer(packet, at) for packet, at in zip(packets, PEERS)] + [packets[-1]]
+    blocks = blocks + [own]
+    sibling_blocks = [to_peer(block, SIBLING) for block in blocks]
+    parts = attend(
+        groups, steps, alive, arrange(steps, packets), blocks, sibling_blocks
+    )
+    cache = store(
+        groups,
+        page_table,
+        [block.reshape(rows // PAGE, PAGE, 2 * HEAD_DIM) for block in blocks],
+    )
+    returned = gather([to_peer(part, at) for part, at in zip(parts, PEERS)] + [parts[-1]])
     attention_out = returned.reshape(KV_HEADS * Q_PER_KV, steps, HEAD_DIM).transpose(1, 0, 2)
     return attention_out.reshape(new_query.shape), cache[None]
 

time: 30.7 us -> 29 us (0.945)
  blocking collectives: 7.22 us -> 0 us
  starting transfers between devices: 9.62 us -> 15.1 us
  waiting for transfers between devices: 3.46 us -> 4.66 us
  local copies, waits for them, and re-layouts: 0.64 us -> 0.01 us
  Pallas kernels: 8.76 us -> 8.43 us
    ppermute x0 -> x10, starting transfers between devices: none -> 9.31 us  [to_peer(): lax.ppermute(array, MEMBERS, [(i, i ^ distance) for i in range(members)])]
    all_to_all x1 -> x0, blocking collectives: 7.22 us -> none  [local(): returned = lax.all_to_all(blended, MEMBERS, 0, 0)]
    ppermute x0 -> x10, waiting for transfers between devices: none -> 4.65 us  [to_peer(): lax.ppermute(array, MEMBERS, [(i, i ^ distance) for i in range(members)])]
    all_to_all x1 -> x0, starting transfers between devices: 3.87 us -> none  [local(): recent = lax.all_to_all(packed, MEMBERS, 0, 0)]
    all_to_all x1 -> x0, waiting for transfers between devices: 2.37 us -> none  [local(): recent = lax.all_to_all(packed, MEMBERS, 0, 0)]
    ppermute x3, waiting for transfers between devices: 1.09 us -> 0.01 us  [local(): lax.ppermute(block, 'group', [(i, goes_to(i)) for i in range(groups)])]
    pallas_call x0 -> x2, Pallas kernels: none -> 0.71 us  [the longest x1 0.69 us: gather(): pl.pallas_call(gather_kernel, in_specs=[pl.BlockSpec(memory_space=pltpu.V...]
    unnamed x7 -> x2, local copies, waits for them, and re-layouts: 0.64 us -> 0.01 us
  transfers between devices with their start and end apart: 4 -> 13, of which waited for: 2 -> 5; matrix products, arithmetic and copies ran while one was open for 0% -> 0% of each run, Pallas kernels for 5% -> 5%
where the time goes in v4:
time: 29 us; the launch traced here: 28.9 us
  starting transfers between devices  15.1 us (52%)
  Pallas kernels  8.43 us (29%)
  waiting for transfers between devices  4.66 us (16%)
  between operations  0.71 us (2%)
    ppermute x10, starting transfers between devices, to_peer(): lax.ppermute(array, MEMBERS, [(i, i ^ distance) for i in range(members)])  9.31 us
    ppermute x3, starting transfers between devices, local(): lax.ppermute(block, 'group', [(i, goes_to(i)) for i in range(groups)])  5.76 us
    pallas_call x1, Pallas kernels, project(): pl.pallas_call(functools.partial(project_kernel, groups, ordered), in_spe...  5.44 us
    ppermute x10, waiting for transfers between devices, to_peer(): lax.ppermute(array, MEMBERS, [(i, i ^ distance) for i in range(members)])  4.65 us
    pallas_call x1, Pallas kernels, store(): pl.pallas_call(functools.partial(store_kernel, groups), in_specs=[pl.Bloc...  1.39 us
    pallas_call x1, Pallas kernels, attend(): pl.pallas_call(functools.partial(attend_kernel, groups, steps), in_specs=...  0.9 us
    pallas_call x1, Pallas kernels, gather(): pl.pallas_call(gather_kernel, in_specs=[pl.BlockSpec(memory_space=pltpu.V...  0.69 us
  transfers between devices with their start and end apart: 13, of which 5 were waited for; matrix products, arithmetic and copies ran while one was open for 0% of the time, Pallas kernels for 5%

profile of v4, /device:TPU:0, one launch (start us, length us, event | category | flops | bytes accessed | tf_op | source)
XLA Modules:
  0.0 28.9 jit_solution(8517968140976464807)
XLA Ops:
  0.6 5.4 %project.1 = (bf16[128,256]{1,0:T(8,128)(2,1)S(1)}, bf16[128,256]{1,0:T(8,128)(2,1)S(1)}, bf16[128,256]{1,0:T(8,128)(2,1)S(1)}, bf16[128,256]{1,0:T(8,128)(2,1)S...) custom-call(s32[4]{0:T(128)} %prompt_hbm.1, ...), custom_call_target="tpu_custom_call" | custom-call | tf_op jit(solution)/shard_map/project/pallas_call | solution.py:150
  6.1 5.1 %collective-permute-start.3 = (bf16[128,256]{1,0:T(8,128)(2,1)S(1)}, bf16[128,256]{1,0:T(8,128)(2,1)S(1)}, u32[]{:S(2)}, u32[]{:S(2)}) collective-permute-start(bf16[128,256]{1,0:T(8,128)(2,1)S(1)} %get-tuple-element.26), channel_id=1, source_target_pairs={{0,24},{8,16},{16,8},{24,0},{1,25},{9,17},{17,9},{25,1},{2,26},{10... | collective-permute-start | bytes 196616 | tf_op jit(solution)/shard_map/ppermute | solution.py:362
  11.2 0.0 collective-permute-start.4
  11.2 0.6 %collective-permute-start.5 = (bf16[128,256]{1,0:T(8,128)(2,1)S(1)}, bf16[128,256]{1,0:T(8,128)(2,1)S(1)}, u32[]{:S(2)}, u32[]{:S(2)}) collective-permute-start(bf16[128,256]{1,0:T(8,128)(2,1)S(1)} %get-tuple-element.28), channel_id=1, source_target_pairs={{0,8},{8,0},{16,24},{24,16},{1,9},{9,1},{17,25},{25,17},{2,10},{10... | collective-permute-start | bytes 196616 | tf_op jit(solution)/shard_map/ppermute | solution.py:362
  11.8 2.6 %collective-permute-start = (bf16[2,40,128]{2,1,0:T(8,128)(2,1)S(1)}, bf16[2,40,128]{2,1,0:T(8,128)(2,1)S(1)}, u32[]{:S(2)}, u32[]{:S(2)}) collective-permute-start(bf16[2,40,128]{2,1,0:T(8,128)(2,1)S(1)} %get-tuple-element.19), channel_id=1, source_target_pairs={{0,5},{1,4},{2,7},{3,6},{4,1},{5,0},{6,3},{7,2},{8,13},{9,12},{10,... | collective-permute-start | bytes 61448 | tf_op jit(solution)/shard_map/ppermute | solution.py:368
  14.4 0.5 %collective-permute-start.1 = (bf16[2,40,128]{2,1,0:T(8,128)(2,1)S(1)}, bf16[2,40,128]{2,1,0:T(8,128)(2,1)S(1)}, u32[]{:S(2)}, u32[]{:S(2)}) collective-permute-start(bf16[2,40,128]{2,1,0:T(8,128)(2,1)S(1)} %get-tuple-element.20), channel_id=1, source_target_pairs={{0,4},{1,5},{2,6},{3,7},{4,0},{5,1},{6,2},{7,3},{8,12},{9,13},{10,... | collective-permute-start | bytes 61448 | tf_op jit(solution)/shard_map/ppermute | solution.py:368
  14.9 1.6 %collective-permute-done.refs_0_ = bf16[2,40,128]{2,1,0:T(8,128)(2,1)S(1)} collective-permute-done((bf16[2,40,128]{2,1,0:T(8,128)(2,1)S(1)}, bf16[2,40,128]{2,1,0:T(8,128)(2,1)S(1)}, u32[]{:S(2)}, u32[]{:S(2)}) %collective-permute-start) | collective-permute-done | bytes 20512 | tf_op jit(solution)/shard_map/ppermute | solution.py:368
  16.5 1.6 %collective-permute-start.2 = (bf16[2,40,128]{2,1,0:T(8,128)(2,1)S(1)}, bf16[2,40,128]{2,1,0:T(8,128)(2,1)S(1)}, u32[]{:S(2)}, u32[]{:S(2)}) collective-permute-start(bf16[2,40,128]{2,1,0:T(8,128)(2,1)S(1)} %get-tuple-element.21), channel_id=1, source_target_pairs={{0,1},{1,0},{2,3},{3,2},{4,5},{5,4},{6,7},{7,6},{8,9},{9,8},{10,11... | collective-permute-start | bytes 61448 | tf_op jit(solution)/shard_map/ppermute | solution.py:368
  18.2 0.1 collective-permute-done.1.refs_1_
  18.2 0.0 collective-permute-start.9
  18.2 0.0 collective-permute-done.3.rest_3_
  18.2 0.5 %collective-permute-start.6 = (bf16[128,256]{1,0:T(8,128)(2,1)S(1)}, bf16[128,256]{1,0:T(8,128)(2,1)S(1)}, u32[]{:S(2)}, u32[]{:S(2)}) collective-permute-start(bf16[128,256]{1,0:T(8,128)(2,1)S(1)} %collective-permute-done.3.rest_3_), channel_id=1, source_target_pairs={{0,2},{1,3},{2,0},{3,1},{4,6},{5,7},{6,4},{7,5},{8,10},{9,11},{10,... | collective-permute-start | bytes 196616 | tf_op jit(solution)/shard_map/ppermute | solution.py:368
  18.7 0.0 collective-permute-done.4.rest_4_
  18.7 0.1 collective-permute-start.7
  18.8 0.0 collective-permute-done.5.rest_5_
  18.8 0.4 %collective-permute-start.8 = (bf16[128,256]{1,0:T(8,128)(2,1)S(1)}, bf16[128,256]{1,0:T(8,128)(2,1)S(1)}, u32[]{:S(2)}, u32[]{:S(2)}) collective-permute-start(bf16[128,256]{1,0:T(8,128)(2,1)S(1)} %collective-permute-done.5.rest_5_), channel_id=1, source_target_pairs={{0,2},{1,3},{2,0},{3,1},{4,6},{5,7},{6,4},{7,5},{8,10},{9,11},{10,... | collective-permute-start | bytes 196616 | tf_op jit(solution)/shard_map/ppermute | solution.py:368
  19.2 1.1 %collective-permute-done.2.refs_2_ = bf16[2,40,128]{2,1,0:T(8,128)(2,1)S(1)} collective-permute-done((bf16[2,40,128]{2,1,0:T(8,128)(2,1)S(1)}, bf16[2,40,128]{2,1,0:T(8,128)(2,1)S(1)}, u32[]{:S(2)}, u32[]{:S(2)}) %collective-permute-start.2) | collective-permute-done | bytes 20512 | tf_op jit(solution)/shard_map/ppermute | solution.py:368
  20.3 0.0 copy-start
  20.3 0.0 collective-permute-done.9.rest_10_
  20.3 0.0 collective-permute-done.6.rest_7_
  20.3 0.0 collective-permute-done.7.rest_8_
  20.4 0.0 collective-permute-done.8.rest_9_
  20.4 0.9 %attend.1 = (bf16[2,32,128]{2,1,0:T(8,128)(2,1)S(1)}, bf16[2,32,128]{2,1,0:T(8,128)(2,1)S(1)}, bf16[2,32,128]{2,1,0:T(8,128)(2,1)S(1)}, bf16[2,32,128]{2,1,0:T(8,128)(2,1)S(1)}) custom-call(f32[128,128]{1,0:T(8,128)S(1)} %get-tuple-element.18.alive_ref, bf16[2,128,128]{2,1,0:T(8,128)(2,1)S(1)} %get-tuple-element.23.rest_0_, ...), custom_call_target="tpu_custom_call" | custom-call | tf_op jit(solution)/shard_map/attend/pallas_call | solution.py:289
  21.3 2.7 %collective-permute-start.10 = (bf16[2,32,128]{2,1,0:T(8,128)(2,1)S(1)}, bf16[2,32,128]{2,1,0:T(8,128)(2,1)S(1)}, u32[]{:S(2)}, u32[]{:S(2)}) collective-permute-start(bf16[2,32,128]{2,1,0:T(8,128)(2,1)S(1)} %get-tuple-element.30), channel_id=1, source_target_pairs={{0,5},{1,4},{2,7},{3,6},{4,1},{5,0},{6,3},{7,2},{8,13},{9,12},{10,... | collective-permute-start | bytes 49160 | tf_op jit(solution)/shard_map/ppermute | solution.py:368
  23.9 0.5 %collective-permute-start.11 = (bf16[2,32,128]{2,1,0:T(8,128)(2,1)S(1)}, bf16[2,32,128]{2,1,0:T(8,128)(2,1)S(1)}, u32[]{:S(2)}, u32[]{:S(2)}) collective-permute-start(bf16[2,32,128]{2,1,0:T(8,128)(2,1)S(1)} %get-tuple-element.31), channel_id=1, source_target_pairs={{0,4},{1,5},{2,6},{3,7},{4,0},{5,1},{6,2},{7,3},{8,12},{9,13},{10,... | collective-permute-start | bytes 49160 | tf_op jit(solution)/shard_map/ppermute | solution.py:368
  24.4 0.4 %collective-permute-start.12 = (bf16[2,32,128]{2,1,0:T(8,128)(2,1)S(1)}, bf16[2,32,128]{2,1,0:T(8,128)(2,1)S(1)}, u32[]{:S(2)}, u32[]{:S(2)}) collective-permute-start(bf16[2,32,128]{2,1,0:T(8,128)(2,1)S(1)} %get-tuple-element.32), channel_id=1, source_target_pairs={{0,1},{1,0},{2,3},{3,2},{4,5},{5,4},{6,7},{7,6},{8,9},{9,8},{10,11... | collective-permute-start | bytes 49160 | tf_op jit(solution)/shard_map/ppermute | solution.py:368
  24.8 0.0 copy-done
  24.8 1.4 %store.1 = bf16[64,8,256]{2,1,0:T(8,128)(2,1)} custom-call(s32[1,64]{1,0:T(1,128)S(1)} %copy-done, bf16[16,8,256]{2,1,0:T(8,128)(2,1)S(1)} %bitcast.22, bf16[16,8,256]{2,1,0:T(8,128)(2,1)S(1)} %bitcast.23, bf16[16,8,256]{2,1,0:T(8,128)(2,1)S(1)} %bitcast.24, bf16[16,8,256]{2,1,0:T(8,128)(2,1)S(1)} %bitcast.21), custom_call_target="tpu_custom_call" | custom-call | flops 20000000000 | tf_op jit(solution)/shard_map/store/pallas_call | solution.py:190
  26.2 0.0 collective-permute-done.10.refs_0_
  26.2 1.4 %collective-permute-done.11.refs_1_ = bf16[2,32,128]{2,1,0:T(8,128)(2,1)S(1)} collective-permute-done((bf16[2,32,128]{2,1,0:T(8,128)(2,1)S(1)}, bf16[2,32,128]{2,1,0:T(8,128)(2,1)S(1)}, u32[]{:S(2)}, u32[]{:S(2)}) %collective-permute-start.11) | collective-permute-done | bytes 16416 | tf_op jit(solution)/shard_map/ppermute | solution.py:368
  27.7 0.5 %collective-permute-done.12.refs_2_ = bf16[2,32,128]{2,1,0:T(8,128)(2,1)S(1)} collective-permute-done((bf16[2,32,128]{2,1,0:T(8,128)(2,1)S(1)}, bf16[2,32,128]{2,1,0:T(8,128)(2,1)S(1)}, u32[]{:S(2)}, u32[]{:S(2)}) %collective-permute-start.12) | collective-permute-done | bytes 16416 | tf_op jit(solution)/shard_map/ppermute | solution.py:368
  28.2 0.7 %gather.1 = bf16[8,32,128]{2,1,0:T(8,128)(2,1)} custom-call(bf16[2,32,128]{2,1,0:T(8,128)(2,1)S(1)} %collective-permute-done.10.refs_0_, bf16[2,32,128]{2,1,0:T(8,128)(2,1)S(1)} %collective-permute-done.11.refs_1_, bf16[2,32,128]{2,1,0:T(8,128)(2,1)S(1)} %collective-permute-done.12.refs_2_, bf16[2,32,128]{2,1,0:T(8,128)(2,1)S(1)} %get-tuple-element.33.refs_3_), custom_call_target="tpu_custom_call" | custom-call | tf_op jit(solution)/shard_map/gather/pallas_call | solution.py:317
  (1 shorter events, 0.0 us)
Async XLA Ops:
  6.1 12.1 %collective-permute-start.3 = (bf16[128,256]{1,0:T(8,128)(2,1)S(1)}, bf16[128,256]{1,0:T(8,128)(2,1)S(1)}, u32[]{:S(2)}, u32[]{:S(2)}) collective-permute-start(bf16[128,256]{1,0:T(8,128)(2,1)S(1)} %get-tuple-element.26), channel_id=1, source_target_pairs={{0,24},{8,16},{16,8},{24,0},{1,25},{9,17},{17,9},{25,1},{2,26},{10... | collective-permute-start | bytes 196616 | tf_op jit(solution)/shard_map/ppermute | solution.py:362
  11.2 7.5 %collective-permute-start.4 = (bf16[128,256]{1,0:T(8,128)(2,1)S(1)}, bf16[128,256]{1,0:T(8,128)(2,1)S(1)}, u32[]{:S(2)}, u32[]{:S(2)}) collective-permute-start(bf16[128,256]{1,0:T(8,128)(2,1)S(1)} %get-tuple-element.27), channel_id=1, source_target_pairs={{0,16},{8,24},{16,0},{24,8},{1,17},{9,25},{17,1},{25,9},{2,18},{10... | collective-permute-start | bytes 196616 | tf_op jit(solution)/shard_map/ppermute | solution.py:362
  11.2 7.6 %collective-permute-start.5 = (bf16[128,256]{1,0:T(8,128)(2,1)S(1)}, bf16[128,256]{1,0:T(8,128)(2,1)S(1)}, u32[]{:S(2)}, u32[]{:S(2)}) collective-permute-start(bf16[128,256]{1,0:T(8,128)(2,1)S(1)} %get-tuple-element.28), channel_id=1, source_target_pairs={{0,8},{8,0},{16,24},{24,16},{1,9},{9,1},{17,25},{25,17},{2,10},{10... | collective-permute-start | bytes 196616 | tf_op jit(solution)/shard_map/ppermute | solution.py:362
  11.8 4.7 %collective-permute-start = (bf16[2,40,128]{2,1,0:T(8,128)(2,1)S(1)}, bf16[2,40,128]{2,1,0:T(8,128)(2,1)S(1)}, u32[]{:S(2)}, u32[]{:S(2)}) collective-permute-start(bf16[2,40,128]{2,1,0:T(8,128)(2,1)S(1)} %get-tuple-element.19), channel_id=1, source_target_pairs={{0,5},{1,4},{2,7},{3,6},{4,1},{5,0},{6,3},{7,2},{8,13},{9,12},{10,... | collective-permute-start | bytes 61448 | tf_op jit(solution)/shard_map/ppermute | solution.py:368
  14.4 3.8 %collective-permute-start.1 = (bf16[2,40,128]{2,1,0:T(8,128)(2,1)S(1)}, bf16[2,40,128]{2,1,0:T(8,128)(2,1)S(1)}, u32[]{:S(2)}, u32[]{:S(2)}) collective-permute-start(bf16[2,40,128]{2,1,0:T(8,128)(2,1)S(1)} %get-tuple-element.20), channel_id=1, source_target_pairs={{0,4},{1,5},{2,6},{3,7},{4,0},{5,1},{6,2},{7,3},{8,12},{9,13},{10,... | collective-permute-start | bytes 61448 | tf_op jit(solution)/shard_map/ppermute | solution.py:368
  16.5 3.8 %collective-permute-start.2 = (bf16[2,40,128]{2,1,0:T(8,128)(2,1)S(1)}, bf16[2,40,128]{2,1,0:T(8,128)(2,1)S(1)}, u32[]{:S(2)}, u32[]{:S(2)}) collective-permute-start(bf16[2,40,128]{2,1,0:T(8,128)(2,1)S(1)} %get-tuple-element.21), channel_id=1, source_target_pairs={{0,1},{1,0},{2,3},{3,2},{4,5},{5,4},{6,7},{7,6},{8,9},{9,8},{10,11... | collective-permute-start | bytes 61448 | tf_op jit(solution)/shard_map/ppermute | solution.py:368
  18.2 2.1 %collective-permute-start.9 = (bf16[128,256]{1,0:T(8,128)(2,1)S(1)}, bf16[128,256]{1,0:T(8,128)(2,1)S(1)}, u32[]{:S(2)}, u32[]{:S(2)}) collective-permute-start(bf16[128,256]{1,0:T(8,128)(2,1)S(1)} %get-tuple-element.29.rest_6_), channel_id=1, source_target_pairs={{0,2},{1,3},{2,0},{3,1},{4,6},{5,7},{6,4},{7,5},{8,10},{9,11},{10,... | collective-permute-start | bytes 196616 | tf_op jit(solution)/shard_map/ppermute | solution.py:368
  18.2 2.1 %collective-permute-start.6 = (bf16[128,256]{1,0:T(8,128)(2,1)S(1)}, bf16[128,256]{1,0:T(8,128)(2,1)S(1)}, u32[]{:S(2)}, u32[]{:S(2)}) collective-permute-start(bf16[128,256]{1,0:T(8,128)(2,1)S(1)} %collective-permute-done.3.rest_3_), channel_id=1, source_target_pairs={{0,2},{1,3},{2,0},{3,1},{4,6},{5,7},{6,4},{7,5},{8,10},{9,11},{10,... | collective-permute-start | bytes 196616 | tf_op jit(solution)/shard_map/ppermute | solution.py:368
  18.7 1.6 %collective-permute-start.7 = (bf16[128,256]{1,0:T(8,128)(2,1)S(1)}, bf16[128,256]{1,0:T(8,128)(2,1)S(1)}, u32[]{:S(2)}, u32[]{:S(2)}) collective-permute-start(bf16[128,256]{1,0:T(8,128)(2,1)S(1)} %collective-permute-done.4.rest_4_), channel_id=1, source_target_pairs={{0,2},{1,3},{2,0},{3,1},{4,6},{5,7},{6,4},{7,5},{8,10},{9,11},{10,... | collective-permute-start | bytes 196616 | tf_op jit(solution)/shard_map/ppermute | solution.py:368
  18.8 1.6 %collective-permute-start.8 = (bf16[128,256]{1,0:T(8,128)(2,1)S(1)}, bf16[128,256]{1,0:T(8,128)(2,1)S(1)}, u32[]{:S(2)}, u32[]{:S(2)}) collective-permute-start(bf16[128,256]{1,0:T(8,128)(2,1)S(1)} %collective-permute-done.5.rest_5_), channel_id=1, source_target_pairs={{0,2},{1,3},{2,0},{3,1},{4,6},{5,7},{6,4},{7,5},{8,10},{9,11},{10,... | collective-permute-start | bytes 196616 | tf_op jit(solution)/shard_map/ppermute | solution.py:368
  20.3 4.5 %copy-start = (s32[1,64]{1,0:T(1,128)S(1)}, s32[1,64]{1,0:T(1,128)}, u32[]{:S(2)}) copy-start(s32[1,64]{1,0:T(1,128)} %table_ref.1) | copy-start | bytes 772
  21.3 5.0 %collective-permute-start.10 = (bf16[2,32,128]{2,1,0:T(8,128)(2,1)S(1)}, bf16[2,32,128]{2,1,0:T(8,128)(2,1)S(1)}, u32[]{:S(2)}, u32[]{:S(2)}) collective-permute-start(bf16[2,32,128]{2,1,0:T(8,128)(2,1)S(1)} %get-tuple-element.30), channel_id=1, source_target_pairs={{0,5},{1,4},{2,7},{3,6},{4,1},{5,0},{6,3},{7,2},{8,13},{9,12},{10,... | collective-permute-start | bytes 49160 | tf_op jit(solution)/shard_map/ppermute | solution.py:368
  23.9 3.7 %collective-permute-start.11 = (bf16[2,32,128]{2,1,0:T(8,128)(2,1)S(1)}, bf16[2,32,128]{2,1,0:T(8,128)(2,1)S(1)}, u32[]{:S(2)}, u32[]{:S(2)}) collective-permute-start(bf16[2,32,128]{2,1,0:T(8,128)(2,1)S(1)} %get-tuple-element.31), channel_id=1, source_target_pairs={{0,4},{1,5},{2,6},{3,7},{4,0},{5,1},{6,2},{7,3},{8,12},{9,13},{10,... | collective-permute-start | bytes 49160 | tf_op jit(solution)/shard_map/ppermute | solution.py:368
  24.4 3.7 %collective-permute-start.12 = (bf16[2,32,128]{2,1,0:T(8,128)(2,1)S(1)}, bf16[2,32,128]{2,1,0:T(8,128)(2,1)S(1)}, u32[]{:S(2)}, u32[]{:S(2)}) collective-permute-start(bf16[2,32,128]{2,1,0:T(8,128)(2,1)S(1)} %get-tuple-element.32), channel_id=1, source_target_pairs={{0,1},{1,0},{2,3},{3,2},{4,5},{5,4},{6,7},{7,6},{8,9},{9,8},{10,11... | collective-permute-start | bytes 49160 | tf_op jit(solution)/shard_map/ppermute | solution.py:368

commit v5 on v4

--- a/solution.py
+++ b/solution.py
@@ -33,6 +33,8 @@
 
 SIBLING = 2
 PEERS = (5, 4, 1)
+NEAR, FAR = 1, 4
+PACKETS = ((NEAR, NEAR ^ FAR), (FAR,), (0,))
 
 
 def in_hbm(array):
@@ -52,8 +54,7 @@
     *rest,
 ):
     prompts = x_hbm.shape[0]
-    packets = len(PEERS) + 1
-    outs, packed, rest = rest[:prompts], rest[prompts : prompts + packets], rest[prompts + packets :]
+    outs, packed, rest = rest[:prompts], rest[prompts : prompts + 3], rest[prompts + 3 :]
     alive_ref, prompt_ref, count_ref, b_ref, query_ref, recent_ref, x_ref, w_ref, total_ref = rest[:9]
     small_sem, x_sem, w_sem = rest[9:]
     chunks, prompts, rows, depth = x_ref.shape
@@ -112,11 +113,12 @@
         copy.wait()
     q_rows = query_ref.shape[1]
     member = lax.axis_index(MEMBERS)
-    for distance, packet in zip(PEERS + (0,), packed):
-        for at in range(2):
-            head = member ^ distance ^ (SIBLING * at)
-            packet[at, :q_rows, :] = query_ref[head]
-            packet[at, q_rows:, :] = recent_ref[head]
+    for distances, packet in zip(PACKETS, packed):
+        for to, distance in enumerate(distances):
+            for at in range(2):
+                head = member ^ distance ^ (SIBLING * at)
+                packet[to, at, :q_rows, :] = query_ref[head]
+                packet[to, at, q_rows:, :] = recent_ref[head]
     own_prompt = prompt_ref[me]
     earlier = jnp.int32(0)
     for g in range(groups):
@@ -142,9 +144,9 @@
     prompts, rows, depth = prompt_hidden.shape
     width = kv_weight.shape[1]
     chunks = depth // CHUNK
-    packet = pltpu.VMEM((2, query.shape[1] + recent.shape[1], HEAD_DIM), query.dtype)
-    packets = [packet] * (len(PEERS) + 1)
-    alive = pltpu.VMEM((len(packets) * query.shape[1], HEAD_DIM), jnp.float32)
+    packet_shape = (2, query.shape[1] + recent.shape[1], HEAD_DIM)
+    packets = [pltpu.VMEM((len(to),) + packet_shape, query.dtype) for to in PACKETS]
+    alive = pltpu.VMEM(((len(PEERS) + 1) * query.shape[1], HEAD_DIM), jnp.float32)
     bias = kv_bias.reshape(1, width)
     operands = (decode_prompt, sample_counts, prompt_hidden, kv_weight, bias, query, recent)
     return pl.pallas_call(
@@ -200,8 +202,25 @@
     )(page_table, *blocks)
 
 
-def arrange_kernel(steps, *refs):
-    packets, (query_ref, key_ref, value_ref) = refs[:-3], refs[-3:]
+def join_kernel(first_ref, second_ref, out_ref):
+    out_ref[0] = first_ref[0]
+    out_ref[1] = second_ref[1]
+
+
+def join(first, second):
+    vmem = pl.BlockSpec(memory_space=pltpu.VMEM)
+    return pl.pallas_call(
+        join_kernel,
+        in_specs=[vmem] * 2,
+        out_specs=vmem,
+        out_shape=pltpu.VMEM(second.shape, second.dtype),
+        compiler_params=pltpu.CompilerParams(vmem_limit_bytes=PACK_VMEM),
+        name="join",
+    )(first, second)
+
+
+def arrange_kernel(steps, far_ref, near_ref, own_ref, query_ref, key_ref, value_ref):
+    packets = (far_ref.at[1], far_ref.at[0], near_ref.at[0], own_ref.at[0])
     q_rows = Q_PER_KV * steps
     for at in range(2):
         recent = jnp.concatenate(
@@ -215,12 +234,12 @@
 
 
 def arrange(steps, packets):
-    samples, dtype = len(packets), packets[0].dtype
+    samples, dtype = len(PEERS) + 1, packets[0].dtype
     vmem = pl.BlockSpec(memory_space=pltpu.VMEM)
     recent = pltpu.VMEM((2, samples * 2 * steps, HEAD_DIM), dtype)
     return pl.pallas_call(
         functools.partial(arrange_kernel, steps),
-        in_specs=[vmem] * samples,
+        in_specs=[vmem] * 3,
         out_specs=[vmem] * 3,
         out_shape=[
             pltpu.VMEM((2, samples * Q_PER_KV * steps, HEAD_DIM), dtype),
@@ -367,7 +386,9 @@
     def to_peer(array, distance):
         return lax.ppermute(array, MEMBERS, [(i, i ^ distance) for i in range(members)])
 
-    packets = [to_peer(packet, at) for packet, at in zip(packets, PEERS)] + [packets[-1]]
+    near, far, mine = packets
+    near = to_peer(near, NEAR)
+    packets = [to_peer(join(far, near), FAR), near, mine]
     blocks = blocks + [own]
     sibling_blocks = [to_peer(block, SIBLING) for block in blocks]
     parts = attend(

time: 29 us -> 27 us (0.931)
  starting transfers between devices: 15.1 us -> 12.9 us
    ppermute x3, waiting for transfers between devices: 0.01 us -> 3.11 us  [local(): lax.ppermute(block, 'group', [(i, goes_to(i)) for i in range(groups)])]
    ppermute x10 -> x9, waiting for transfers between devices: 4.65 us -> 1.68 us  [to_peer(): lax.ppermute(array, MEMBERS, [(i, i ^ distance) for i in range(members)])]
    ppermute x3, starting transfers between devices: 5.76 us -> 4.39 us  [local(): lax.ppermute(block, 'group', [(i, goes_to(i)) for i in range(groups)])]
    ppermute x10 -> x9, starting transfers between devices: 9.31 us -> 8.54 us  [to_peer(): lax.ppermute(array, MEMBERS, [(i, i ^ distance) for i in range(members)])]
  transfers between devices with their start and end apart: 13 -> 12, of which waited for: 5 -> 7; matrix products, arithmetic and copies ran while one was open for 0% -> 0% of each run, Pallas kernels for 5% -> 5%
where the time goes in v5:
time: 27 us; the launch traced here: 26.8 us
  starting transfers between devices  12.9 us (48%)
  Pallas kernels  8.43 us (31%)
  waiting for transfers between devices  4.79 us (18%)
  between operations  0.7 us (3%)
    ppermute x9, starting transfers between devices, to_peer(): lax.ppermute(array, MEMBERS, [(i, i ^ distance) for i in range(members)])  8.54 us
    pallas_call x1, Pallas kernels, project(): pl.pallas_call(functools.partial(project_kernel, groups, ordered), in_spe...  5.44 us
    ppermute x3, starting transfers between devices, local(): lax.ppermute(block, 'group', [(i, goes_to(i)) for i in range(groups)])  4.39 us
    ppermute x3, waiting for transfers between devices, local(): lax.ppermute(block, 'group', [(i, goes_to(i)) for i in range(groups)])  3.11 us
    ppermute x9, waiting for transfers between devices, to_peer(): lax.ppermute(array, MEMBERS, [(i, i ^ distance) for i in range(members)])  1.68 us
    pallas_call x1, Pallas kernels, store(): pl.pallas_call(functools.partial(store_kernel, groups), in_specs=[pl.Bloc...  1.39 us
    pallas_call x1, Pallas kernels, attend(): pl.pallas_call(functools.partial(attend_kernel, groups, steps), in_specs=...  0.9 us
    pallas_call x1, Pallas kernels, gather(): pl.pallas_call(gather_kernel, in_specs=[pl.BlockSpec(memory_space=pltpu.V...  0.69 us
  transfers between devices with their start and end apart: 12, of which 7 were waited for; matrix products, arithmetic and copies ran while one was open for 0% of the time, Pallas kernels for 5%

profile of v5, /device:TPU:0, one launch (start us, length us, event | category | flops | bytes accessed | tf_op | source)
XLA Modules:
  0.0 26.8 jit_solution(12678434819873533481)
XLA Ops:
  0.6 5.4 %project.1 = (bf16[128,256]{1,0:T(8,128)(2,1)S(1)}, bf16[128,256]{1,0:T(8,128)(2,1)S(1)}, bf16[128,256]{1,0:T(8,128)(2,1)S(1)}, bf16[128,256]{1,0:T(8,128)(2,1)S...) custom-call(s32[4]{0:T(128)} %prompt_hbm.1, ...), custom_call_target="tpu_custom_call" | custom-call | tf_op jit(solution)/shard_map/project/pallas_call | solution.py:152
  6.1 3.0 %collective-permute-start = (bf16[2,2,40,128]{3,2,1,0:T(8,128)(2,1)S(1)}, bf16[2,2,40,128]{3,2,1,0:T(8,128)(2,1)S(1)}, u32[]{:S(2)}, u32[]{:S(2)}) collective-permute-start(bf16[2,2,40,128]{3,2,1,0:T(8,128)(2,1)S(1)} %get-tuple-element.19), channel_id=1, source_target_pairs={{0,1},{1,0},{2,3},{3,2},{4,5},{5,4},{6,7},{7,6},{8,9},{9,8},{10,11... | collective-permute-start | bytes 122888 | tf_op jit(solution)/shard_map/ppermute | solution.py:387
  9.1 3.6 %collective-permute-start.2 = (bf16[128,256]{1,0:T(8,128)(2,1)S(1)}, bf16[128,256]{1,0:T(8,128)(2,1)S(1)}, u32[]{:S(2)}, u32[]{:S(2)}) collective-permute-start(bf16[128,256]{1,0:T(8,128)(2,1)S(1)} %get-tuple-element.24), channel_id=1, source_target_pairs={{0,24},{8,16},{16,8},{24,0},{1,25},{9,17},{17,9},{25,1},{2,26},{10... | collective-permute-start | bytes 196616 | tf_op jit(solution)/shard_map/ppermute | solution.py:381
  12.7 0.0 collective-permute-start.3
  12.7 0.8 %collective-permute-start.4 = (bf16[128,256]{1,0:T(8,128)(2,1)S(1)}, bf16[128,256]{1,0:T(8,128)(2,1)S(1)}, u32[]{:S(2)}, u32[]{:S(2)}) collective-permute-start(bf16[128,256]{1,0:T(8,128)(2,1)S(1)} %get-tuple-element.26), channel_id=1, source_target_pairs={{0,8},{8,0},{16,24},{24,16},{1,9},{9,1},{17,25},{25,17},{2,10},{10... | collective-permute-start | bytes 196616 | tf_op jit(solution)/shard_map/ppermute | solution.py:381
  13.5 0.0 collective-permute-done.second_ref.near_ref
  13.5 1.5 %collective-permute-start.1 = (bf16[2,2,40,128]{3,2,1,0:T(8,128)(2,1)S(1)}, bf16[2,2,40,128]{3,2,1,0:T(8,128)(2,1)S(1)}, u32[]{:S(2)}, u32[]{:S(2)}) collective-permute-start(bf16[2,2,40,128]{3,2,1,0:T(8,128)(2,1)S(1)} %join.1), channel_id=1, source_target_pairs={{0,4},{1,5},{2,6},{3,7},{4,0},{5,1},{6,2},{7,3},{8,12},{9,13},{10,... | collective-permute-start | bytes 122888 | tf_op jit(solution)/shard_map/ppermute | solution.py:387
  15.0 0.0 collective-permute-start.8
  15.0 0.9 %collective-permute-done.2.rest_3_ = bf16[128,256]{1,0:T(8,128)(2,1)S(1)} collective-permute-done((bf16[128,256]{1,0:T(8,128)(2,1)S(1)}, bf16[128,256]{1,0:T(8,128)(2,1)S(1)}, u32[]{:S(2)}, u32[]{:S(2)}) %collective-permute-start.2) | collective-permute-done | bytes 65568 | tf_op jit(solution)/shard_map/ppermute | solution.py:381
  15.9 0.0 collective-permute-start.5
  15.9 2.1 %collective-permute-done.3.rest_4_ = bf16[128,256]{1,0:T(8,128)(2,1)S(1)} collective-permute-done((bf16[128,256]{1,0:T(8,128)(2,1)S(1)}, bf16[128,256]{1,0:T(8,128)(2,1)S(1)}, u32[]{:S(2)}, u32[]{:S(2)}) %collective-permute-start.3) | collective-permute-done | bytes 65568 | tf_op jit(solution)/shard_map/ppermute | solution.py:381
  18.1 0.0 collective-permute-start.6
  18.1 0.1 collective-permute-done.4.rest_5_
  18.1 0.5 %collective-permute-start.7 = (bf16[128,256]{1,0:T(8,128)(2,1)S(1)}, bf16[128,256]{1,0:T(8,128)(2,1)S(1)}, u32[]{:S(2)}, u32[]{:S(2)}) collective-permute-start(bf16[128,256]{1,0:T(8,128)(2,1)S(1)} %collective-permute-done.4.rest_5_), channel_id=1, source_target_pairs={{0,2},{1,3},{2,0},{3,1},{4,6},{5,7},{6,4},{7,5},{8,10},{9,11},{10,... | collective-permute-start | bytes 196616 | tf_op jit(solution)/shard_map/ppermute | solution.py:387
  18.6 0.0 collective-permute-done.1.far_ref
  18.6 0.0 copy-start
  18.6 0.0 collective-permute-done.8.rest_10_
  18.6 0.0 collective-permute-done.5.rest_7_
  18.6 0.7 %collective-permute-done.6.rest_8_ = bf16[128,256]{1,0:T(8,128)(2,1)S(1)} collective-permute-done((bf16[128,256]{1,0:T(8,128)(2,1)S(1)}, bf16[128,256]{1,0:T(8,128)(2,1)S(1)}, u32[]{:S(2)}, u32[]{:S(2)}) %collective-permute-start.6) | collective-permute-done | bytes 65568 | tf_op jit(solution)/shard_map/ppermute | solution.py:387
  19.3 0.2 collective-permute-done.7.rest_9_
  19.5 0.9 %attend.1 = (bf16[2,32,128]{2,1,0:T(8,128)(2,1)S(1)}, bf16[2,32,128]{2,1,0:T(8,128)(2,1)S(1)}, bf16[2,32,128]{2,1,0:T(8,128)(2,1)S(1)}, bf16[2,32,128]{2,1,0:T(8,128)(2,1)S(1)}) custom-call(f32[128,128]{1,0:T(8,128)S(1)} %get-tuple-element.17.alive_ref, bf16[2,128,128]{2,1,0:T(8,128)(2,1)S(1)} %get-tuple-element.21.rest_0_, ...), custom_call_target="tpu_custom_call" | custom-call | tf_op jit(solution)/shard_map/attend/pallas_call | solution.py:308
  20.4 1.6 %collective-permute-start.9 = (bf16[2,32,128]{2,1,0:T(8,128)(2,1)S(1)}, bf16[2,32,128]{2,1,0:T(8,128)(2,1)S(1)}, u32[]{:S(2)}, u32[]{:S(2)}) collective-permute-start(bf16[2,32,128]{2,1,0:T(8,128)(2,1)S(1)} %get-tuple-element.28), channel_id=1, source_target_pairs={{0,5},{1,4},{2,7},{3,6},{4,1},{5,0},{6,3},{7,2},{8,13},{9,12},{10,... | collective-permute-start | bytes 49160 | tf_op jit(solution)/shard_map/ppermute | solution.py:387
  21.9 0.5 %collective-permute-start.10 = (bf16[2,32,128]{2,1,0:T(8,128)(2,1)S(1)}, bf16[2,32,128]{2,1,0:T(8,128)(2,1)S(1)}, u32[]{:S(2)}, u32[]{:S(2)}) collective-permute-start(bf16[2,32,128]{2,1,0:T(8,128)(2,1)S(1)} %get-tuple-element.29), channel_id=1, source_target_pairs={{0,4},{1,5},{2,6},{3,7},{4,0},{5,1},{6,2},{7,3},{8,12},{9,13},{10,... | collective-permute-start | bytes 49160 | tf_op jit(solution)/shard_map/ppermute | solution.py:387
  22.4 1.5 %collective-permute-start.11 = (bf16[2,32,128]{2,1,0:T(8,128)(2,1)S(1)}, bf16[2,32,128]{2,1,0:T(8,128)(2,1)S(1)}, u32[]{:S(2)}, u32[]{:S(2)}) collective-permute-start(bf16[2,32,128]{2,1,0:T(8,128)(2,1)S(1)} %get-tuple-element.30), channel_id=1, source_target_pairs={{0,1},{1,0},{2,3},{3,2},{4,5},{5,4},{6,7},{7,6},{8,9},{9,8},{10,11... | collective-permute-start | bytes 49160 | tf_op jit(solution)/shard_map/ppermute | solution.py:387
  23.9 0.0 copy-done
  23.9 1.4 %store.1 = bf16[64,8,256]{2,1,0:T(8,128)(2,1)} custom-call(s32[1,64]{1,0:T(1,128)S(1)} %copy-done, bf16[16,8,256]{2,1,0:T(8,128)(2,1)S(1)} %bitcast.22, bf16[16,8,256]{2,1,0:T(8,128)(2,1)S(1)} %bitcast.23, bf16[16,8,256]{2,1,0:T(8,128)(2,1)S(1)} %bitcast.24, bf16[16,8,256]{2,1,0:T(8,128)(2,1)S(1)} %bitcast.21), custom_call_target="tpu_custom_call" | custom-call | flops 20000000000 | tf_op jit(solution)/shard_map/store/pallas_call | solution.py:192
  25.3 0.0 collective-permute-done.9.refs_0_
  25.3 0.3 %collective-permute-done.10.refs_1_ = bf16[2,32,128]{2,1,0:T(8,128)(2,1)S(1)} collective-permute-done((bf16[2,32,128]{2,1,0:T(8,128)(2,1)S(1)}, bf16[2,32,128]{2,1,0:T(8,128)(2,1)S(1)}, u32[]{:S(2)}, u32[]{:S(2)}) %collective-permute-start.10) | collective-permute-done | bytes 16416 | tf_op jit(solution)/shard_map/ppermute | solution.py:387
  25.7 0.5 %collective-permute-done.11.refs_2_ = bf16[2,32,128]{2,1,0:T(8,128)(2,1)S(1)} collective-permute-done((bf16[2,32,128]{2,1,0:T(8,128)(2,1)S(1)}, bf16[2,32,128]{2,1,0:T(8,128)(2,1)S(1)}, u32[]{:S(2)}, u32[]{:S(2)}) %collective-permute-start.11) | collective-permute-done | bytes 16416 | tf_op jit(solution)/shard_map/ppermute | solution.py:387
  26.1 0.7 %gather.1 = bf16[8,32,128]{2,1,0:T(8,128)(2,1)} custom-call(bf16[2,32,128]{2,1,0:T(8,128)(2,1)S(1)} %collective-permute-done.9.refs_0_, bf16[2,32,128]{2,1,0:T(8,128)(2,1)S(1)} %collective-permute-done.10.refs_1_, bf16[2,32,128]{2,1,0:T(8,128)(2,1)S(1)} %collective-permute-done.11.refs_2_, bf16[2,32,128]{2,1,0:T(8,128)(2,1)S(1)} %get-tuple-element.31.refs_3_), custom_call_target="tpu_custom_call" | custom-call | tf_op jit(solution)/shard_map/gather/pallas_call | solution.py:336
  (2 shorter events, 0.0 us)
Async XLA Ops:
  6.1 7.4 %collective-permute-start = (bf16[2,2,40,128]{3,2,1,0:T(8,128)(2,1)S(1)}, bf16[2,2,40,128]{3,2,1,0:T(8,128)(2,1)S(1)}, u32[]{:S(2)}, u32[]{:S(2)}) collective-permute-start(bf16[2,2,40,128]{3,2,1,0:T(8,128)(2,1)S(1)} %get-tuple-element.19), channel_id=1, source_target_pairs={{0,1},{1,0},{2,3},{3,2},{4,5},{5,4},{6,7},{7,6},{8,9},{9,8},{10,11... | collective-permute-start | bytes 122888 | tf_op jit(solution)/shard_map/ppermute | solution.py:387
  9.1 6.9 %collective-permute-start.2 = (bf16[128,256]{1,0:T(8,128)(2,1)S(1)}, bf16[128,256]{1,0:T(8,128)(2,1)S(1)}, u32[]{:S(2)}, u32[]{:S(2)}) collective-permute-start(bf16[128,256]{1,0:T(8,128)(2,1)S(1)} %get-tuple-element.24), channel_id=1, source_target_pairs={{0,24},{8,16},{16,8},{24,0},{1,25},{9,17},{17,9},{25,1},{2,26},{10... | collective-permute-start | bytes 196616 | tf_op jit(solution)/shard_map/ppermute | solution.py:381
  12.7 5.4 %collective-permute-start.3 = (bf16[128,256]{1,0:T(8,128)(2,1)S(1)}, bf16[128,256]{1,0:T(8,128)(2,1)S(1)}, u32[]{:S(2)}, u32[]{:S(2)}) collective-permute-start(bf16[128,256]{1,0:T(8,128)(2,1)S(1)} %get-tuple-element.25), channel_id=1, source_target_pairs={{0,16},{8,24},{16,0},{24,8},{1,17},{9,25},{17,1},{25,9},{2,18},{10... | collective-permute-start | bytes 196616 | tf_op jit(solution)/shard_map/ppermute | solution.py:381
  12.7 5.4 %collective-permute-start.4 = (bf16[128,256]{1,0:T(8,128)(2,1)S(1)}, bf16[128,256]{1,0:T(8,128)(2,1)S(1)}, u32[]{:S(2)}, u32[]{:S(2)}) collective-permute-start(bf16[128,256]{1,0:T(8,128)(2,1)S(1)} %get-tuple-element.26), channel_id=1, source_target_pairs={{0,8},{8,0},{16,24},{24,16},{1,9},{9,1},{17,25},{25,17},{2,10},{10... | collective-permute-start | bytes 196616 | tf_op jit(solution)/shard_map/ppermute | solution.py:381
  13.5 5.1 %collective-permute-start.1 = (bf16[2,2,40,128]{3,2,1,0:T(8,128)(2,1)S(1)}, bf16[2,2,40,128]{3,2,1,0:T(8,128)(2,1)S(1)}, u32[]{:S(2)}, u32[]{:S(2)}) collective-permute-start(bf16[2,2,40,128]{3,2,1,0:T(8,128)(2,1)S(1)} %join.1), channel_id=1, source_target_pairs={{0,4},{1,5},{2,6},{3,7},{4,0},{5,1},{6,2},{7,3},{8,12},{9,13},{10,... | collective-permute-start | bytes 122888 | tf_op jit(solution)/shard_map/ppermute | solution.py:387
  15.0 3.6 %collective-permute-start.8 = (bf16[128,256]{1,0:T(8,128)(2,1)S(1)}, bf16[128,256]{1,0:T(8,128)(2,1)S(1)}, u32[]{:S(2)}, u32[]{:S(2)}) collective-permute-start(bf16[128,256]{1,0:T(8,128)(2,1)S(1)} %get-tuple-element.27.rest_6_), channel_id=1, source_target_pairs={{0,2},{1,3},{2,0},{3,1},{4,6},{5,7},{6,4},{7,5},{8,10},{9,11},{10,... | collective-permute-start | bytes 196616 | tf_op jit(solution)/shard_map/ppermute | solution.py:387
  15.9 2.7 %collective-permute-start.5 = (bf16[128,256]{1,0:T(8,128)(2,1)S(1)}, bf16[128,256]{1,0:T(8,128)(2,1)S(1)}, u32[]{:S(2)}, u32[]{:S(2)}) collective-permute-start(bf16[128,256]{1,0:T(8,128)(2,1)S(1)} %collective-permute-done.2.rest_3_), channel_id=1, source_target_pairs={{0,2},{1,3},{2,0},{3,1},{4,6},{5,7},{6,4},{7,5},{8,10},{9,11},{10,... | collective-permute-start | bytes 196616 | tf_op jit(solution)/shard_map/ppermute | solution.py:387
  18.1 1.3 %collective-permute-start.6 = (bf16[128,256]{1,0:T(8,128)(2,1)S(1)}, bf16[128,256]{1,0:T(8,128)(2,1)S(1)}, u32[]{:S(2)}, u32[]{:S(2)}) collective-permute-start(bf16[128,256]{1,0:T(8,128)(2,1)S(1)} %collective-permute-done.3.rest_4_), channel_id=1, source_target_pairs={{0,2},{1,3},{2,0},{3,1},{4,6},{5,7},{6,4},{7,5},{8,10},{9,11},{10,... | collective-permute-start | bytes 196616 | tf_op jit(solution)/shard_map/ppermute | solution.py:387
  18.1 1.4 %collective-permute-start.7 = (bf16[128,256]{1,0:T(8,128)(2,1)S(1)}, bf16[128,256]{1,0:T(8,128)(2,1)S(1)}, u32[]{:S(2)}, u32[]{:S(2)}) collective-permute-start(bf16[128,256]{1,0:T(8,128)(2,1)S(1)} %collective-permute-done.4.rest_5_), channel_id=1, source_target_pairs={{0,2},{1,3},{2,0},{3,1},{4,6},{5,7},{6,4},{7,5},{8,10},{9,11},{10,... | collective-permute-start | bytes 196616 | tf_op jit(solution)/shard_map/ppermute | solution.py:387
  18.6 5.4 %copy-start = (s32[1,64]{1,0:T(1,128)S(1)}, s32[1,64]{1,0:T(1,128)}, u32[]{:S(2)}) copy-start(s32[1,64]{1,0:T(1,128)} %table_ref.1) | copy-start | bytes 772
  20.4 5.0 %collective-permute-start.9 = (bf16[2,32,128]{2,1,0:T(8,128)(2,1)S(1)}, bf16[2,32,128]{2,1,0:T(8,128)(2,1)S(1)}, u32[]{:S(2)}, u32[]{:S(2)}) collective-permute-start(bf16[2,32,128]{2,1,0:T(8,128)(2,1)S(1)} %get-tuple-element.28), channel_id=1, source_target_pairs={{0,5},{1,4},{2,7},{3,6},{4,1},{5,0},{6,3},{7,2},{8,13},{9,12},{10,... | collective-permute-start | bytes 49160 | tf_op jit(solution)/shard_map/ppermute | solution.py:387
  21.9 3.7 %collective-permute-start.10 = (bf16[2,32,128]{2,1,0:T(8,128)(2,1)S(1)}, bf16[2,32,128]{2,1,0:T(8,128)(2,1)S(1)}, u32[]{:S(2)}, u32[]{:S(2)}) collective-permute-start(bf16[2,32,128]{2,1,0:T(8,128)(2,1)S(1)} %get-tuple-element.29), channel_id=1, source_target_pairs={{0,4},{1,5},{2,6},{3,7},{4,0},{5,1},{6,2},{7,3},{8,12},{9,13},{10,... | collective-permute-start | bytes 49160 | tf_op jit(solution)/shard_map/ppermute | solution.py:387
  22.4 3.7 %collective-permute-start.11 = (bf16[2,32,128]{2,1,0:T(8,128)(2,1)S(1)}, bf16[2,32,128]{2,1,0:T(8,128)(2,1)S(1)}, u32[]{:S(2)}, u32[]{:S(2)}) collective-permute-start(bf16[2,32,128]{2,1,0:T(8,128)(2,1)S(1)} %get-tuple-element.30), channel_id=1, source_target_pairs={{0,1},{1,0},{2,3},{3,2},{4,5},{5,4},{6,7},{7,6},{8,9},{9,8},{10,11... | collective-permute-start | bytes 49160 | tf_op jit(solution)/shard_map/ppermute | solution.py:387

commit v6 on v5

--- a/solution.py
+++ b/solution.py
@@ -287,32 +287,58 @@
     return jnp.where(alive > 0.0, blended, 0.0)
 
 
-def attend_kernel(groups, steps, alive_ref, *rest):
-    arranged, rest = rest[:3], rest[3:]
-    head_blocks, outs = (rest[:groups], rest[groups : 2 * groups]), rest[2 * groups :]
+def attend_own_kernel(groups, steps, alive_ref, query_ref, key_ref, value_ref, *rest):
+    blocks, out_ref = rest[:groups], rest[groups]
+    out_ref[...] = attend_head(
+        steps,
+        alive_ref[...],
+        query_ref[0],
+        key_ref[0],
+        value_ref[0],
+        [block[...] for block in blocks],
+    ).astype(out_ref.dtype)
+
+
+def attend_own(groups, steps, alive, arranged, blocks):
+    vmem = pl.BlockSpec(memory_space=pltpu.VMEM)
+    return pl.pallas_call(
+        functools.partial(attend_own_kernel, groups, steps),
+        in_specs=[vmem] * (1 + len(arranged) + groups),
+        out_specs=vmem,
+        out_shape=pltpu.VMEM(arranged[0].shape[1:], jnp.bfloat16),
+        cost_estimate=pl.CostEstimate(flops=HIDE_FLOPS, transcendentals=0, bytes_accessed=0),
+        compiler_params=pltpu.CompilerParams(vmem_limit_bytes=VMEM_LIMIT),
+        name="attend_own",
+    )(alive, *arranged, *blocks)
+
+
+def attend_kernel(groups, steps, alive_ref, query_ref, key_ref, value_ref, own_ref, *rest):
+    blocks, outs = rest[:groups], rest[groups:]
     q_rows = Q_PER_KV * steps
-    for at, refs in enumerate(head_blocks):
-        blended = attend_head(
-            steps,
-            alive_ref[...],
-            *[ref[at] for ref in arranged],
-            [block[...] for block in refs],
-        ).astype(jnp.bfloat16)
-        for to, out in enumerate(outs):
-            out[at] = blended[to * q_rows : (to + 1) * q_rows]
-
-
-def attend(groups, steps, alive, arranged, own_blocks, sibling_blocks):
+    blended = attend_head(
+        steps,
+        alive_ref[...],
+        query_ref[1],
+        key_ref[1],
+        value_ref[1],
+        [block[...] for block in blocks],
+    ).astype(jnp.bfloat16)
+    for to, out in enumerate(outs):
+        out[0] = own_ref[to * q_rows : (to + 1) * q_rows]
+        out[1] = blended[to * q_rows : (to + 1) * q_rows]
+
+
+def attend(groups, steps, alive, arranged, own, blocks):
     packets = len(PEERS) + 1
     vmem = pl.BlockSpec(memory_space=pltpu.VMEM)
     return pl.pallas_call(
         functools.partial(attend_kernel, groups, steps),
-        in_specs=[vmem] * (1 + len(arranged) + 2 * groups),
+        in_specs=[vmem] * (2 + len(arranged) + groups),
         out_specs=[vmem] * packets,
         out_shape=[pltpu.VMEM((2, Q_PER_KV * steps, HEAD_DIM), jnp.bfloat16)] * packets,
         compiler_params=pltpu.CompilerParams(vmem_limit_bytes=VMEM_LIMIT),
         name="attend",
-    )(alive, *arranged, *own_blocks, *sibling_blocks)
+    )(alive, *arranged, own, *blocks)
 
 
 def gather_kernel(*refs):
@@ -390,10 +416,11 @@
     near = to_peer(near, NEAR)
     packets = [to_peer(join(far, near), FAR), near, mine]
     blocks = blocks + [own]
-    sibling_blocks = [to_peer(block, SIBLING) for block in blocks]
-    parts = attend(
-        groups, steps, alive, arrange(steps, packets), blocks, sibling_blocks
-    )
+    ready = [own] + blocks[:-3] + [blocks[-2], blocks[-3]]
+    sibling_blocks = [to_peer(block, SIBLING) for block in ready]
+    arranged = arrange(steps, packets)
+    own_head = attend_own(groups, steps, alive, arranged, ready)
+    parts = attend(groups, steps, alive, arranged, own_head, sibling_blocks)
     cache = store(
         groups,
         page_table,

time: 27 us -> 26.5 us (0.981)
  waiting for transfers between devices: 4.79 us -> 4.27 us
    pallas_call x0 -> x1, Pallas kernels: none -> 0.54 us  [attend_own(): pl.pallas_call(functools.partial(attend_own_kernel, groups, steps), in_sp...]
    pallas_call x1, Pallas kernels: 0.9 us -> 0.54 us  [attend(): pl.pallas_call(functools.partial(attend_kernel, groups, steps), in_specs=...]
    ppermute x3, waiting for transfers between devices: 3.11 us -> 2.78 us  [local(): lax.ppermute(block, 'group', [(i, goes_to(i)) for i in range(groups)])]
  transfers between devices with their start and end apart: 12 -> 12, of which waited for: 7 -> 6; matrix products, arithmetic and copies ran while one was open for 0% -> 0% of each run, Pallas kernels for 5% -> 7%
where the time goes in v6:
time: 26.5 us; the launch traced here: 26.3 us
  starting transfers between devices  12.7 us (48%)
  Pallas kernels  8.62 us (33%)
  waiting for transfers between devices  4.27 us (16%)
  between operations  0.72 us (3%)
    ppermute x9, starting transfers between devices, to_peer(): lax.ppermute(array, MEMBERS, [(i, i ^ distance) for i in range(members)])  8.34 us
    pallas_call x1, Pallas kernels, project(): pl.pallas_call(functools.partial(project_kernel, groups, ordered), in_spe...  5.44 us
    ppermute x3, starting transfers between devices, local(): lax.ppermute(block, 'group', [(i, goes_to(i)) for i in range(groups)])  4.39 us
    ppermute x3, waiting for transfers between devices, local(): lax.ppermute(block, 'group', [(i, goes_to(i)) for i in range(groups)])  2.78 us
    ppermute x9, waiting for transfers between devices, to_peer(): lax.ppermute(array, MEMBERS, [(i, i ^ distance) for i in range(members)])  1.49 us
    pallas_call x1, Pallas kernels, store(): pl.pallas_call(functools.partial(store_kernel, groups), in_specs=[pl.Bloc...  1.39 us
    pallas_call x1, Pallas kernels, gather(): pl.pallas_call(gather_kernel, in_specs=[pl.BlockSpec(memory_space=pltpu.V...  0.69 us
    pallas_call x1, Pallas kernels, attend_own(): pl.pallas_call(functools.partial(attend_own_kernel, groups, steps), in_sp...  0.54 us
  transfers between devices with their start and end apart: 12, of which 6 were waited for; matrix products, arithmetic and copies ran while one was open for 0% of the time, Pallas kernels for 7%

profile of v6, /device:TPU:0, one launch (start us, length us, event | category | flops | bytes accessed | tf_op | source)
XLA Modules:
  0.0 26.3 jit_solution(1155324260596203249)
XLA Ops:
  0.6 5.4 %project.1 = (bf16[128,256]{1,0:T(8,128)(2,1)S(1)}, bf16[128,256]{1,0:T(8,128)(2,1)S(1)}, bf16[128,256]{1,0:T(8,128)(2,1)S(1)}, bf16[128,256]{1,0:T(8,128)(2,1)S...) custom-call(s32[4]{0:T(128)} %prompt_hbm.1, ...), custom_call_target="tpu_custom_call" | custom-call | tf_op jit(solution)/shard_map/project/pallas_call | solution.py:152
  6.1 3.0 %collective-permute-start = (bf16[2,2,40,128]{3,2,1,0:T(8,128)(2,1)S(1)}, bf16[2,2,40,128]{3,2,1,0:T(8,128)(2,1)S(1)}, u32[]{:S(2)}, u32[]{:S(2)}) collective-permute-start(bf16[2,2,40,128]{3,2,1,0:T(8,128)(2,1)S(1)} %get-tuple-element.19), channel_id=1, source_target_pairs={{0,1},{1,0},{2,3},{3,2},{4,5},{5,4},{6,7},{7,6},{8,9},{9,8},{10,11... | collective-permute-start | bytes 122888 | tf_op jit(solution)/shard_map/ppermute | solution.py:413
  9.1 3.6 %collective-permute-start.2 = (bf16[128,256]{1,0:T(8,128)(2,1)S(1)}, bf16[128,256]{1,0:T(8,128)(2,1)S(1)}, u32[]{:S(2)}, u32[]{:S(2)}) collective-permute-start(bf16[128,256]{1,0:T(8,128)(2,1)S(1)} %get-tuple-element.25), channel_id=1, source_target_pairs={{0,24},{8,16},{16,8},{24,0},{1,25},{9,17},{17,9},{25,1},{2,26},{10... | collective-permute-start | bytes 196616 | tf_op jit(solution)/shard_map/ppermute | solution.py:407
  12.7 0.0 collective-permute-start.3
  12.7 0.8 %collective-permute-start.4 = (bf16[128,256]{1,0:T(8,128)(2,1)S(1)}, bf16[128,256]{1,0:T(8,128)(2,1)S(1)}, u32[]{:S(2)}, u32[]{:S(2)}) collective-permute-start(bf16[128,256]{1,0:T(8,128)(2,1)S(1)} %get-tuple-element.27), channel_id=1, source_target_pairs={{0,16},{8,24},{16,0},{24,8},{1,17},{9,25},{17,1},{25,9},{2,18},{10... | collective-permute-start | bytes 196616 | tf_op jit(solution)/shard_map/ppermute | solution.py:407
  13.5 0.0 collective-permute-done.second_ref.near_ref
  13.5 1.5 %collective-permute-start.1 = (bf16[2,2,40,128]{3,2,1,0:T(8,128)(2,1)S(1)}, bf16[2,2,40,128]{3,2,1,0:T(8,128)(2,1)S(1)}, u32[]{:S(2)}, u32[]{:S(2)}) collective-permute-start(bf16[2,2,40,128]{3,2,1,0:T(8,128)(2,1)S(1)} %join.1), channel_id=1, source_target_pairs={{0,4},{1,5},{2,6},{3,7},{4,0},{5,1},{6,2},{7,3},{8,12},{9,13},{10,... | collective-permute-start | bytes 122888 | tf_op jit(solution)/shard_map/ppermute | solution.py:413
  15.0 0.0 collective-permute-start.5
  15.0 0.3 collective-permute-done.2.rest_1_
  15.3 0.3 collective-permute-start.6
  15.5 1.8 %collective-permute-done.3.rest_2_ = bf16[128,256]{1,0:T(8,128)(2,1)S(1)} collective-permute-done((bf16[128,256]{1,0:T(8,128)(2,1)S(1)}, bf16[128,256]{1,0:T(8,128)(2,1)S(1)}, u32[]{:S(2)}, u32[]{:S(2)}) %collective-permute-start.3) | collective-permute-done | bytes 65568 | tf_op jit(solution)/shard_map/ppermute | solution.py:407
  17.3 0.0 collective-permute-start.7
  17.3 0.7 %collective-permute-done.4.rest_3_ = bf16[128,256]{1,0:T(8,128)(2,1)S(1)} collective-permute-done((bf16[128,256]{1,0:T(8,128)(2,1)S(1)}, bf16[128,256]{1,0:T(8,128)(2,1)S(1)}, u32[]{:S(2)}, u32[]{:S(2)}) %collective-permute-start.4) | collective-permute-done | bytes 65568 | tf_op jit(solution)/shard_map/ppermute | solution.py:407
  18.0 0.0 collective-permute-start.8
  18.0 0.0 collective-permute-done.1.far_ref
  18.1 0.0 copy-start
  18.1 0.5 %attend_own.1.own_ref = bf16[128,128]{1,0:T(8,128)(2,1)S(1)} custom-call(f32[128,128]{1,0:T(8,128)S(1)} %get-tuple-element.17.alive_ref, bf16[2,128,128]{2,1,0:T(8,128)(2,1)S(1)} %get-tuple-element.21.query_ref, bf16[2,32,128]{2,1,0:T(8,128)(2,1)S(1)} %get-tuple-element.22.key_ref, bf16[2,32,128]{2,1,0:T(8,128)(2,1)S(1)} %get-tuple-element.23.value_ref, ...), custom_call_target="tpu_custom_call" | custom-call | flops 20000000000 | tf_op jit(solution)/shard_map/attend_own/pallas_call | solution.py:304
  18.6 0.0 collective-permute-done.5.rest_0_
  18.6 0.0 collective-permute-done.6.rest_1_
  18.6 0.0 collective-permute-done.7.rest_2_
  18.7 0.6 %collective-permute-done.8.rest_3_ = bf16[128,256]{1,0:T(8,128)(2,1)S(1)} collective-permute-done((bf16[128,256]{1,0:T(8,128)(2,1)S(1)}, bf16[128,256]{1,0:T(8,128)(2,1)S(1)}, u32[]{:S(2)}, u32[]{:S(2)}) %collective-permute-start.8) | collective-permute-done | bytes 65568 | tf_op jit(solution)/shard_map/ppermute | solution.py:413
  19.3 0.5 %attend.1 = (bf16[2,32,128]{2,1,0:T(8,128)(2,1)S(1)}, bf16[2,32,128]{2,1,0:T(8,128)(2,1)S(1)}, bf16[2,32,128]{2,1,0:T(8,128)(2,1)S(1)}, bf16[2,32,128]{2,1,0:T(8,128)(2,1)S(1)}) custom-call(f32[128,128]{1,0:T(8,128)S(1)} %get-tuple-element.17.alive_ref, bf16[2,128,128]{2,1,0:T(8,128)(2,1)S(1)} %get-tuple-element.21.query_ref, ...), custom_call_target="tpu_custom_call" | custom-call | tf_op jit(solution)/shard_map/attend/pallas_call | solution.py:334
  19.8 1.6 %collective-permute-start.9 = (bf16[2,32,128]{2,1,0:T(8,128)(2,1)S(1)}, bf16[2,32,128]{2,1,0:T(8,128)(2,1)S(1)}, u32[]{:S(2)}, u32[]{:S(2)}) collective-permute-start(bf16[2,32,128]{2,1,0:T(8,128)(2,1)S(1)} %get-tuple-element.28), channel_id=1, source_target_pairs={{0,5},{1,4},{2,7},{3,6},{4,1},{5,0},{6,3},{7,2},{8,13},{9,12},{10,... | collective-permute-start | bytes 49160 | tf_op jit(solution)/shard_map/ppermute | solution.py:413
  21.4 0.5 %collective-permute-start.10 = (bf16[2,32,128]{2,1,0:T(8,128)(2,1)S(1)}, bf16[2,32,128]{2,1,0:T(8,128)(2,1)S(1)}, u32[]{:S(2)}, u32[]{:S(2)}) collective-permute-start(bf16[2,32,128]{2,1,0:T(8,128)(2,1)S(1)} %get-tuple-element.29), channel_id=1, source_target_pairs={{0,4},{1,5},{2,6},{3,7},{4,0},{5,1},{6,2},{7,3},{8,12},{9,13},{10,... | collective-permute-start | bytes 49160 | tf_op jit(solution)/shard_map/ppermute | solution.py:413
  21.9 1.5 %collective-permute-start.11 = (bf16[2,32,128]{2,1,0:T(8,128)(2,1)S(1)}, bf16[2,32,128]{2,1,0:T(8,128)(2,1)S(1)}, u32[]{:S(2)}, u32[]{:S(2)}) collective-permute-start(bf16[2,32,128]{2,1,0:T(8,128)(2,1)S(1)} %get-tuple-element.30), channel_id=1, source_target_pairs={{0,1},{1,0},{2,3},{3,2},{4,5},{5,4},{6,7},{7,6},{8,9},{9,8},{10,11... | collective-permute-start | bytes 49160 | tf_op jit(solution)/shard_map/ppermute | solution.py:413
  23.4 0.0 copy-done
  23.4 1.4 %store.1 = bf16[64,8,256]{2,1,0:T(8,128)(2,1)} custom-call(s32[1,64]{1,0:T(1,128)S(1)} %copy-done, bf16[16,8,256]{2,1,0:T(8,128)(2,1)S(1)} %bitcast.22, bf16[16,8,256]{2,1,0:T(8,128)(2,1)S(1)} %bitcast.24, bf16[16,8,256]{2,1,0:T(8,128)(2,1)S(1)} %bitcast.23, bf16[16,8,256]{2,1,0:T(8,128)(2,1)S(1)} %bitcast.21), custom_call_target="tpu_custom_call" | custom-call | flops 20000000000 | tf_op jit(solution)/shard_map/store/pallas_call | solution.py:192
  24.8 0.0 collective-permute-done.9.refs_0_
  24.8 0.3 %collective-permute-done.10.refs_1_ = bf16[2,32,128]{2,1,0:T(8,128)(2,1)S(1)} collective-permute-done((bf16[2,32,128]{2,1,0:T(8,128)(2,1)S(1)}, bf16[2,32,128]{2,1,0:T(8,128)(2,1)S(1)}, u32[]{:S(2)}, u32[]{:S(2)}) %collective-permute-start.10) | collective-permute-done | bytes 16416 | tf_op jit(solution)/shard_map/ppermute | solution.py:413
  25.1 0.5 %collective-permute-done.11.refs_2_ = bf16[2,32,128]{2,1,0:T(8,128)(2,1)S(1)} collective-permute-done((bf16[2,32,128]{2,1,0:T(8,128)(2,1)S(1)}, bf16[2,32,128]{2,1,0:T(8,128)(2,1)S(1)}, u32[]{:S(2)}, u32[]{:S(2)}) %collective-permute-start.11) | collective-permute-done | bytes 16416 | tf_op jit(solution)/shard_map/ppermute | solution.py:413
  25.6 0.7 %gather.1 = bf16[8,32,128]{2,1,0:T(8,128)(2,1)} custom-call(bf16[2,32,128]{2,1,0:T(8,128)(2,1)S(1)} %collective-permute-done.9.refs_0_, bf16[2,32,128]{2,1,0:T(8,128)(2,1)S(1)} %collective-permute-done.10.refs_1_, bf16[2,32,128]{2,1,0:T(8,128)(2,1)S(1)} %collective-permute-done.11.refs_2_, bf16[2,32,128]{2,1,0:T(8,128)(2,1)S(1)} %get-tuple-element.31.refs_3_), custom_call_target="tpu_custom_call" | custom-call | tf_op jit(solution)/shard_map/gather/pallas_call | solution.py:362
  (2 shorter events, 0.0 us)
Async XLA Ops:
  6.1 7.4 %collective-permute-start = (bf16[2,2,40,128]{3,2,1,0:T(8,128)(2,1)S(1)}, bf16[2,2,40,128]{3,2,1,0:T(8,128)(2,1)S(1)}, u32[]{:S(2)}, u32[]{:S(2)}) collective-permute-start(bf16[2,2,40,128]{3,2,1,0:T(8,128)(2,1)S(1)} %get-tuple-element.19), channel_id=1, source_target_pairs={{0,1},{1,0},{2,3},{3,2},{4,5},{5,4},{6,7},{7,6},{8,9},{9,8},{10,11... | collective-permute-start | bytes 122888 | tf_op jit(solution)/shard_map/ppermute | solution.py:413
  9.1 6.2 %collective-permute-start.2 = (bf16[128,256]{1,0:T(8,128)(2,1)S(1)}, bf16[128,256]{1,0:T(8,128)(2,1)S(1)}, u32[]{:S(2)}, u32[]{:S(2)}) collective-permute-start(bf16[128,256]{1,0:T(8,128)(2,1)S(1)} %get-tuple-element.25), channel_id=1, source_target_pairs={{0,24},{8,16},{16,8},{24,0},{1,25},{9,17},{17,9},{25,1},{2,26},{10... | collective-permute-start | bytes 196616 | tf_op jit(solution)/shard_map/ppermute | solution.py:407
  12.7 4.6 %collective-permute-start.3 = (bf16[128,256]{1,0:T(8,128)(2,1)S(1)}, bf16[128,256]{1,0:T(8,128)(2,1)S(1)}, u32[]{:S(2)}, u32[]{:S(2)}) collective-permute-start(bf16[128,256]{1,0:T(8,128)(2,1)S(1)} %get-tuple-element.26), channel_id=1, source_target_pairs={{0,8},{8,0},{16,24},{24,16},{1,9},{9,1},{17,25},{25,17},{2,10},{10... | collective-permute-start | bytes 196616 | tf_op jit(solution)/shard_map/ppermute | solution.py:407
  12.7 5.4 %collective-permute-start.4 = (bf16[128,256]{1,0:T(8,128)(2,1)S(1)}, bf16[128,256]{1,0:T(8,128)(2,1)S(1)}, u32[]{:S(2)}, u32[]{:S(2)}) collective-permute-start(bf16[128,256]{1,0:T(8,128)(2,1)S(1)} %get-tuple-element.27), channel_id=1, source_target_pairs={{0,16},{8,24},{16,0},{24,8},{1,17},{9,25},{17,1},{25,9},{2,18},{10... | collective-permute-start | bytes 196616 | tf_op jit(solution)/shard_map/ppermute | solution.py:407
  13.5 4.6 %collective-permute-start.1 = (bf16[2,2,40,128]{3,2,1,0:T(8,128)(2,1)S(1)}, bf16[2,2,40,128]{3,2,1,0:T(8,128)(2,1)S(1)}, u32[]{:S(2)}, u32[]{:S(2)}) collective-permute-start(bf16[2,2,40,128]{3,2,1,0:T(8,128)(2,1)S(1)} %join.1), channel_id=1, source_target_pairs={{0,4},{1,5},{2,6},{3,7},{4,0},{5,1},{6,2},{7,3},{8,12},{9,13},{10,... | collective-permute-start | bytes 122888 | tf_op jit(solution)/shard_map/ppermute | solution.py:413
  15.0 3.6 %collective-permute-start.5 = (bf16[128,256]{1,0:T(8,128)(2,1)S(1)}, bf16[128,256]{1,0:T(8,128)(2,1)S(1)}, u32[]{:S(2)}, u32[]{:S(2)}) collective-permute-start(bf16[128,256]{1,0:T(8,128)(2,1)S(1)} %get-tuple-element.24.rest_0_), channel_id=1, source_target_pairs={{0,2},{1,3},{2,0},{3,1},{4,6},{5,7},{6,4},{7,5},{8,10},{9,11},{10,... | collective-permute-start | bytes 196616 | tf_op jit(solution)/shard_map/ppermute | solution.py:413
  15.3 3.4 %collective-permute-start.6 = (bf16[128,256]{1,0:T(8,128)(2,1)S(1)}, bf16[128,256]{1,0:T(8,128)(2,1)S(1)}, u32[]{:S(2)}, u32[]{:S(2)}) collective-permute-start(bf16[128,256]{1,0:T(8,128)(2,1)S(1)} %collective-permute-done.2.rest_1_), channel_id=1, source_target_pairs={{0,2},{1,3},{2,0},{3,1},{4,6},{5,7},{6,4},{7,5},{8,10},{9,11},{10,... | collective-permute-start | bytes 196616 | tf_op jit(solution)/shard_map/ppermute | solution.py:413
  17.3 1.3 %collective-permute-start.7 = (bf16[128,256]{1,0:T(8,128)(2,1)S(1)}, bf16[128,256]{1,0:T(8,128)(2,1)S(1)}, u32[]{:S(2)}, u32[]{:S(2)}) collective-permute-start(bf16[128,256]{1,0:T(8,128)(2,1)S(1)} %collective-permute-done.3.rest_2_), channel_id=1, source_target_pairs={{0,2},{1,3},{2,0},{3,1},{4,6},{5,7},{6,4},{7,5},{8,10},{9,11},{10,... | collective-permute-start | bytes 196616 | tf_op jit(solution)/shard_map/ppermute | solution.py:413
  18.0 1.3 %collective-permute-start.8 = (bf16[128,256]{1,0:T(8,128)(2,1)S(1)}, bf16[128,256]{1,0:T(8,128)(2,1)S(1)}, u32[]{:S(2)}, u32[]{:S(2)}) collective-permute-start(bf16[128,256]{1,0:T(8,128)(2,1)S(1)} %collective-permute-done.4.rest_3_), channel_id=1, source_target_pairs={{0,2},{1,3},{2,0},{3,1},{4,6},{5,7},{6,4},{7,5},{8,10},{9,11},{10,... | collective-permute-start | bytes 196616 | tf_op jit(solution)/shard_map/ppermute | solution.py:413
  18.1 5.3 %copy-start = (s32[1,64]{1,0:T(1,128)S(1)}, s32[1,64]{1,0:T(1,128)}, u32[]{:S(2)}) copy-start(s32[1,64]{1,0:T(1,128)} %table_ref.1) | copy-start | bytes 772
  19.8 5.0 %collective-permute-start.9 = (bf16[2,32,128]{2,1,0:T(8,128)(2,1)S(1)}, bf16[2,32,128]{2,1,0:T(8,128)(2,1)S(1)}, u32[]{:S(2)}, u32[]{:S(2)}) collective-permute-start(bf16[2,32,128]{2,1,0:T(8,128)(2,1)S(1)} %get-tuple-element.28), channel_id=1, source_target_pairs={{0,5},{1,4},{2,7},{3,6},{4,1},{5,0},{6,3},{7,2},{8,13},{9,12},{10,... | collective-permute-start | bytes 49160 | tf_op jit(solution)/shard_map/ppermute | solution.py:413
  21.4 3.7 %collective-permute-start.10 = (bf16[2,32,128]{2,1,0:T(8,128)(2,1)S(1)}, bf16[2,32,128]{2,1,0:T(8,128)(2,1)S(1)}, u32[]{:S(2)}, u32[]{:S(2)}) collective-permute-start(bf16[2,32,128]{2,1,0:T(8,128)(2,1)S(1)} %get-tuple-element.29), channel_id=1, source_target_pairs={{0,4},{1,5},{2,6},{3,7},{4,0},{5,1},{6,2},{7,3},{8,12},{9,13},{10,... | collective-permute-start | bytes 49160 | tf_op jit(solution)/shard_map/ppermute | solution.py:413
  21.9 3.7 %collective-permute-start.11 = (bf16[2,32,128]{2,1,0:T(8,128)(2,1)S(1)}, bf16[2,32,128]{2,1,0:T(8,128)(2,1)S(1)}, u32[]{:S(2)}, u32[]{:S(2)}) collective-permute-start(bf16[2,32,128]{2,1,0:T(8,128)(2,1)S(1)} %get-tuple-element.30), channel_id=1, source_target_pairs={{0,1},{1,0},{2,3},{3,2},{4,5},{5,4},{6,7},{7,6},{8,9},{9,8},{10,11... | collective-permute-start | bytes 49160 | tf_op jit(solution)/shard_map/ppermute | solution.py:413

commit v7 on v6

--- a/solution.py
+++ b/solution.py
@@ -172,34 +172,47 @@
     )(*map(in_hbm, operands))
 
 
-def store_kernel(groups, table_ref, *rest):
-    blocks, (cache_ref, sem) = rest[:groups], rest[groups:]
+def store_kernel(groups, picks, table_ref, *rest):
+    blocks, (cache_ref, sem) = rest[: len(picks)], rest[-2:]
     me = lax.axis_index("group")
     pages = blocks[0].shape[0]
     sources = [source(me) for _, source in partners(groups)] + [me]
-    for block, source in zip(blocks, sources):
-
-        def place(j, carry, block=block, source=source):
+    for block, at in zip(blocks, picks):
+
+        def place(j, carry, block=block, source=sources[at]):
             slot = table_ref[0, source * pages + j]
             pltpu.make_async_copy(block.at[j], cache_ref.at[slot], sem).start()
             return carry
 
         lax.fori_loop(0, pages, place, 0, unroll=True)
-    pltpu.make_async_copy(cache_ref, cache_ref, sem).wait()
-
-
-def store(groups, page_table, blocks):
-    return pl.pallas_call(
-        functools.partial(store_kernel, groups),
-        in_specs=[pl.BlockSpec(memory_space=pltpu.SMEM)]
-        + [pl.BlockSpec(memory_space=pltpu.VMEM)] * groups,
+    stored = cache_ref.at[pl.ds(0, len(picks) * pages)]
+    pltpu.make_async_copy(stored, stored, sem).wait()
+
+
+def store(groups, picks, page_table, blocks, cache=None):
+    pages = rows_of(blocks)
+    operands = [page_table] + pages
+    specs = [pl.BlockSpec(memory_space=pltpu.SMEM)] + [pl.BlockSpec(memory_space=pltpu.VMEM)] * len(pages)
+    aliases = {}
+    if cache is not None:
+        aliases = {len(operands): 0}
+        operands.append(cache)
+        specs.append(pl.BlockSpec(memory_space=pl.ANY))
+    return pl.pallas_call(
+        functools.partial(store_kernel, groups, picks),
+        in_specs=specs,
         out_specs=pl.BlockSpec(memory_space=pl.ANY),
-        out_shape=jax.ShapeDtypeStruct((page_table.shape[1],) + blocks[0].shape[1:], jnp.bfloat16),
+        out_shape=pltpu.HBM((page_table.shape[1],) + pages[0].shape[1:], jnp.bfloat16),
+        input_output_aliases=aliases,
         scratch_shapes=[pltpu.SemaphoreType.DMA],
         cost_estimate=pl.CostEstimate(flops=HIDE_FLOPS, transcendentals=0, bytes_accessed=0),
         compiler_params=pltpu.CompilerParams(vmem_limit_bytes=PACK_VMEM),
         name="store",
-    )(page_table, *blocks)
+    )(*operands)
+
+
+def rows_of(blocks):
+    return [block.reshape(block.shape[0] // PAGE, PAGE, 2 * HEAD_DIM) for block in blocks]
 
 
 def join_kernel(first_ref, second_ref, out_ref):
@@ -269,25 +282,23 @@
         row // q_rows == column // (2 * steps), column % (2 * steps) <= row % steps
     )
     recent_score = jnp.where(visible, recent_score, -jnp.inf)
-    scores = [scored(block[:, :HEAD_DIM]) for block in blocks]
-    highest = functools.reduce(jnp.maximum, scores).max(axis=1, keepdims=True)
+    score = scored(jnp.concatenate([block[:, :HEAD_DIM] for block in blocks], axis=0))
+    highest = jnp.max(score, axis=1, keepdims=True)
     highest = jnp.maximum(highest, jnp.max(recent_score, axis=1, keepdims=True))
     recent_weight = jnp.exp(recent_score - highest)
-    weights = [jnp.exp(score - highest) for score in scores]
-    total = functools.reduce(jnp.add, weights).sum(axis=1, keepdims=True)
+    weight = jnp.exp(score - highest)
+    total = jnp.sum(weight, axis=1, keepdims=True)
     total = total + jnp.sum(recent_weight, axis=1, keepdims=True)
+    values = jnp.concatenate([block[:, HEAD_DIM:] for block in blocks], axis=0)
     blended = jnp.dot(
         recent_weight.astype(jnp.bfloat16), recent_value, preferred_element_type=jnp.float32
-    )
-    for weight, block in zip(weights, blocks):
-        blended = blended + jnp.dot(
-            weight.astype(jnp.bfloat16), block[:, HEAD_DIM:], preferred_element_type=jnp.float32
-        )
+    ) + jnp.dot(weight.astype(jnp.bfloat16), values, preferred_element_type=jnp.float32)
     blended = blended / total
     return jnp.where(alive > 0.0, blended, 0.0)
 
 
-def attend_own_kernel(groups, steps, alive_ref, query_ref, key_ref, value_ref, *rest):
+def attend_own_kernel(groups, steps, cache_ref, alive_ref, query_ref, key_ref, value_ref, *rest):
+    del cache_ref
     blocks, out_ref = rest[:groups], rest[groups]
     out_ref[...] = attend_head(
         steps,
@@ -299,17 +310,17 @@
     ).astype(out_ref.dtype)
 
 
-def attend_own(groups, steps, alive, arranged, blocks):
+def attend_own(groups, steps, cache, alive, arranged, blocks):
     vmem = pl.BlockSpec(memory_space=pltpu.VMEM)
     return pl.pallas_call(
         functools.partial(attend_own_kernel, groups, steps),
-        in_specs=[vmem] * (1 + len(arranged) + groups),
+        in_specs=[pl.BlockSpec(memory_space=pl.ANY)] + [vmem] * (1 + len(arranged) + groups),
         out_specs=vmem,
         out_shape=pltpu.VMEM(arranged[0].shape[1:], jnp.bfloat16),
         cost_estimate=pl.CostEstimate(flops=HIDE_FLOPS, transcendentals=0, bytes_accessed=0),
         compiler_params=pltpu.CompilerParams(vmem_limit_bytes=VMEM_LIMIT),
         name="attend_own",
-    )(alive, *arranged, *blocks)
+    )(in_hbm(cache), alive, *arranged, *blocks)
 
 
 def attend_kernel(groups, steps, alive_ref, query_ref, key_ref, value_ref, own_ref, *rest):
@@ -419,13 +430,12 @@
     ready = [own] + blocks[:-3] + [blocks[-2], blocks[-3]]
     sibling_blocks = [to_peer(block, SIBLING) for block in ready]
     arranged = arrange(steps, packets)
-    own_head = attend_own(groups, steps, alive, arranged, ready)
+    early = (groups - 1,)
+    cache = store(groups, early, page_table, [blocks[at] for at in early])
+    own_head = attend_own(groups, steps, cache, alive, arranged, ready)
     parts = attend(groups, steps, alive, arranged, own_head, sibling_blocks)
-    cache = store(
-        groups,
-        page_table,
-        [block.reshape(rows // PAGE, PAGE, 2 * HEAD_DIM) for block in blocks],
-    )
+    late = tuple(at for at in range(groups) if at not in early)
+    cache = store(groups, late, page_table, [blocks[at] for at in late], cache)
     returned = gather([to_peer(part, at) for part, at in zip(parts, PEERS)] + [parts[-1]])
     attention_out = returned.reshape(KV_HEADS * Q_PER_KV, steps, HEAD_DIM).transpose(1, 0, 2)
     return attention_out.reshape(new_query.shape), cache[None]

time: 26.5 us -> 26.4 us (level)
  waiting for transfers between devices: 4.27 us -> 3.18 us
  Pallas kernels: 8.62 us -> 9.59 us
    ppermute x3, waiting for transfers between devices: 2.78 us -> 1.51 us  [local(): lax.ppermute(block, 'group', [(i, goes_to(i)) for i in range(groups)])]
    pallas_call x1 -> x2, Pallas kernels: 1.39 us -> 2.54 us  [store(): pl.pallas_call(functools.partial(store_kernel, groups, picks), in_specs=s...]
  transfers between devices with their start and end apart: 12 -> 12, of which waited for: 6 -> 5; matrix products, arithmetic and copies ran while one was open for 0% -> 0% of each run, Pallas kernels for 7% -> 11%
where the time goes in v7:
time: 26.4 us; the launch traced here: 26.3 us
  starting transfers between devices  12.8 us (48%)
  Pallas kernels  9.59 us (36%)
  waiting for transfers between devices  3.18 us (12%)
  between operations  0.73 us (3%)
    ppermute x9, starting transfers between devices, to_peer(): lax.ppermute(array, MEMBERS, [(i, i ^ distance) for i in range(members)])  8.37 us
    pallas_call x1, Pallas kernels, project(): pl.pallas_call(functools.partial(project_kernel, groups, ordered), in_spe...  5.44 us
    ppermute x3, starting transfers between devices, local(): lax.ppermute(block, 'group', [(i, goes_to(i)) for i in range(groups)])  4.39 us
    pallas_call x2, Pallas kernels, store(): pl.pallas_call(functools.partial(store_kernel, groups, picks), in_specs=s...  2.54 us
    ppermute x9, waiting for transfers between devices, to_peer(): lax.ppermute(array, MEMBERS, [(i, i ^ distance) for i in range(members)])  1.66 us
    ppermute x3, waiting for transfers between devices, local(): lax.ppermute(block, 'group', [(i, goes_to(i)) for i in range(groups)])  1.51 us
    pallas_call x1, Pallas kernels, gather(): pl.pallas_call(gather_kernel, in_specs=[pl.BlockSpec(memory_space=pltpu.V...  0.69 us
  transfers between devices with their start and end apart: 12, of which 5 were waited for; matrix products, arithmetic and copies ran while one was open for 0% of the time, Pallas kernels for 11%

profile of v7, /device:TPU:0, one launch (start us, length us, event | category | flops | bytes accessed | tf_op | source)
XLA Modules:
  0.0 26.3 jit_solution(10450068558165128338)
XLA Ops:
  0.6 0.0 copy-start
  0.6 5.4 %project.1 = (bf16[128,256]{1,0:T(8,128)(2,1)S(1)}, bf16[128,256]{1,0:T(8,128)(2,1)S(1)}, bf16[128,256]{1,0:T(8,128)(2,1)S(1)}, bf16[128,256]{1,0:T(8,128)(2,1)S...) custom-call(s32[4]{0:T(128)} %prompt_hbm.1, ...), custom_call_target="tpu_custom_call" | custom-call | tf_op jit(solution)/shard_map/project/pallas_call | solution.py:152
  6.1 3.0 %collective-permute-start = (bf16[2,2,40,128]{3,2,1,0:T(8,128)(2,1)S(1)}, bf16[2,2,40,128]{3,2,1,0:T(8,128)(2,1)S(1)}, u32[]{:S(2)}, u32[]{:S(2)}) collective-permute-start(bf16[2,2,40,128]{3,2,1,0:T(8,128)(2,1)S(1)} %get-tuple-element.19), channel_id=1, source_target_pairs={{0,1},{1,0},{2,3},{3,2},{4,5},{5,4},{6,7},{7,6},{8,9},{9,8},{10,11... | collective-permute-start | bytes 122888 | tf_op jit(solution)/shard_map/ppermute | solution.py:424
  9.1 3.6 %collective-permute-start.2 = (bf16[128,256]{1,0:T(8,128)(2,1)S(1)}, bf16[128,256]{1,0:T(8,128)(2,1)S(1)}, u32[]{:S(2)}, u32[]{:S(2)}) collective-permute-start(bf16[128,256]{1,0:T(8,128)(2,1)S(1)} %get-tuple-element.25), channel_id=1, source_target_pairs={{0,24},{8,16},{16,8},{24,0},{1,25},{9,17},{17,9},{25,1},{2,26},{10... | collective-permute-start | bytes 196616 | tf_op jit(solution)/shard_map/ppermute | solution.py:418
  12.7 0.0 collective-permute-start.3
  12.7 0.8 %collective-permute-start.4 = (bf16[128,256]{1,0:T(8,128)(2,1)S(1)}, bf16[128,256]{1,0:T(8,128)(2,1)S(1)}, u32[]{:S(2)}, u32[]{:S(2)}) collective-permute-start(bf16[128,256]{1,0:T(8,128)(2,1)S(1)} %get-tuple-element.27), channel_id=1, source_target_pairs={{0,16},{8,24},{16,0},{24,8},{1,17},{9,25},{17,1},{25,9},{2,18},{10... | collective-permute-start | bytes 196616 | tf_op jit(solution)/shard_map/ppermute | solution.py:418
  13.5 0.0 collective-permute-start.5
  13.5 0.0 collective-permute-done.second_ref.near_ref
  13.5 1.6 %collective-permute-start.1 = (bf16[2,2,40,128]{3,2,1,0:T(8,128)(2,1)S(1)}, bf16[2,2,40,128]{3,2,1,0:T(8,128)(2,1)S(1)}, u32[]{:S(2)}, u32[]{:S(2)}) collective-permute-start(bf16[2,2,40,128]{3,2,1,0:T(8,128)(2,1)S(1)} %join.1), channel_id=1, source_target_pairs={{0,4},{1,5},{2,6},{3,7},{4,0},{5,1},{6,2},{7,3},{8,12},{9,13},{10,... | collective-permute-start | bytes 122888 | tf_op jit(solution)/shard_map/ppermute | solution.py:424
  15.1 0.0 copy-done
  15.1 1.2 %store.2.cache_ref.rest_3_ = bf16[64,8,256]{2,1,0:T(8,128)(2,1)} custom-call(s32[1,64]{1,0:T(1,128)S(1)} %copy-done, bf16[16,8,256]{2,1,0:T(8,128)(2,1)S(1)} %bitcast.24), custom_call_target="tpu_custom_call" | custom-call | flops 20000000000 | tf_op jit(solution)/shard_map/store/pallas_call | solution.py:201
  16.3 0.0 collective-permute-done.2.rest_1_
  16.3 0.2 collective-permute-start.6
  16.5 0.8 %collective-permute-done.3.rest_2_ = bf16[128,256]{1,0:T(8,128)(2,1)S(1)} collective-permute-done((bf16[128,256]{1,0:T(8,128)(2,1)S(1)}, bf16[128,256]{1,0:T(8,128)(2,1)S(1)}, u32[]{:S(2)}, u32[]{:S(2)}) %collective-permute-start.3) | collective-permute-done | bytes 65568 | tf_op jit(solution)/shard_map/ppermute | solution.py:418
  17.3 0.0 collective-permute-start.7
  17.3 0.7 %collective-permute-done.4.rest_3_ = bf16[128,256]{1,0:T(8,128)(2,1)S(1)} collective-permute-done((bf16[128,256]{1,0:T(8,128)(2,1)S(1)}, bf16[128,256]{1,0:T(8,128)(2,1)S(1)}, u32[]{:S(2)}, u32[]{:S(2)}) %collective-permute-start.4) | collective-permute-done | bytes 65568 | tf_op jit(solution)/shard_map/ppermute | solution.py:418
  18.1 0.0 collective-permute-start.8
  18.1 0.0 collective-permute-done.1.far_ref
  18.1 0.5 %attend_own.1.own_ref = bf16[128,128]{1,0:T(8,128)(2,1)S(1)} custom-call(bf16[64,8,256]{2,1,0:T(8,128)(2,1)} %store.2.cache_ref.rest_3_, f32[128,128]{1,0:T(8,128)S(1)} %get-tuple-element.17.alive_ref, bf16[2,128,128]{2,1,0:T(8,128)(2,1)S(1)} %get-tuple-element.21.query_ref, bf16[2,32,128]{2,1,0:T(8,128)(2,1)S(1)} %get-tuple-element.22.key_ref, ...), custom_call_target="tpu_custom_call" | custom-call | flops 20000000000 | tf_op jit(solution)/shard_map/attend_own/pallas_call | solution.py:315
  18.5 0.0 collective-permute-done.5.rest_0_
  18.5 0.0 collective-permute-done.6.rest_1_
  18.6 0.0 collective-permute-done.7.rest_2_
  18.6 0.7 %collective-permute-done.8.rest_3_ = bf16[128,256]{1,0:T(8,128)(2,1)S(1)} collective-permute-done((bf16[128,256]{1,0:T(8,128)(2,1)S(1)}, bf16[128,256]{1,0:T(8,128)(2,1)S(1)}, u32[]{:S(2)}, u32[]{:S(2)}) %collective-permute-start.8) | collective-permute-done | bytes 65568 | tf_op jit(solution)/shard_map/ppermute | solution.py:424
  19.3 0.4 %attend.1 = (bf16[2,32,128]{2,1,0:T(8,128)(2,1)S(1)}, bf16[2,32,128]{2,1,0:T(8,128)(2,1)S(1)}, bf16[2,32,128]{2,1,0:T(8,128)(2,1)S(1)}, bf16[2,32,128]{2,1,0:T(8,128)(2,1)S(1)}) custom-call(f32[128,128]{1,0:T(8,128)S(1)} %get-tuple-element.17.alive_ref, bf16[2,128,128]{2,1,0:T(8,128)(2,1)S(1)} %get-tuple-element.21.query_ref, ...), custom_call_target="tpu_custom_call" | custom-call | tf_op jit(solution)/shard_map/attend/pallas_call | solution.py:345
  19.8 1.6 %collective-permute-start.9 = (bf16[2,32,128]{2,1,0:T(8,128)(2,1)S(1)}, bf16[2,32,128]{2,1,0:T(8,128)(2,1)S(1)}, u32[]{:S(2)}, u32[]{:S(2)}) collective-permute-start(bf16[2,32,128]{2,1,0:T(8,128)(2,1)S(1)} %get-tuple-element.28), channel_id=1, source_target_pairs={{0,5},{1,4},{2,7},{3,6},{4,1},{5,0},{6,3},{7,2},{8,13},{9,12},{10,... | collective-permute-start | bytes 49160 | tf_op jit(solution)/shard_map/ppermute | solution.py:424
  21.3 0.5 %collective-permute-start.10 = (bf16[2,32,128]{2,1,0:T(8,128)(2,1)S(1)}, bf16[2,32,128]{2,1,0:T(8,128)(2,1)S(1)}, u32[]{:S(2)}, u32[]{:S(2)}) collective-permute-start(bf16[2,32,128]{2,1,0:T(8,128)(2,1)S(1)} %get-tuple-element.29), channel_id=1, source_target_pairs={{0,4},{1,5},{2,6},{3,7},{4,0},{5,1},{6,2},{7,3},{8,12},{9,13},{10,... | collective-permute-start | bytes 49160 | tf_op jit(solution)/shard_map/ppermute | solution.py:424
  21.8 1.5 %collective-permute-start.11 = (bf16[2,32,128]{2,1,0:T(8,128)(2,1)S(1)}, bf16[2,32,128]{2,1,0:T(8,128)(2,1)S(1)}, u32[]{:S(2)}, u32[]{:S(2)}) collective-permute-start(bf16[2,32,128]{2,1,0:T(8,128)(2,1)S(1)} %get-tuple-element.30), channel_id=1, source_target_pairs={{0,1},{1,0},{2,3},{3,2},{4,5},{5,4},{6,7},{7,6},{8,9},{9,8},{10,11... | collective-permute-start | bytes 49160 | tf_op jit(solution)/shard_map/ppermute | solution.py:424
  23.3 1.3 %store.3 = bf16[64,8,256]{2,1,0:T(8,128)(2,1)} custom-call(s32[1,64]{1,0:T(1,128)S(1)} %copy-done, bf16[16,8,256]{2,1,0:T(8,128)(2,1)S(1)} %bitcast.21, bf16[16,8,256]{2,1,0:T(8,128)(2,1)S(1)} %bitcast.23, bf16[16,8,256]{2,1,0:T(8,128)(2,1)S(1)} %bitcast.22, bf16[64,8,256]{2,1,0:T(8,128)(2,1)} %store.2.cache_ref.rest_3_), custom_call_target="tpu_custom_call", output_to_operand_aliasing={{}: (4, {})} | custom-call | flops 20000000000 | tf_op jit(solution)/shard_map/store/pallas_call | solution.py:201
  24.7 0.0 collective-permute-done.9.refs_0_
  24.7 0.4 %collective-permute-done.10.refs_1_ = bf16[2,32,128]{2,1,0:T(8,128)(2,1)S(1)} collective-permute-done((bf16[2,32,128]{2,1,0:T(8,128)(2,1)S(1)}, bf16[2,32,128]{2,1,0:T(8,128)(2,1)S(1)}, u32[]{:S(2)}, u32[]{:S(2)}) %collective-permute-start.10) | collective-permute-done | bytes 16416 | tf_op jit(solution)/shard_map/ppermute | solution.py:424
  25.1 0.5 %collective-permute-done.11.refs_2_ = bf16[2,32,128]{2,1,0:T(8,128)(2,1)S(1)} collective-permute-done((bf16[2,32,128]{2,1,0:T(8,128)(2,1)S(1)}, bf16[2,32,128]{2,1,0:T(8,128)(2,1)S(1)}, u32[]{:S(2)}, u32[]{:S(2)}) %collective-permute-start.11) | collective-permute-done | bytes 16416 | tf_op jit(solution)/shard_map/ppermute | solution.py:424
  25.6 0.7 %gather.1 = bf16[8,32,128]{2,1,0:T(8,128)(2,1)} custom-call(bf16[2,32,128]{2,1,0:T(8,128)(2,1)S(1)} %collective-permute-done.9.refs_0_, bf16[2,32,128]{2,1,0:T(8,128)(2,1)S(1)} %collective-permute-done.10.refs_1_, bf16[2,32,128]{2,1,0:T(8,128)(2,1)S(1)} %collective-permute-done.11.refs_2_, bf16[2,32,128]{2,1,0:T(8,128)(2,1)S(1)} %get-tuple-element.31.refs_3_), custom_call_target="tpu_custom_call" | custom-call | tf_op jit(solution)/shard_map/gather/pallas_call | solution.py:373
  (2 shorter events, 0.0 us)
Async XLA Ops:
  0.6 14.5 %copy-start = (s32[1,64]{1,0:T(1,128)S(1)}, s32[1,64]{1,0:T(1,128)}, u32[]{:S(2)}) copy-start(s32[1,64]{1,0:T(1,128)} %table_ref.3) | copy-start | bytes 772
  6.1 7.4 %collective-permute-start = (bf16[2,2,40,128]{3,2,1,0:T(8,128)(2,1)S(1)}, bf16[2,2,40,128]{3,2,1,0:T(8,128)(2,1)S(1)}, u32[]{:S(2)}, u32[]{:S(2)}) collective-permute-start(bf16[2,2,40,128]{3,2,1,0:T(8,128)(2,1)S(1)} %get-tuple-element.19), channel_id=1, source_target_pairs={{0,1},{1,0},{2,3},{3,2},{4,5},{5,4},{6,7},{7,6},{8,9},{9,8},{10,11... | collective-permute-start | bytes 122888 | tf_op jit(solution)/shard_map/ppermute | solution.py:424
  9.1 7.2 %collective-permute-start.2 = (bf16[128,256]{1,0:T(8,128)(2,1)S(1)}, bf16[128,256]{1,0:T(8,128)(2,1)S(1)}, u32[]{:S(2)}, u32[]{:S(2)}) collective-permute-start(bf16[128,256]{1,0:T(8,128)(2,1)S(1)} %get-tuple-element.25), channel_id=1, source_target_pairs={{0,24},{8,16},{16,8},{24,0},{1,25},{9,17},{17,9},{25,1},{2,26},{10... | collective-permute-start | bytes 196616 | tf_op jit(solution)/shard_map/ppermute | solution.py:418
  12.7 4.6 %collective-permute-start.3 = (bf16[128,256]{1,0:T(8,128)(2,1)S(1)}, bf16[128,256]{1,0:T(8,128)(2,1)S(1)}, u32[]{:S(2)}, u32[]{:S(2)}) collective-permute-start(bf16[128,256]{1,0:T(8,128)(2,1)S(1)} %get-tuple-element.26), channel_id=1, source_target_pairs={{0,8},{8,0},{16,24},{24,16},{1,9},{9,1},{17,25},{25,17},{2,10},{10... | collective-permute-start | bytes 196616 | tf_op jit(solution)/shard_map/ppermute | solution.py:418
  12.7 5.4 %collective-permute-start.4 = (bf16[128,256]{1,0:T(8,128)(2,1)S(1)}, bf16[128,256]{1,0:T(8,128)(2,1)S(1)}, u32[]{:S(2)}, u32[]{:S(2)}) collective-permute-start(bf16[128,256]{1,0:T(8,128)(2,1)S(1)} %get-tuple-element.27), channel_id=1, source_target_pairs={{0,16},{8,24},{16,0},{24,8},{1,17},{9,25},{17,1},{25,9},{2,18},{10... | collective-permute-start | bytes 196616 | tf_op jit(solution)/shard_map/ppermute | solution.py:418
  13.5 5.1 %collective-permute-start.5 = (bf16[128,256]{1,0:T(8,128)(2,1)S(1)}, bf16[128,256]{1,0:T(8,128)(2,1)S(1)}, u32[]{:S(2)}, u32[]{:S(2)}) collective-permute-start(bf16[128,256]{1,0:T(8,128)(2,1)S(1)} %get-tuple-element.24.rest_0_), channel_id=1, source_target_pairs={{0,2},{1,3},{2,0},{3,1},{4,6},{5,7},{6,4},{7,5},{8,10},{9,11},{10,... | collective-permute-start | bytes 196616 | tf_op jit(solution)/shard_map/ppermute | solution.py:424
  13.5 4.6 %collective-permute-start.1 = (bf16[2,2,40,128]{3,2,1,0:T(8,128)(2,1)S(1)}, bf16[2,2,40,128]{3,2,1,0:T(8,128)(2,1)S(1)}, u32[]{:S(2)}, u32[]{:S(2)}) collective-permute-start(bf16[2,2,40,128]{3,2,1,0:T(8,128)(2,1)S(1)} %join.1), channel_id=1, source_target_pairs={{0,4},{1,5},{2,6},{3,7},{4,0},{5,1},{6,2},{7,3},{8,12},{9,13},{10,... | collective-permute-start | bytes 122888 | tf_op jit(solution)/shard_map/ppermute | solution.py:424
  16.3 2.2 %collective-permute-start.6 = (bf16[128,256]{1,0:T(8,128)(2,1)S(1)}, bf16[128,256]{1,0:T(8,128)(2,1)S(1)}, u32[]{:S(2)}, u32[]{:S(2)}) collective-permute-start(bf16[128,256]{1,0:T(8,128)(2,1)S(1)} %collective-permute-done.2.rest_1_), channel_id=1, source_target_pairs={{0,2},{1,3},{2,0},{3,1},{4,6},{5,7},{6,4},{7,5},{8,10},{9,11},{10,... | collective-permute-start | bytes 196616 | tf_op jit(solution)/shard_map/ppermute | solution.py:424
  17.3 1.3 %collective-permute-start.7 = (bf16[128,256]{1,0:T(8,128)(2,1)S(1)}, bf16[128,256]{1,0:T(8,128)(2,1)S(1)}, u32[]{:S(2)}, u32[]{:S(2)}) collective-permute-start(bf16[128,256]{1,0:T(8,128)(2,1)S(1)} %collective-permute-done.3.rest_2_), channel_id=1, source_target_pairs={{0,2},{1,3},{2,0},{3,1},{4,6},{5,7},{6,4},{7,5},{8,10},{9,11},{10,... | collective-permute-start | bytes 196616 | tf_op jit(solution)/shard_map/ppermute | solution.py:424
  18.1 1.3 %collective-permute-start.8 = (bf16[128,256]{1,0:T(8,128)(2,1)S(1)}, bf16[128,256]{1,0:T(8,128)(2,1)S(1)}, u32[]{:S(2)}, u32[]{:S(2)}) collective-permute-start(bf16[128,256]{1,0:T(8,128)(2,1)S(1)} %collective-permute-done.4.rest_3_), channel_id=1, source_target_pairs={{0,2},{1,3},{2,0},{3,1},{4,6},{5,7},{6,4},{7,5},{8,10},{9,11},{10,... | collective-permute-start | bytes 196616 | tf_op jit(solution)/shard_map/ppermute | solution.py:424
  19.8 4.9 %collective-permute-start.9 = (bf16[2,32,128]{2,1,0:T(8,128)(2,1)S(1)}, bf16[2,32,128]{2,1,0:T(8,128)(2,1)S(1)}, u32[]{:S(2)}, u32[]{:S(2)}) collective-permute-start(bf16[2,32,128]{2,1,0:T(8,128)(2,1)S(1)} %get-tuple-element.28), channel_id=1, source_target_pairs={{0,5},{1,4},{2,7},{3,6},{4,1},{5,0},{6,3},{7,2},{8,13},{9,12},{10,... | collective-permute-start | bytes 49160 | tf_op jit(solution)/shard_map/ppermute | solution.py:424
  21.3 3.7 %collective-permute-start.10 = (bf16[2,32,128]{2,1,0:T(8,128)(2,1)S(1)}, bf16[2,32,128]{2,1,0:T(8,128)(2,1)S(1)}, u32[]{:S(2)}, u32[]{:S(2)}) collective-permute-start(bf16[2,32,128]{2,1,0:T(8,128)(2,1)S(1)} %get-tuple-element.29), channel_id=1, source_target_pairs={{0,4},{1,5},{2,6},{3,7},{4,0},{5,1},{6,2},{7,3},{8,12},{9,13},{10,... | collective-permute-start | bytes 49160 | tf_op jit(solution)/shard_map/ppermute | solution.py:424
  21.8 3.7 %collective-permute-start.11 = (bf16[2,32,128]{2,1,0:T(8,128)(2,1)S(1)}, bf16[2,32,128]{2,1,0:T(8,128)(2,1)S(1)}, u32[]{:S(2)}, u32[]{:S(2)}) collective-permute-start(bf16[2,32,128]{2,1,0:T(8,128)(2,1)S(1)} %get-tuple-element.30), channel_id=1, source_target_pairs={{0,1},{1,0},{2,3},{3,2},{4,5},{5,4},{6,7},{7,6},{8,9},{9,8},{10,11... | collective-permute-start | bytes 49160 | tf_op jit(solution)/shard_map/ppermute | solution.py:424

commit v8 on v7

--- a/solution.py
+++ b/solution.py
@@ -334,9 +334,10 @@
         value_ref[1],
         [block[...] for block in blocks],
     ).astype(jnp.bfloat16)
+    side = jnp.where(lax.axis_index(MEMBERS) & SIBLING == 0, 0, 1)
     for to, out in enumerate(outs):
-        out[0] = own_ref[to * q_rows : (to + 1) * q_rows]
-        out[1] = blended[to * q_rows : (to + 1) * q_rows]
+        out[side] = own_ref[to * q_rows : (to + 1) * q_rows]
+        out[1 - side] = blended[to * q_rows : (to + 1) * q_rows]
 
 
 def attend(groups, steps, alive, arranged, own, blocks):
@@ -357,11 +358,10 @@
     member = lax.axis_index(MEMBERS)
     copies = []
     for distance, part in zip(PEERS + (0,), parts):
-        for at in range(2):
-            head = member ^ distance ^ (SIBLING * at)
-            copies.append(
-                pltpu.make_async_copy(part.at[at], out_ref.at[head], sem.at[len(copies)])
-            )
+        head = member ^ distance
+        copies.append(
+            pltpu.make_async_copy(part, out_ref.at[head // 4, :, head % 2], sem.at[len(copies)])
+        )
     for copy in copies:
         copy.start()
     for copy in copies:
@@ -374,8 +374,8 @@
         gather_kernel,
         in_specs=[pl.BlockSpec(memory_space=pltpu.VMEM)] * len(parts),
         out_specs=pl.BlockSpec(memory_space=pl.ANY),
-        out_shape=pltpu.HBM((heads, rows, width), parts[0].dtype),
-        scratch_shapes=[pltpu.SemaphoreType.DMA((heads,))],
+        out_shape=pltpu.HBM((heads // 4, 2, 2, rows, width), parts[0].dtype),
+        scratch_shapes=[pltpu.SemaphoreType.DMA((len(parts),))],
         compiler_params=pltpu.CompilerParams(vmem_limit_bytes=PACK_VMEM),
         name="gather",
     )(*parts)

time: 26.4 us -> 26.4 us (level)
  no operation moved by 1% of the time
where the time goes in v8:
time: 26.4 us; the launch traced here: 26.2 us
  starting transfers between devices  12.8 us (48%)
  Pallas kernels  9.55 us (36%)
  waiting for transfers between devices  3.18 us (12%)
  between operations  0.73 us (3%)
    ppermute x9, starting transfers between devices, to_peer(): lax.ppermute(array, MEMBERS, [(i, i ^ distance) for i in range(members)])  8.37 us
    pallas_call x1, Pallas kernels, project(): pl.pallas_call(functools.partial(project_kernel, groups, ordered), in_spe...  5.44 us
    ppermute x3, starting transfers between devices, local(): lax.ppermute(block, 'group', [(i, goes_to(i)) for i in range(groups)])  4.39 us
    pallas_call x2, Pallas kernels, store(): pl.pallas_call(functools.partial(store_kernel, groups, picks), in_specs=s...  2.54 us
    ppermute x9, waiting for transfers between devices, to_peer(): lax.ppermute(array, MEMBERS, [(i, i ^ distance) for i in range(members)])  1.66 us
    ppermute x3, waiting for transfers between devices, local(): lax.ppermute(block, 'group', [(i, goes_to(i)) for i in range(groups)])  1.51 us
    pallas_call x1, Pallas kernels, gather(): pl.pallas_call(gather_kernel, in_specs=[pl.BlockSpec(memory_space=pltpu.V...  0.66 us
  transfers between devices with their start and end apart: 12, of which 5 were waited for; matrix products, arithmetic and copies ran while one was open for 0% of the time, Pallas kernels for 11%

profile of v8, /device:TPU:0, one launch (start us, length us, event | category | flops | bytes accessed | tf_op | source)
XLA Modules:
  0.0 26.2 jit_solution(10539026199855164577)
XLA Ops:
  0.6 0.0 copy-start
  0.6 5.4 %project.1 = (bf16[128,256]{1,0:T(8,128)(2,1)S(1)}, bf16[128,256]{1,0:T(8,128)(2,1)S(1)}, bf16[128,256]{1,0:T(8,128)(2,1)S(1)}, bf16[128,256]{1,0:T(8,128)(2,1)S...) custom-call(s32[4]{0:T(128)} %prompt_hbm.1, ...), custom_call_target="tpu_custom_call" | custom-call | tf_op jit(solution)/shard_map/project/pallas_call | solution.py:152
  6.1 3.0 %collective-permute-start = (bf16[2,2,40,128]{3,2,1,0:T(8,128)(2,1)S(1)}, bf16[2,2,40,128]{3,2,1,0:T(8,128)(2,1)S(1)}, u32[]{:S(2)}, u32[]{:S(2)}) collective-permute-start(bf16[2,2,40,128]{3,2,1,0:T(8,128)(2,1)S(1)} %get-tuple-element.19), channel_id=1, source_target_pairs={{0,1},{1,0},{2,3},{3,2},{4,5},{5,4},{6,7},{7,6},{8,9},{9,8},{10,11... | collective-permute-start | bytes 122888 | tf_op jit(solution)/shard_map/ppermute | solution.py:424
  9.1 3.6 %collective-permute-start.2 = (bf16[128,256]{1,0:T(8,128)(2,1)S(1)}, bf16[128,256]{1,0:T(8,128)(2,1)S(1)}, u32[]{:S(2)}, u32[]{:S(2)}) collective-permute-start(bf16[128,256]{1,0:T(8,128)(2,1)S(1)} %get-tuple-element.25), channel_id=1, source_target_pairs={{0,24},{8,16},{16,8},{24,0},{1,25},{9,17},{17,9},{25,1},{2,26},{10... | collective-permute-start | bytes 196616 | tf_op jit(solution)/shard_map/ppermute | solution.py:418
  12.7 0.0 collective-permute-start.3
  12.7 0.8 %collective-permute-start.4 = (bf16[128,256]{1,0:T(8,128)(2,1)S(1)}, bf16[128,256]{1,0:T(8,128)(2,1)S(1)}, u32[]{:S(2)}, u32[]{:S(2)}) collective-permute-start(bf16[128,256]{1,0:T(8,128)(2,1)S(1)} %get-tuple-element.27), channel_id=1, source_target_pairs={{0,16},{8,24},{16,0},{24,8},{1,17},{9,25},{17,1},{25,9},{2,18},{10... | collective-permute-start | bytes 196616 | tf_op jit(solution)/shard_map/ppermute | solution.py:418
  13.5 0.0 collective-permute-start.5
  13.5 0.0 collective-permute-done.second_ref.near_ref
  13.5 1.6 %collective-permute-start.1 = (bf16[2,2,40,128]{3,2,1,0:T(8,128)(2,1)S(1)}, bf16[2,2,40,128]{3,2,1,0:T(8,128)(2,1)S(1)}, u32[]{:S(2)}, u32[]{:S(2)}) collective-permute-start(bf16[2,2,40,128]{3,2,1,0:T(8,128)(2,1)S(1)} %join.1), channel_id=1, source_target_pairs={{0,4},{1,5},{2,6},{3,7},{4,0},{5,1},{6,2},{7,3},{8,12},{9,13},{10,... | collective-permute-start | bytes 122888 | tf_op jit(solution)/shard_map/ppermute | solution.py:424
  15.1 0.0 copy-done
  15.1 1.2 %store.2.cache_ref.rest_3_ = bf16[64,8,256]{2,1,0:T(8,128)(2,1)} custom-call(s32[1,64]{1,0:T(1,128)S(1)} %copy-done, bf16[16,8,256]{2,1,0:T(8,128)(2,1)S(1)} %bitcast.24), custom_call_target="tpu_custom_call" | custom-call | flops 20000000000 | tf_op jit(solution)/shard_map/store/pallas_call | solution.py:201
  16.3 0.0 collective-permute-done.2.rest_1_
  16.3 0.2 collective-permute-start.6
  16.5 0.8 %collective-permute-done.3.rest_2_ = bf16[128,256]{1,0:T(8,128)(2,1)S(1)} collective-permute-done((bf16[128,256]{1,0:T(8,128)(2,1)S(1)}, bf16[128,256]{1,0:T(8,128)(2,1)S(1)}, u32[]{:S(2)}, u32[]{:S(2)}) %collective-permute-start.3) | collective-permute-done | bytes 65568 | tf_op jit(solution)/shard_map/ppermute | solution.py:418
  17.3 0.0 collective-permute-start.7
  17.3 0.7 %collective-permute-done.4.rest_3_ = bf16[128,256]{1,0:T(8,128)(2,1)S(1)} collective-permute-done((bf16[128,256]{1,0:T(8,128)(2,1)S(1)}, bf16[128,256]{1,0:T(8,128)(2,1)S(1)}, u32[]{:S(2)}, u32[]{:S(2)}) %collective-permute-start.4) | collective-permute-done | bytes 65568 | tf_op jit(solution)/shard_map/ppermute | solution.py:418
  18.1 0.0 collective-permute-start.8
  18.1 0.0 collective-permute-done.1.far_ref
  18.1 0.5 %attend_own.1.own_ref = bf16[128,128]{1,0:T(8,128)(2,1)S(1)} custom-call(bf16[64,8,256]{2,1,0:T(8,128)(2,1)} %store.2.cache_ref.rest_3_, f32[128,128]{1,0:T(8,128)S(1)} %get-tuple-element.17.alive_ref, bf16[2,128,128]{2,1,0:T(8,128)(2,1)S(1)} %get-tuple-element.21.query_ref, bf16[2,32,128]{2,1,0:T(8,128)(2,1)S(1)} %get-tuple-element.22.key_ref, ...), custom_call_target="tpu_custom_call" | custom-call | flops 20000000000 | tf_op jit(solution)/shard_map/attend_own/pallas_call | solution.py:315
  18.5 0.0 collective-permute-done.5.rest_0_
  18.5 0.0 collective-permute-done.6.rest_1_
  18.6 0.0 collective-permute-done.7.rest_2_
  18.6 0.7 %collective-permute-done.8.rest_3_ = bf16[128,256]{1,0:T(8,128)(2,1)S(1)} collective-permute-done((bf16[128,256]{1,0:T(8,128)(2,1)S(1)}, bf16[128,256]{1,0:T(8,128)(2,1)S(1)}, u32[]{:S(2)}, u32[]{:S(2)}) %collective-permute-start.8) | collective-permute-done | bytes 65568 | tf_op jit(solution)/shard_map/ppermute | solution.py:424
  19.3 0.4 %attend.1 = (bf16[2,32,128]{2,1,0:T(8,128)(2,1)S(1)}, bf16[2,32,128]{2,1,0:T(8,128)(2,1)S(1)}, bf16[2,32,128]{2,1,0:T(8,128)(2,1)S(1)}, bf16[2,32,128]{2,1,0:T(8,128)(2,1)S(1)}) custom-call(f32[128,128]{1,0:T(8,128)S(1)} %get-tuple-element.17.alive_ref, bf16[2,128,128]{2,1,0:T(8,128)(2,1)S(1)} %get-tuple-element.21.query_ref, ...), custom_call_target="tpu_custom_call" | custom-call | tf_op jit(solution)/shard_map/attend/pallas_call | solution.py:346
  19.8 1.6 %collective-permute-start.9 = (bf16[2,32,128]{2,1,0:T(8,128)(2,1)S(1)}, bf16[2,32,128]{2,1,0:T(8,128)(2,1)S(1)}, u32[]{:S(2)}, u32[]{:S(2)}) collective-permute-start(bf16[2,32,128]{2,1,0:T(8,128)(2,1)S(1)} %get-tuple-element.28), channel_id=1, source_target_pairs={{0,5},{1,4},{2,7},{3,6},{4,1},{5,0},{6,3},{7,2},{8,13},{9,12},{10,... | collective-permute-start | bytes 49160 | tf_op jit(solution)/shard_map/ppermute | solution.py:424
  21.3 0.5 %collective-permute-start.10 = (bf16[2,32,128]{2,1,0:T(8,128)(2,1)S(1)}, bf16[2,32,128]{2,1,0:T(8,128)(2,1)S(1)}, u32[]{:S(2)}, u32[]{:S(2)}) collective-permute-start(bf16[2,32,128]{2,1,0:T(8,128)(2,1)S(1)} %get-tuple-element.29), channel_id=1, source_target_pairs={{0,4},{1,5},{2,6},{3,7},{4,0},{5,1},{6,2},{7,3},{8,12},{9,13},{10,... | collective-permute-start | bytes 49160 | tf_op jit(solution)/shard_map/ppermute | solution.py:424
  21.8 1.5 %collective-permute-start.11 = (bf16[2,32,128]{2,1,0:T(8,128)(2,1)S(1)}, bf16[2,32,128]{2,1,0:T(8,128)(2,1)S(1)}, u32[]{:S(2)}, u32[]{:S(2)}) collective-permute-start(bf16[2,32,128]{2,1,0:T(8,128)(2,1)S(1)} %get-tuple-element.30), channel_id=1, source_target_pairs={{0,1},{1,0},{2,3},{3,2},{4,5},{5,4},{6,7},{7,6},{8,9},{9,8},{10,11... | collective-permute-start | bytes 49160 | tf_op jit(solution)/shard_map/ppermute | solution.py:424
  23.3 1.3 %store.3 = bf16[64,8,256]{2,1,0:T(8,128)(2,1)} custom-call(s32[1,64]{1,0:T(1,128)S(1)} %copy-done, bf16[16,8,256]{2,1,0:T(8,128)(2,1)S(1)} %bitcast.21, bf16[16,8,256]{2,1,0:T(8,128)(2,1)S(1)} %bitcast.23, bf16[16,8,256]{2,1,0:T(8,128)(2,1)S(1)} %bitcast.22, bf16[64,8,256]{2,1,0:T(8,128)(2,1)} %store.2.cache_ref.rest_3_), custom_call_target="tpu_custom_call", output_to_operand_aliasing={{}: (4, {})} | custom-call | flops 20000000000 | tf_op jit(solution)/shard_map/store/pallas_call | solution.py:201
  24.7 0.0 collective-permute-done.9.refs_0_
  24.7 0.4 %collective-permute-done.10.refs_1_ = bf16[2,32,128]{2,1,0:T(8,128)(2,1)S(1)} collective-permute-done((bf16[2,32,128]{2,1,0:T(8,128)(2,1)S(1)}, bf16[2,32,128]{2,1,0:T(8,128)(2,1)S(1)}, u32[]{:S(2)}, u32[]{:S(2)}) %collective-permute-start.10) | collective-permute-done | bytes 16416 | tf_op jit(solution)/shard_map/ppermute | solution.py:424
  25.1 0.5 %collective-permute-done.11.refs_2_ = bf16[2,32,128]{2,1,0:T(8,128)(2,1)S(1)} collective-permute-done((bf16[2,32,128]{2,1,0:T(8,128)(2,1)S(1)}, bf16[2,32,128]{2,1,0:T(8,128)(2,1)S(1)}, u32[]{:S(2)}, u32[]{:S(2)}) %collective-permute-start.11) | collective-permute-done | bytes 16416 | tf_op jit(solution)/shard_map/ppermute | solution.py:424
  25.6 0.7 %gather.1 = bf16[2,2,2,32,128]{4,3,2,1,0:T(8,128)(2,1)} custom-call(bf16[2,32,128]{2,1,0:T(8,128)(2,1)S(1)} %collective-permute-done.9.refs_0_, bf16[2,32,128]{2,1,0:T(8,128)(2,1)S(1)} %collective-permute-done.10.refs_1_, bf16[2,32,128]{2,1,0:T(8,128)(2,1)S(1)} %collective-permute-done.11.refs_2_, bf16[2,32,128]{2,1,0:T(8,128)(2,1)S(1)} %get-tuple-element.31.refs_3_), custom_call_target="tpu_custom_call" | custom-call | tf_op jit(solution)/shard_map/gather/pallas_call | solution.py:373
  (2 shorter events, 0.0 us)
Async XLA Ops:
  0.6 14.5 %copy-start = (s32[1,64]{1,0:T(1,128)S(1)}, s32[1,64]{1,0:T(1,128)}, u32[]{:S(2)}) copy-start(s32[1,64]{1,0:T(1,128)} %table_ref.3) | copy-start | bytes 772
  6.1 7.4 %collective-permute-start = (bf16[2,2,40,128]{3,2,1,0:T(8,128)(2,1)S(1)}, bf16[2,2,40,128]{3,2,1,0:T(8,128)(2,1)S(1)}, u32[]{:S(2)}, u32[]{:S(2)}) collective-permute-start(bf16[2,2,40,128]{3,2,1,0:T(8,128)(2,1)S(1)} %get-tuple-element.19), channel_id=1, source_target_pairs={{0,1},{1,0},{2,3},{3,2},{4,5},{5,4},{6,7},{7,6},{8,9},{9,8},{10,11... | collective-permute-start | bytes 122888 | tf_op jit(solution)/shard_map/ppermute | solution.py:424
  9.1 7.2 %collective-permute-start.2 = (bf16[128,256]{1,0:T(8,128)(2,1)S(1)}, bf16[128,256]{1,0:T(8,128)(2,1)S(1)}, u32[]{:S(2)}, u32[]{:S(2)}) collective-permute-start(bf16[128,256]{1,0:T(8,128)(2,1)S(1)} %get-tuple-element.25), channel_id=1, source_target_pairs={{0,24},{8,16},{16,8},{24,0},{1,25},{9,17},{17,9},{25,1},{2,26},{10... | collective-permute-start | bytes 196616 | tf_op jit(solution)/shard_map/ppermute | solution.py:418
  12.7 4.6 %collective-permute-start.3 = (bf16[128,256]{1,0:T(8,128)(2,1)S(1)}, bf16[128,256]{1,0:T(8,128)(2,1)S(1)}, u32[]{:S(2)}, u32[]{:S(2)}) collective-permute-start(bf16[128,256]{1,0:T(8,128)(2,1)S(1)} %get-tuple-element.26), channel_id=1, source_target_pairs={{0,8},{8,0},{16,24},{24,16},{1,9},{9,1},{17,25},{25,17},{2,10},{10... | collective-permute-start | bytes 196616 | tf_op jit(solution)/shard_map/ppermute | solution.py:418
  12.7 5.4 %collective-permute-start.4 = (bf16[128,256]{1,0:T(8,128)(2,1)S(1)}, bf16[128,256]{1,0:T(8,128)(2,1)S(1)}, u32[]{:S(2)}, u32[]{:S(2)}) collective-permute-start(bf16[128,256]{1,0:T(8,128)(2,1)S(1)} %get-tuple-element.27), channel_id=1, source_target_pairs={{0,16},{8,24},{16,0},{24,8},{1,17},{9,25},{17,1},{25,9},{2,18},{10... | collective-permute-start | bytes 196616 | tf_op jit(solution)/shard_map/ppermute | solution.py:418
  13.5 5.1 %collective-permute-start.5 = (bf16[128,256]{1,0:T(8,128)(2,1)S(1)}, bf16[128,256]{1,0:T(8,128)(2,1)S(1)}, u32[]{:S(2)}, u32[]{:S(2)}) collective-permute-start(bf16[128,256]{1,0:T(8,128)(2,1)S(1)} %get-tuple-element.24.rest_0_), channel_id=1, source_target_pairs={{0,2},{1,3},{2,0},{3,1},{4,6},{5,7},{6,4},{7,5},{8,10},{9,11},{10,... | collective-permute-start | bytes 196616 | tf_op jit(solution)/shard_map/ppermute | solution.py:424
  13.5 4.6 %collective-permute-start.1 = (bf16[2,2,40,128]{3,2,1,0:T(8,128)(2,1)S(1)}, bf16[2,2,40,128]{3,2,1,0:T(8,128)(2,1)S(1)}, u32[]{:S(2)}, u32[]{:S(2)}) collective-permute-start(bf16[2,2,40,128]{3,2,1,0:T(8,128)(2,1)S(1)} %join.1), channel_id=1, source_target_pairs={{0,4},{1,5},{2,6},{3,7},{4,0},{5,1},{6,2},{7,3},{8,12},{9,13},{10,... | collective-permute-start | bytes 122888 | tf_op jit(solution)/shard_map/ppermute | solution.py:424
  16.3 2.2 %collective-permute-start.6 = (bf16[128,256]{1,0:T(8,128)(2,1)S(1)}, bf16[128,256]{1,0:T(8,128)(2,1)S(1)}, u32[]{:S(2)}, u32[]{:S(2)}) collective-permute-start(bf16[128,256]{1,0:T(8,128)(2,1)S(1)} %collective-permute-done.2.rest_1_), channel_id=1, source_target_pairs={{0,2},{1,3},{2,0},{3,1},{4,6},{5,7},{6,4},{7,5},{8,10},{9,11},{10,... | collective-permute-start | bytes 196616 | tf_op jit(solution)/shard_map/ppermute | solution.py:424
  17.3 1.3 %collective-permute-start.7 = (bf16[128,256]{1,0:T(8,128)(2,1)S(1)}, bf16[128,256]{1,0:T(8,128)(2,1)S(1)}, u32[]{:S(2)}, u32[]{:S(2)}) collective-permute-start(bf16[128,256]{1,0:T(8,128)(2,1)S(1)} %collective-permute-done.3.rest_2_), channel_id=1, source_target_pairs={{0,2},{1,3},{2,0},{3,1},{4,6},{5,7},{6,4},{7,5},{8,10},{9,11},{10,... | collective-permute-start | bytes 196616 | tf_op jit(solution)/shard_map/ppermute | solution.py:424
  18.1 1.3 %collective-permute-start.8 = (bf16[128,256]{1,0:T(8,128)(2,1)S(1)}, bf16[128,256]{1,0:T(8,128)(2,1)S(1)}, u32[]{:S(2)}, u32[]{:S(2)}) collective-permute-start(bf16[128,256]{1,0:T(8,128)(2,1)S(1)} %collective-permute-done.4.rest_3_), channel_id=1, source_target_pairs={{0,2},{1,3},{2,0},{3,1},{4,6},{5,7},{6,4},{7,5},{8,10},{9,11},{10,... | collective-permute-start | bytes 196616 | tf_op jit(solution)/shard_map/ppermute | solution.py:424
  19.8 4.9 %collective-permute-start.9 = (bf16[2,32,128]{2,1,0:T(8,128)(2,1)S(1)}, bf16[2,32,128]{2,1,0:T(8,128)(2,1)S(1)}, u32[]{:S(2)}, u32[]{:S(2)}) collective-permute-start(bf16[2,32,128]{2,1,0:T(8,128)(2,1)S(1)} %get-tuple-element.28), channel_id=1, source_target_pairs={{0,5},{1,4},{2,7},{3,6},{4,1},{5,0},{6,3},{7,2},{8,13},{9,12},{10,... | collective-permute-start | bytes 49160 | tf_op jit(solution)/shard_map/ppermute | solution.py:424
  21.3 3.7 %collective-permute-start.10 = (bf16[2,32,128]{2,1,0:T(8,128)(2,1)S(1)}, bf16[2,32,128]{2,1,0:T(8,128)(2,1)S(1)}, u32[]{:S(2)}, u32[]{:S(2)}) collective-permute-start(bf16[2,32,128]{2,1,0:T(8,128)(2,1)S(1)} %get-tuple-element.29), channel_id=1, source_target_pairs={{0,4},{1,5},{2,6},{3,7},{4,0},{5,1},{6,2},{7,3},{8,12},{9,13},{10,... | collective-permute-start | bytes 49160 | tf_op jit(solution)/shard_map/ppermute | solution.py:424
  21.8 3.7 %collective-permute-start.11 = (bf16[2,32,128]{2,1,0:T(8,128)(2,1)S(1)}, bf16[2,32,128]{2,1,0:T(8,128)(2,1)S(1)}, u32[]{:S(2)}, u32[]{:S(2)}) collective-permute-start(bf16[2,32,128]{2,1,0:T(8,128)(2,1)S(1)} %get-tuple-element.30), channel_id=1, source_target_pairs={{0,1},{1,0},{2,3},{3,2},{4,5},{5,4},{6,7},{7,6},{8,9},{9,8},{10,11... | collective-permute-start | bytes 49160 | tf_op jit(solution)/shard_map/ppermute | solution.py:424

commit v9 on v8

--- a/solution.py
+++ b/solution.py
@@ -232,9 +232,15 @@
     )(first, second)
 
 
-def arrange_kernel(steps, far_ref, near_ref, own_ref, query_ref, key_ref, value_ref):
+def arrange_kernel(steps, far_ref, near_ref, own_ref, query_ref, key_ref, value_ref, mask_ref):
     packets = (far_ref.at[1], far_ref.at[0], near_ref.at[0], own_ref.at[0])
     q_rows = Q_PER_KV * steps
+    row = lax.broadcasted_iota(jnp.int32, mask_ref.shape, 0)
+    column = lax.broadcasted_iota(jnp.int32, mask_ref.shape, 1)
+    visible = jnp.logical_and(
+        row // q_rows == column // (2 * steps), column % (2 * steps) <= row % steps
+    )
+    mask_ref[...] = jnp.where(visible, 0.0, -jnp.inf)
     for at in range(2):
         recent = jnp.concatenate(
             [packet[at, q_rows:, :].astype(jnp.float32) for packet in packets], axis=0
@@ -253,11 +259,12 @@
     return pl.pallas_call(
         functools.partial(arrange_kernel, steps),
         in_specs=[vmem] * 3,
-        out_specs=[vmem] * 3,
+        out_specs=[vmem] * 4,
         out_shape=[
             pltpu.VMEM((2, samples * Q_PER_KV * steps, HEAD_DIM), dtype),
             recent,
             recent,
+            pltpu.VMEM((samples * Q_PER_KV * steps, samples * 2 * steps), jnp.float32),
         ],
         cost_estimate=pl.CostEstimate(flops=HIDE_FLOPS, transcendentals=0, bytes_accessed=0),
         compiler_params=pltpu.CompilerParams(vmem_limit_bytes=PACK_VMEM),
@@ -265,8 +272,7 @@
     )(*packets)
 
 
-def attend_head(steps, alive, query, recent_key, recent_value, blocks):
-    q_rows = Q_PER_KV * steps
+def attend_head(alive, query, recent_key, recent_value, mask, blocks):
     scaling = HEAD_DIM ** (-0.5)
     contract = (((1,), (1,)), ((), ()))
 
@@ -276,12 +282,7 @@
         )
 
     recent_score = scored(recent_key)
-    row = lax.broadcasted_iota(jnp.int32, recent_score.shape, 0)
-    column = lax.broadcasted_iota(jnp.int32, recent_score.shape, 1)
-    visible = jnp.logical_and(
-        row // q_rows == column // (2 * steps), column % (2 * steps) <= row % steps
-    )
-    recent_score = jnp.where(visible, recent_score, -jnp.inf)
+    recent_score = recent_score + mask
     score = scored(jnp.concatenate([block[:, :HEAD_DIM] for block in blocks], axis=0))
     highest = jnp.max(score, axis=1, keepdims=True)
     highest = jnp.maximum(highest, jnp.max(recent_score, axis=1, keepdims=True))
@@ -297,15 +298,15 @@
     return jnp.where(alive > 0.0, blended, 0.0)
 
 
-def attend_own_kernel(groups, steps, cache_ref, alive_ref, query_ref, key_ref, value_ref, *rest):
+def attend_own_kernel(groups, steps, cache_ref, alive_ref, query_ref, key_ref, value_ref, mask_ref, *rest):
     del cache_ref
     blocks, out_ref = rest[:groups], rest[groups]
     out_ref[...] = attend_head(
-        steps,
         alive_ref[...],
         query_ref[0],
         key_ref[0],
         value_ref[0],
+        mask_ref[...],
         [block[...] for block in blocks],
     ).astype(out_ref.dtype)
 
@@ -323,15 +324,15 @@
     )(in_hbm(cache), alive, *arranged, *blocks)
 
 
-def attend_kernel(groups, steps, alive_ref, query_ref, key_ref, value_ref, own_ref, *rest):
+def attend_kernel(groups, steps, alive_ref, query_ref, key_ref, value_ref, mask_ref, own_ref, *rest):
     blocks, outs = rest[:groups], rest[groups:]
     q_rows = Q_PER_KV * steps
     blended = attend_head(
-        steps,
         alive_ref[...],
         query_ref[1],
         key_ref[1],
         value_ref[1],
+        mask_ref[...],
         [block[...] for block in blocks],
     ).astype(jnp.bfloat16)
     side = jnp.where(lax.axis_index(MEMBERS) & SIBLING == 0, 0, 1)

time: 26.4 us -> 26.4 us (level)
  transfers between devices with their start and end apart: 12 -> 12, of which waited for: 5 -> 5; matrix products, arithmetic and copies ran while one was open for 0% -> 0% of each run, Pallas kernels for 11% -> 12%
where the time goes in v9:
time: 26.4 us; the launch traced here: 26.2 us
  starting transfers between devices  12.8 us (48%)
  Pallas kernels  9.57 us (36%)
  waiting for transfers between devices  3.15 us (12%)
  between operations  0.74 us (3%)
    ppermute x9, starting transfers between devices, to_peer(): lax.ppermute(array, MEMBERS, [(i, i ^ distance) for i in range(members)])  8.37 us
    pallas_call x1, Pallas kernels, project(): pl.pallas_call(functools.partial(project_kernel, groups, ordered), in_spe...  5.44 us
    ppermute x3, starting transfers between devices, local(): lax.ppermute(block, 'group', [(i, goes_to(i)) for i in range(groups)])  4.39 us
    pallas_call x2, Pallas kernels, store(): pl.pallas_call(functools.partial(store_kernel, groups, picks), in_specs=s...  2.54 us
    ppermute x9, waiting for transfers between devices, to_peer(): lax.ppermute(array, MEMBERS, [(i, i ^ distance) for i in range(members)])  1.64 us
    ppermute x3, waiting for transfers between devices, local(): lax.ppermute(block, 'group', [(i, goes_to(i)) for i in range(groups)])  1.51 us
    pallas_call x1, Pallas kernels, gather(): pl.pallas_call(gather_kernel, in_specs=[pl.BlockSpec(memory_space=pltpu.V...  0.66 us
  transfers between devices with their start and end apart: 12, of which 5 were waited for; matrix products, arithmetic and copies ran while one was open for 0% of the time, Pallas kernels for 12%

profile of v9, /device:TPU:0, one launch (start us, length us, event | category | flops | bytes accessed | tf_op | source)
XLA Modules:
  0.0 26.2 jit_solution(18383745281011265162)
XLA Ops:
  0.6 0.0 copy-start
  0.6 5.4 %project.1 = (bf16[128,256]{1,0:T(8,128)(2,1)S(1)}, bf16[128,256]{1,0:T(8,128)(2,1)S(1)}, bf16[128,256]{1,0:T(8,128)(2,1)S(1)}, bf16[128,256]{1,0:T(8,128)(2,1)S...) custom-call(s32[4]{0:T(128)} %prompt_hbm.1, ...), custom_call_target="tpu_custom_call" | custom-call | tf_op jit(solution)/shard_map/project/pallas_call | solution.py:152
  6.1 3.0 %collective-permute-start = (bf16[2,2,40,128]{3,2,1,0:T(8,128)(2,1)S(1)}, bf16[2,2,40,128]{3,2,1,0:T(8,128)(2,1)S(1)}, u32[]{:S(2)}, u32[]{:S(2)}) collective-permute-start(bf16[2,2,40,128]{3,2,1,0:T(8,128)(2,1)S(1)} %get-tuple-element.20), channel_id=1, source_target_pairs={{0,1},{1,0},{2,3},{3,2},{4,5},{5,4},{6,7},{7,6},{8,9},{9,8},{10,11... | collective-permute-start | bytes 122888 | tf_op jit(solution)/shard_map/ppermute | solution.py:425
  9.1 3.6 %collective-permute-start.2 = (bf16[128,256]{1,0:T(8,128)(2,1)S(1)}, bf16[128,256]{1,0:T(8,128)(2,1)S(1)}, u32[]{:S(2)}, u32[]{:S(2)}) collective-permute-start(bf16[128,256]{1,0:T(8,128)(2,1)S(1)} %get-tuple-element.27), channel_id=1, source_target_pairs={{0,24},{8,16},{16,8},{24,0},{1,25},{9,17},{17,9},{25,1},{2,26},{10... | collective-permute-start | bytes 196616 | tf_op jit(solution)/shard_map/ppermute | solution.py:419
  12.7 0.0 collective-permute-start.3
  12.7 0.8 %collective-permute-start.4 = (bf16[128,256]{1,0:T(8,128)(2,1)S(1)}, bf16[128,256]{1,0:T(8,128)(2,1)S(1)}, u32[]{:S(2)}, u32[]{:S(2)}) collective-permute-start(bf16[128,256]{1,0:T(8,128)(2,1)S(1)} %get-tuple-element.29), channel_id=1, source_target_pairs={{0,16},{8,24},{16,0},{24,8},{1,17},{9,25},{17,1},{25,9},{2,18},{10... | collective-permute-start | bytes 196616 | tf_op jit(solution)/shard_map/ppermute | solution.py:419
  13.5 0.0 collective-permute-start.5
  13.5 0.0 collective-permute-done.second_ref.near_ref
  13.5 1.6 %collective-permute-start.1 = (bf16[2,2,40,128]{3,2,1,0:T(8,128)(2,1)S(1)}, bf16[2,2,40,128]{3,2,1,0:T(8,128)(2,1)S(1)}, u32[]{:S(2)}, u32[]{:S(2)}) collective-permute-start(bf16[2,2,40,128]{3,2,1,0:T(8,128)(2,1)S(1)} %join.1), channel_id=1, source_target_pairs={{0,4},{1,5},{2,6},{3,7},{4,0},{5,1},{6,2},{7,3},{8,12},{9,13},{10,... | collective-permute-start | bytes 122888 | tf_op jit(solution)/shard_map/ppermute | solution.py:425
  15.1 0.0 copy-done
  15.1 1.2 %store.2.cache_ref.rest_3_ = bf16[64,8,256]{2,1,0:T(8,128)(2,1)} custom-call(s32[1,64]{1,0:T(1,128)S(1)} %copy-done, bf16[16,8,256]{2,1,0:T(8,128)(2,1)S(1)} %bitcast.24), custom_call_target="tpu_custom_call" | custom-call | flops 20000000000 | tf_op jit(solution)/shard_map/store/pallas_call | solution.py:201
  16.3 0.0 collective-permute-done.2.rest_1_
  16.3 0.2 collective-permute-start.6
  16.5 0.8 %collective-permute-done.3.rest_2_ = bf16[128,256]{1,0:T(8,128)(2,1)S(1)} collective-permute-done((bf16[128,256]{1,0:T(8,128)(2,1)S(1)}, bf16[128,256]{1,0:T(8,128)(2,1)S(1)}, u32[]{:S(2)}, u32[]{:S(2)}) %collective-permute-start.3) | collective-permute-done | bytes 65568 | tf_op jit(solution)/shard_map/ppermute | solution.py:419
  17.3 0.0 collective-permute-start.7
  17.3 0.7 %collective-permute-done.4.rest_3_ = bf16[128,256]{1,0:T(8,128)(2,1)S(1)} collective-permute-done((bf16[128,256]{1,0:T(8,128)(2,1)S(1)}, bf16[128,256]{1,0:T(8,128)(2,1)S(1)}, u32[]{:S(2)}, u32[]{:S(2)}) %collective-permute-start.4) | collective-permute-done | bytes 65568 | tf_op jit(solution)/shard_map/ppermute | solution.py:419
  18.1 0.0 collective-permute-start.8
  18.1 0.0 collective-permute-done.1.far_ref
  18.1 0.5 %attend_own.1.own_ref = bf16[128,128]{1,0:T(8,128)(2,1)S(1)} custom-call(bf16[64,8,256]{2,1,0:T(8,128)(2,1)} %store.2.cache_ref.rest_3_, f32[128,128]{1,0:T(8,128)S(1)} %get-tuple-element.18.alive_ref, bf16[2,128,128]{2,1,0:T(8,128)(2,1)S(1)} %get-tuple-element.22.query_ref, bf16[2,32,128]{2,1,0:T(8,128)(2,1)S(1)} %get-tuple-element.23.key_ref, ...), custom_call_target="tpu_custom_call" | custom-call | flops 20000000000 | tf_op jit(solution)/shard_map/attend_own/pallas_call | solution.py:316
  18.6 0.0 collective-permute-done.5.rest_0_
  18.6 0.0 collective-permute-done.6.rest_1_
  18.6 0.0 collective-permute-done.7.rest_2_
  18.6 0.7 %collective-permute-done.8.rest_3_ = bf16[128,256]{1,0:T(8,128)(2,1)S(1)} collective-permute-done((bf16[128,256]{1,0:T(8,128)(2,1)S(1)}, bf16[128,256]{1,0:T(8,128)(2,1)S(1)}, u32[]{:S(2)}, u32[]{:S(2)}) %collective-permute-start.8) | collective-permute-done | bytes 65568 | tf_op jit(solution)/shard_map/ppermute | solution.py:425
  19.3 0.4 %attend.1 = (bf16[2,32,128]{2,1,0:T(8,128)(2,1)S(1)}, bf16[2,32,128]{2,1,0:T(8,128)(2,1)S(1)}, bf16[2,32,128]{2,1,0:T(8,128)(2,1)S(1)}, bf16[2,32,128]{2,1,0:T(8,128)(2,1)S(1)}) custom-call(f32[128,128]{1,0:T(8,128)S(1)} %get-tuple-element.18.alive_ref, bf16[2,128,128]{2,1,0:T(8,128)(2,1)S(1)} %get-tuple-element.22.query_ref, ...), custom_call_target="tpu_custom_call" | custom-call | tf_op jit(solution)/shard_map/attend/pallas_call | solution.py:347
  19.8 1.6 %collective-permute-start.9 = (bf16[2,32,128]{2,1,0:T(8,128)(2,1)S(1)}, bf16[2,32,128]{2,1,0:T(8,128)(2,1)S(1)}, u32[]{:S(2)}, u32[]{:S(2)}) collective-permute-start(bf16[2,32,128]{2,1,0:T(8,128)(2,1)S(1)} %get-tuple-element.30), channel_id=1, source_target_pairs={{0,5},{1,4},{2,7},{3,6},{4,1},{5,0},{6,3},{7,2},{8,13},{9,12},{10,... | collective-permute-start | bytes 49160 | tf_op jit(solution)/shard_map/ppermute | solution.py:425
  21.3 0.5 %collective-permute-start.10 = (bf16[2,32,128]{2,1,0:T(8,128)(2,1)S(1)}, bf16[2,32,128]{2,1,0:T(8,128)(2,1)S(1)}, u32[]{:S(2)}, u32[]{:S(2)}) collective-permute-start(bf16[2,32,128]{2,1,0:T(8,128)(2,1)S(1)} %get-tuple-element.31), channel_id=1, source_target_pairs={{0,4},{1,5},{2,6},{3,7},{4,0},{5,1},{6,2},{7,3},{8,12},{9,13},{10,... | collective-permute-start | bytes 49160 | tf_op jit(solution)/shard_map/ppermute | solution.py:425
  21.8 1.5 %collective-permute-start.11 = (bf16[2,32,128]{2,1,0:T(8,128)(2,1)S(1)}, bf16[2,32,128]{2,1,0:T(8,128)(2,1)S(1)}, u32[]{:S(2)}, u32[]{:S(2)}) collective-permute-start(bf16[2,32,128]{2,1,0:T(8,128)(2,1)S(1)} %get-tuple-element.32), channel_id=1, source_target_pairs={{0,1},{1,0},{2,3},{3,2},{4,5},{5,4},{6,7},{7,6},{8,9},{9,8},{10,11... | collective-permute-start | bytes 49160 | tf_op jit(solution)/shard_map/ppermute | solution.py:425
  23.3 1.3 %store.3 = bf16[64,8,256]{2,1,0:T(8,128)(2,1)} custom-call(s32[1,64]{1,0:T(1,128)S(1)} %copy-done, bf16[16,8,256]{2,1,0:T(8,128)(2,1)S(1)} %bitcast.21, bf16[16,8,256]{2,1,0:T(8,128)(2,1)S(1)} %bitcast.23, bf16[16,8,256]{2,1,0:T(8,128)(2,1)S(1)} %bitcast.22, bf16[64,8,256]{2,1,0:T(8,128)(2,1)} %store.2.cache_ref.rest_3_), custom_call_target="tpu_custom_call", output_to_operand_aliasing={{}: (4, {})} | custom-call | flops 20000000000 | tf_op jit(solution)/shard_map/store/pallas_call | solution.py:201
  24.7 0.0 collective-permute-done.9.refs_0_
  24.7 0.4 %collective-permute-done.10.refs_1_ = bf16[2,32,128]{2,1,0:T(8,128)(2,1)S(1)} collective-permute-done((bf16[2,32,128]{2,1,0:T(8,128)(2,1)S(1)}, bf16[2,32,128]{2,1,0:T(8,128)(2,1)S(1)}, u32[]{:S(2)}, u32[]{:S(2)}) %collective-permute-start.10) | collective-permute-done | bytes 16416 | tf_op jit(solution)/shard_map/ppermute | solution.py:425
  25.1 0.5 %collective-permute-done.11.refs_2_ = bf16[2,32,128]{2,1,0:T(8,128)(2,1)S(1)} collective-permute-done((bf16[2,32,128]{2,1,0:T(8,128)(2,1)S(1)}, bf16[2,32,128]{2,1,0:T(8,128)(2,1)S(1)}, u32[]{:S(2)}, u32[]{:S(2)}) %collective-permute-start.11) | collective-permute-done | bytes 16416 | tf_op jit(solution)/shard_map/ppermute | solution.py:425
  25.6 0.7 %gather.1 = bf16[2,2,2,32,128]{4,3,2,1,0:T(8,128)(2,1)} custom-call(bf16[2,32,128]{2,1,0:T(8,128)(2,1)S(1)} %collective-permute-done.9.refs_0_, bf16[2,32,128]{2,1,0:T(8,128)(2,1)S(1)} %collective-permute-done.10.refs_1_, bf16[2,32,128]{2,1,0:T(8,128)(2,1)S(1)} %collective-permute-done.11.refs_2_, bf16[2,32,128]{2,1,0:T(8,128)(2,1)S(1)} %get-tuple-element.33.refs_3_), custom_call_target="tpu_custom_call" | custom-call | tf_op jit(solution)/shard_map/gather/pallas_call | solution.py:374
  (2 shorter events, 0.0 us)
Async XLA Ops:
  0.6 14.5 %copy-start = (s32[1,64]{1,0:T(1,128)S(1)}, s32[1,64]{1,0:T(1,128)}, u32[]{:S(2)}) copy-start(s32[1,64]{1,0:T(1,128)} %table_ref.3) | copy-start | bytes 772
  6.1 7.4 %collective-permute-start = (bf16[2,2,40,128]{3,2,1,0:T(8,128)(2,1)S(1)}, bf16[2,2,40,128]{3,2,1,0:T(8,128)(2,1)S(1)}, u32[]{:S(2)}, u32[]{:S(2)}) collective-permute-start(bf16[2,2,40,128]{3,2,1,0:T(8,128)(2,1)S(1)} %get-tuple-element.20), channel_id=1, source_target_pairs={{0,1},{1,0},{2,3},{3,2},{4,5},{5,4},{6,7},{7,6},{8,9},{9,8},{10,11... | collective-permute-start | bytes 122888 | tf_op jit(solution)/shard_map/ppermute | solution.py:425
  9.1 7.2 %collective-permute-start.2 = (bf16[128,256]{1,0:T(8,128)(2,1)S(1)}, bf16[128,256]{1,0:T(8,128)(2,1)S(1)}, u32[]{:S(2)}, u32[]{:S(2)}) collective-permute-start(bf16[128,256]{1,0:T(8,128)(2,1)S(1)} %get-tuple-element.27), channel_id=1, source_target_pairs={{0,24},{8,16},{16,8},{24,0},{1,25},{9,17},{17,9},{25,1},{2,26},{10... | collective-permute-start | bytes 196616 | tf_op jit(solution)/shard_map/ppermute | solution.py:419
  12.7 4.6 %collective-permute-start.3 = (bf16[128,256]{1,0:T(8,128)(2,1)S(1)}, bf16[128,256]{1,0:T(8,128)(2,1)S(1)}, u32[]{:S(2)}, u32[]{:S(2)}) collective-permute-start(bf16[128,256]{1,0:T(8,128)(2,1)S(1)} %get-tuple-element.28), channel_id=1, source_target_pairs={{0,8},{8,0},{16,24},{24,16},{1,9},{9,1},{17,25},{25,17},{2,10},{10... | collective-permute-start | bytes 196616 | tf_op jit(solution)/shard_map/ppermute | solution.py:419
  12.7 5.4 %collective-permute-start.4 = (bf16[128,256]{1,0:T(8,128)(2,1)S(1)}, bf16[128,256]{1,0:T(8,128)(2,1)S(1)}, u32[]{:S(2)}, u32[]{:S(2)}) collective-permute-start(bf16[128,256]{1,0:T(8,128)(2,1)S(1)} %get-tuple-element.29), channel_id=1, source_target_pairs={{0,16},{8,24},{16,0},{24,8},{1,17},{9,25},{17,1},{25,9},{2,18},{10... | collective-permute-start | bytes 196616 | tf_op jit(solution)/shard_map/ppermute | solution.py:419
  13.5 5.1 %collective-permute-start.5 = (bf16[128,256]{1,0:T(8,128)(2,1)S(1)}, bf16[128,256]{1,0:T(8,128)(2,1)S(1)}, u32[]{:S(2)}, u32[]{:S(2)}) collective-permute-start(bf16[128,256]{1,0:T(8,128)(2,1)S(1)} %get-tuple-element.26.rest_0_), channel_id=1, source_target_pairs={{0,2},{1,3},{2,0},{3,1},{4,6},{5,7},{6,4},{7,5},{8,10},{9,11},{10,... | collective-permute-start | bytes 196616 | tf_op jit(solution)/shard_map/ppermute | solution.py:425
  13.5 4.6 %collective-permute-start.1 = (bf16[2,2,40,128]{3,2,1,0:T(8,128)(2,1)S(1)}, bf16[2,2,40,128]{3,2,1,0:T(8,128)(2,1)S(1)}, u32[]{:S(2)}, u32[]{:S(2)}) collective-permute-start(bf16[2,2,40,128]{3,2,1,0:T(8,128)(2,1)S(1)} %join.1), channel_id=1, source_target_pairs={{0,4},{1,5},{2,6},{3,7},{4,0},{5,1},{6,2},{7,3},{8,12},{9,13},{10,... | collective-permute-start | bytes 122888 | tf_op jit(solution)/shard_map/ppermute | solution.py:425
  16.3 2.3 %collective-permute-start.6 = (bf16[128,256]{1,0:T(8,128)(2,1)S(1)}, bf16[128,256]{1,0:T(8,128)(2,1)S(1)}, u32[]{:S(2)}, u32[]{:S(2)}) collective-permute-start(bf16[128,256]{1,0:T(8,128)(2,1)S(1)} %collective-permute-done.2.rest_1_), channel_id=1, source_target_pairs={{0,2},{1,3},{2,0},{3,1},{4,6},{5,7},{6,4},{7,5},{8,10},{9,11},{10,... | collective-permute-start | bytes 196616 | tf_op jit(solution)/shard_map/ppermute | solution.py:425
  17.3 1.3 %collective-permute-start.7 = (bf16[128,256]{1,0:T(8,128)(2,1)S(1)}, bf16[128,256]{1,0:T(8,128)(2,1)S(1)}, u32[]{:S(2)}, u32[]{:S(2)}) collective-permute-start(bf16[128,256]{1,0:T(8,128)(2,1)S(1)} %collective-permute-done.3.rest_2_), channel_id=1, source_target_pairs={{0,2},{1,3},{2,0},{3,1},{4,6},{5,7},{6,4},{7,5},{8,10},{9,11},{10,... | collective-permute-start | bytes 196616 | tf_op jit(solution)/shard_map/ppermute | solution.py:425
  18.1 1.3 %collective-permute-start.8 = (bf16[128,256]{1,0:T(8,128)(2,1)S(1)}, bf16[128,256]{1,0:T(8,128)(2,1)S(1)}, u32[]{:S(2)}, u32[]{:S(2)}) collective-permute-start(bf16[128,256]{1,0:T(8,128)(2,1)S(1)} %collective-permute-done.4.rest_3_), channel_id=1, source_target_pairs={{0,2},{1,3},{2,0},{3,1},{4,6},{5,7},{6,4},{7,5},{8,10},{9,11},{10,... | collective-permute-start | bytes 196616 | tf_op jit(solution)/shard_map/ppermute | solution.py:425
  19.8 4.9 %collective-permute-start.9 = (bf16[2,32,128]{2,1,0:T(8,128)(2,1)S(1)}, bf16[2,32,128]{2,1,0:T(8,128)(2,1)S(1)}, u32[]{:S(2)}, u32[]{:S(2)}) collective-permute-start(bf16[2,32,128]{2,1,0:T(8,128)(2,1)S(1)} %get-tuple-element.30), channel_id=1, source_target_pairs={{0,5},{1,4},{2,7},{3,6},{4,1},{5,0},{6,3},{7,2},{8,13},{9,12},{10,... | collective-permute-start | bytes 49160 | tf_op jit(solution)/shard_map/ppermute | solution.py:425
  21.3 3.7 %collective-permute-start.10 = (bf16[2,32,128]{2,1,0:T(8,128)(2,1)S(1)}, bf16[2,32,128]{2,1,0:T(8,128)(2,1)S(1)}, u32[]{:S(2)}, u32[]{:S(2)}) collective-permute-start(bf16[2,32,128]{2,1,0:T(8,128)(2,1)S(1)} %get-tuple-element.31), channel_id=1, source_target_pairs={{0,4},{1,5},{2,6},{3,7},{4,0},{5,1},{6,2},{7,3},{8,12},{9,13},{10,... | collective-permute-start | bytes 49160 | tf_op jit(solution)/shard_map/ppermute | solution.py:425
  21.8 3.7 %collective-permute-start.11 = (bf16[2,32,128]{2,1,0:T(8,128)(2,1)S(1)}, bf16[2,32,128]{2,1,0:T(8,128)(2,1)S(1)}, u32[]{:S(2)}, u32[]{:S(2)}) collective-permute-start(bf16[2,32,128]{2,1,0:T(8,128)(2,1)S(1)} %get-tuple-element.32), channel_id=1, source_target_pairs={{0,1},{1,0},{2,3},{3,2},{4,5},{5,4},{6,7},{7,6},{8,9},{9,8},{10,11... | collective-permute-start | bytes 49160 | tf_op jit(solution)/shard_map/ppermute | solution.py:425
